TPU v7x, 128 devices: a whole 4x4x4 slice. The times are simulated.
128 devices in a mesh: ep: 8 (over x, z_hi), fsdp: 16 (over y, z_lo, core).
Axes of the slice: x: 4, y: 4, z: 4 (z_hi: 2, z_lo: 2; z = z_hi * 2 + z_lo), core: 2. Of those that a mesh axis runs over, the one named last changes fastest.
Arguments:
- tokens: bfloat16 [16384, 5120], P(('ep', 'fsdp')), may hold values from -6 to 6
- norm_gain: bfloat16 [5120], P('fsdp'), may hold values from 0.099609375 to 1.8984375
- router_weight: bfloat16 [5120, 64], P('fsdp'), may hold values from -0.078125 to 0.078125
- up_weight: bfloat16 [128, 5120, 768], P(('ep', 'fsdp')), may hold values from -0.078125 to 0.078125
- down_weight: bfloat16 [128, 768, 5120], P(('ep', 'fsdp')), may hold values from -0.15625 to 0.15625
- expert_ids: int32 [16384, 2], P(('ep', 'fsdp')), may hold values from 0 to 63, all different within a row; in each aligned block of 128 rows (0 to 127, 128 to 255, ...) at most 6 rows name the same one
- cotangent: bfloat16 [16384, 5120], P(('ep', 'fsdp')), may hold values from -24 to 24
Outputs:
- mixed: bfloat16 [16384, 5120], P(('ep', 'fsdp'))
- grad_tokens: bfloat16 [16384, 5120], P(('ep', 'fsdp'))
- grad_router: float32 [5120, 64], P('fsdp')
- grad_gain: float32 [5120], P('fsdp')
Inputs may be any that keep to these rules, and one draw needn't show every extreme that they name: `expert_ids`: each row names two different experts; among the 128 rows of one device no expert is named more than 6 times.
All inputs are finite; a program needn't handle non-finite values.
Results may differ from a plain program's by a relative error of at most 0.0072.
Values may be sent and summed in bfloat16 or wider, within the bound.
No kernel may reach another device: no remote copies, remote signals or barrier semaphores. Data moves between devices by JAX's collectives and lax.ppermute only.
A program may use at most 192 MiB of HBM per device.

v0:
```python
import math

import jax
import jax.numpy as jnp
from jax import lax
from jax.sharding import PartitionSpec as P

EPS = 1e-06


def from_partner(value, axis, distance):
    mask = 2**distance
    pairs = [(source, source ^ mask) for source in range(lax.axis_size(axis))]
    return lax.ppermute(value, axis, pairs)


def norm_rows(rows, gain):
    scale = lax.rsqrt(jnp.mean(rows * rows, axis=-1, keepdims=True) + EPS)
    return rows * scale * gain


def gelu_tanh(values):
    return jax.nn.gelu(values, approximate=True)


def add_halves(first, second):
    return (first.astype(jnp.float32) + second.astype(jnp.float32)).astype(jnp.bfloat16)


def body(tokens, norm_gain, router_weight, up_weight, down_weight, expert_ids, cotangent):
    tok_rows, features = tokens.shape
    ep_count = lax.axis_size("ep")
    fsdp_count = lax.axis_size("fsdp")
    experts = ep_count * fsdp_count // 2
    capacity = 2 * ((3 * tok_rows + 2 * experts - 1) // (2 * experts))
    half_cap = capacity // 2
    half_index = lax.axis_index("fsdp") % 2
    gain_full, router_full = (
        lax.all_gather(norm_gain, "fsdp", axis=0, tiled=True),
        lax.all_gather(router_weight, "fsdp", axis=0, tiled=True),
    )
    x_float = tokens.astype(jnp.float32)
    normed_float, norm_back = jax.vjp(norm_rows, x_float, gain_full.astype(jnp.float32))
    normed = normed_float.astype(jnp.bfloat16)
    logits = jnp.dot(normed, router_full, preferred_element_type=jnp.float32)
    expert_iota = lax.broadcasted_iota(jnp.int32, (1, 1, experts), 2)
    chosen_mask = (expert_ids[:, :, None] == expert_iota).astype(jnp.float32)
    gates = jax.nn.sigmoid(jnp.sum(chosen_mask * logits[:, None, :], axis=-1))
    flat_mask = chosen_mask.reshape(tok_rows * 2, experts)
    running = jnp.cumsum(flat_mask, axis=0)
    count_of = jnp.sum(flat_mask * (running - 1.0), axis=-1).astype(jnp.int32)
    slot_of = (count_of + lax.axis_index("fsdp")) % capacity
    position = expert_ids.reshape(-1) * capacity + slot_of
    slot_iota = lax.broadcasted_iota(jnp.int32, (experts * capacity, 1), 0)
    placing = (slot_iota == position[None, :]).astype(jnp.bfloat16)
    token_place = jnp.sum(placing.reshape(experts * capacity, tok_rows, 2), axis=-1)
    up_own = up_weight[0]
    down_own = down_weight[0]

    def dispatch(buffer):
        single = buffer.reshape(ep_count, fsdp_count // 2, 1, capacity, features)
        blocks = jnp.broadcast_to(single, (ep_count, fsdp_count // 2, 2, capacity, features))
        blocks = blocks.reshape(ep_count, fsdp_count, capacity, features)
        arrived = lax.all_to_all(
            lax.all_to_all(blocks, "ep", split_axis=0, concat_axis=0, tiled=True),
            "fsdp",
            split_axis=1,
            concat_axis=1,
            tiled=True,
        )
        return arrived.reshape(-1, features)

    def collect(partial_rows):
        halves = partial_rows.reshape(ep_count, fsdp_count, 2, half_cap, features)
        own_half = lax.dynamic_index_in_dim(halves, half_index, 2, keepdims=False)
        other_half = lax.dynamic_index_in_dim(halves, 1 - half_index, 2, keepdims=False)
        result = add_halves(own_half, from_partner(other_half, "fsdp", 0))
        returned = lax.all_to_all(
            lax.all_to_all(result, "ep", split_axis=0, concat_axis=0, tiled=True),
            "fsdp",
            split_axis=1,
            concat_axis=1,
            tiled=True,
        )
        flat_back = returned.reshape(experts * capacity, features)
        gathered = jnp.einsum("pa,pd->ad", placing, flat_back, preferred_element_type=jnp.float32)
        return gathered.reshape(tok_rows, 2, features)

    row_block = dispatch(
        jnp.dot(token_place, normed, preferred_element_type=jnp.float32).astype(jnp.bfloat16)
    )
    pre_act = jnp.dot(row_block, up_own, preferred_element_type=jnp.float32)
    hidden_f, gelu_back = jax.vjp(gelu_tanh, pre_act)
    partial_out = jnp.dot(
        hidden_f.astype(jnp.bfloat16), down_own, preferred_element_type=jnp.float32
    ).astype(jnp.bfloat16)
    expert_out = collect(partial_out)
    mixed = (x_float + jnp.sum(gates[:, :, None] * expert_out, axis=1)).astype(jnp.bfloat16)
    cot_float = cotangent.astype(jnp.float32)
    gated_cot = (
        (gates[:, :, None] * cot_float[:, None, :])
        .reshape(tok_rows * 2, features)
        .astype(jnp.bfloat16)
    )
    cot_block = dispatch(
        jnp.dot(placing, gated_cot, preferred_element_type=jnp.float32).astype(jnp.bfloat16)
    )
    grad_act = jnp.einsum("rd,hd->rh", cot_block, down_own, preferred_element_type=jnp.float32)
    grad_hidden = gelu_back(grad_act)[0].astype(jnp.bfloat16)
    grad_part = jnp.einsum(
        "rh,dh->rd", grad_hidden, up_own, preferred_element_type=jnp.float32
    ).astype(jnp.bfloat16)
    grad_rows = collect(grad_part)
    grad_gate = jnp.sum(cot_float[:, None, :] * expert_out, axis=-1)
    grad_choice = grad_gate * gates * (1.0 - gates)
    grad_logits = jnp.sum(chosen_mask * grad_choice[:, :, None], axis=1)
    grad_normed = jnp.sum(grad_rows, axis=1) + jnp.dot(
        grad_logits, router_full.astype(jnp.float32).T, precision=lax.Precision.HIGHEST
    )
    grad_x_float, gain_term = norm_back(grad_normed)
    grad_tokens = (cot_float + grad_x_float).astype(jnp.bfloat16)
    router_term = jnp.dot(
        normed.astype(jnp.float32).T, grad_logits, precision=lax.Precision.HIGHEST
    )
    scale = 1.0 / math.sqrt(tok_rows * ep_count * fsdp_count)
    shard_rows = features // fsdp_count
    router_total, gain_total = lax.psum((router_term, gain_term), ("ep", "fsdp"))
    start = lax.axis_index("fsdp") * shard_rows
    router_share = lax.dynamic_slice_in_dim(router_total, start, shard_rows, 0)
    gain_share = lax.dynamic_slice_in_dim(gain_total, start, shard_rows, 0)
    return (mixed, grad_tokens, router_share * scale, gain_share * scale)


def solution(mesh):
    in_specs = (
        P(("ep", "fsdp"), None),
        P("fsdp"),
        P("fsdp", None),
        P(("ep", "fsdp"), None, None),
        P(("ep", "fsdp"), None, None),
        P(("ep", "fsdp"), None),
        P(("ep", "fsdp"), None),
    )
    out_specs = (P(("ep", "fsdp"), None), P(("ep", "fsdp"), None), P("fsdp", None), P("fsdp"))
    return jax.shard_map(body, mesh=mesh, in_specs=in_specs, out_specs=out_specs, check_vma=False)
```

profile of v0, /device:TPU:1, one launch (start us, length us, event | category | flops | bytes accessed | tf_op | source)
XLA Modules:
  0.0 1193.4 jit_solution(18368938620581523959)
XLA Ops:
  12.0 53.6 %all-reduce = bf16[5120]{0:T(1024)(128)(2,1)S(1)} all-reduce(bf16[5120]{0:T(1024)(128)(2,1)S(1)} %dynamic-update-slice), channel_id=1, replica_groups=mesh['ep'=8,'fsdp'=16] {'fsdp'}, use_global_device_ids=true, to_apply=%add | all-reduce | flops 5120 | bytes 20480
  67.9 23.2 %all-gather = bf16[16,320,64]{1,2,0:T(8,128)(2,1)S(1)} all-gather(bf16[1,320,64]{1,2,0:T(8,128)(2,1)} %bitcast.64), channel_id=1, replica_groups=mesh['ep'=8,'fsdp'=16] {'fsdp'}, dimensions={0}, use_global_device_ids=true | all-gather | bytes 696320 | tf_op jit(solution)/shard_map/all_gather | solution.py:40
  99.3 7.4 mul.213
  106.8 5.7 convolution_convert_fusion.3
  112.5 7.1 broadcast_in_dim.12
  124.4 7.2 broadcast_in_dim.13
  131.6 16.4 %reshape.185 = bf16[8,16,6,5120]{3,1,2,0:T(8,128)(2,1)} reshape(bf16[8,8,2,6,5120]{4,2,1,3,0:T(2,128)(2,1)} %broadcast_in_dim.13) | data formatting | bytes 15728640 | tf_op jit(solution)/shard_map/reshape | solution.py:63
  148.0 7.0 all-to-all-start.4
  158.5 7.1 broadcast_in_dim.10
  170.3 7.3 broadcast_in_dim.11
  177.6 16.3 %reshape.181 = bf16[8,16,6,5120]{3,1,2,0:T(8,128)(2,1)} reshape(bf16[8,8,2,6,5120]{4,2,1,3,0:T(2,128)(2,1)} %broadcast_in_dim.11) | data formatting | bytes 15728640 | tf_op jit(solution)/shard_map/reshape | solution.py:63
  193.9 69.5 %all-to-all-done.4 = bf16[8,16,6,5120]{3,1,2,0:T(8,128)(2,1)} async-done(((bf16[8,16,6,5120]{3,1,2,0:T(8,128)(2,1)}), bf16[8,16,6,5120]{3,1,2,0:T(8,128)(2,1)}, u32[]{:S(2)}, u32[]{:S(2)}) %all-to-all-start.4) | async-done | bytes 7864352 | tf_op jit(solution)/shard_map/all_to_all | solution.py:65
  268.5 10.7 copy.129
  279.1 97.1 %all-to-all-done = bf16[8,16,6,5120]{3,1,2,0:T(8,128)(2,1)} async-done(((bf16[8,16,6,5120]{3,1,2,0:T(8,128)(2,1)}), bf16[8,16,6,5120]{3,1,2,0:T(8,128)(2,1)}, u32[]{:S(2)}, u32[]{:S(2)}) %all-to-all-start) | async-done | bytes 7864352 | tf_op jit(solution)/shard_map/all_to_all | solution.py:65
  376.3 16.6 %all-to-all-start.5 = ((bf16[8,16,6,5120]{3,0,2,1:T(8,128)(2,1)}), bf16[8,16,6,5120]{3,0,2,1:T(8,128)(2,1)}, u32[]{:S(2)}, u32[]{:S(2)}) async-start(bf16[8,16,6,5120]{3,0,2,1:T(8,128)(2,1)} %copy.129), calls=%async_computation.5 | async-start | bytes 15728640 | tf_op jit(solution)/shard_map/all_to_all | solution.py:64
  392.9 10.7 copy.119
  403.6 104.5 %all-to-all-done.5 = bf16[8,16,6,5120]{3,0,2,1:T(8,128)(2,1)} async-done(((bf16[8,16,6,5120]{3,0,2,1:T(8,128)(2,1)}), bf16[8,16,6,5120]{3,0,2,1:T(8,128)(2,1)}, u32[]{:S(2)}, u32[]{:S(2)}) %all-to-all-start.5) | async-done | bytes 7864352 | tf_op jit(solution)/shard_map/all_to_all | solution.py:64
  508.2 12.6 %all-to-all-start.1 = ((bf16[8,16,6,5120]{3,0,2,1:T(8,128)(2,1)}), bf16[8,16,6,5120]{3,0,2,1:T(8,128)(2,1)}, u32[]{:S(2)}, u32[]{:S(2)}) async-start(bf16[8,16,6,5120]{3,0,2,1:T(8,128)(2,1)} %copy.119), calls=%async_computation.1 | async-start | bytes 15728640 | tf_op jit(solution)/shard_map/all_to_all | solution.py:64
  520.8 11.5 copy.130
  532.3 13.2 %reshape.186 = bf16[768,5120]{1,0:T(8,128)(2,1)} reshape(bf16[8,16,6,5120]{3,2,1,0:T(8,128)(2,1)} %copy.130) | data formatting | bytes 15728640 | tf_op jit(solution)/shard_map/reshape | solution.py:71
  545.5 97.6 %all-to-all-done.1 = bf16[8,16,6,5120]{3,0,2,1:T(8,128)(2,1)} async-done(((bf16[8,16,6,5120]{3,0,2,1:T(8,128)(2,1)}), bf16[8,16,6,5120]{3,0,2,1:T(8,128)(2,1)}, u32[]{:S(2)}, u32[]{:S(2)}) %all-to-all-start.1) | async-done | bytes 7864352 | tf_op jit(solution)/shard_map/all_to_all | solution.py:64
  643.1 11.5 copy.120
  654.5 13.3 %reshape.182 = bf16[768,5120]{1,0:T(8,128)(2,1)} reshape(bf16[8,16,6,5120]{3,2,1,0:T(8,128)(2,1)} %copy.120) | data formatting | bytes 15728640 | tf_op jit(solution)/shard_map/reshape | solution.py:71
  667.8 11.2 fusion.6
  679.0 12.1 %convolution_convert_fusion.1 = bf16[768,5120]{1,0:T(8,128)(2,1)} fusion(bf16[1,768,5120]{2,1,0:T(8,128)(2,1)} %param.11, f32[768,768]{1,0:T(8,128)S(1)} %fusion.6), kind=kOutput, calls=%fused_computation.1 | convolution fusion | flops 6049038336 | bytes 18087936 | tf_op jit(solution)/shard_map/dot_general | solution.py:94
  691.2 7.5 fusion.24
  698.6 12.1 %convolution_convert_fusion = bf16[768,5120]{1,0:T(8,128)(2,1)} fusion(bf16[768,768]{1,0:T(8,128)(2,1)S(1)} %fusion.24, bf16[1,5120,768]{2,1,0:T(8,128)(2,1)} %param.10), kind=kOutput, calls=%fused_computation | convolution fusion | flops 6043729920 | bytes 16908288 | tf_op jit(solution)/shard_map/rh,dh->rd/dot_general | solution.py:110
  710.7 14.0 %reshape.187 = bf16[8,16,2,3,5120]{4,3,2,1,0:T(4,128)(2,1)} reshape(bf16[768,5120]{1,0:T(8,128)(2,1)} %convolution_convert_fusion) | data formatting | bytes 15728640 | tf_op jit(solution)/shard_map/reshape | solution.py:74
  724.7 14.0 %reshape.183 = bf16[8,16,2,3,5120]{4,3,2,1,0:T(4,128)(2,1)} reshape(bf16[768,5120]{1,0:T(8,128)(2,1)} %convolution_convert_fusion.1) | data formatting | bytes 15728640 | tf_op jit(solution)/shard_map/reshape | solution.py:74
  738.7 13.6 %constant_dynamic-slice_fusion.1 = (bf16[8,16,1,3,5120]{4,3,2,1,0:T(4,128)(2,1)}, bf16[8,16,1,3,5120]{4,3,2,1,0:T(4,128)(2,1)S(1)}, bf16[8,16,1,3,5120]{4,3,2,1,0:T(4,128)(2,1)S(1)}, bf16[8,16,1,3,5120]{4,3,2,1,0:T(4,128)(2,1)S(1)}) fusion(bf16[8,16,2,3,5120]{4,3,2,1,0:T(4,128)(2,1)} %reshape.187, s32[]{:T(128)S(6)} %select_n.36, s32[]{:T(128)S(6)} %select_n.37, ...), kind=kLoop, calls=%fused_computation.78 | loop fusion | bytes 31457288 | tf_op jit(solution)/shard_map/jit(dynamic_index_in_dim)/dynamic_slice | solution.py:75
  769.6 7.6 fusion
  777.3 47.9 %all-to-all-done.2 = bf16[8,16,3,5120]{3,1,2,0:T(8,128)(2,1)} async-done(((bf16[8,16,3,5120]{3,1,2,0:T(8,128)(2,1)}), bf16[8,16,3,5120]{3,1,2,0:T(8,128)(2,1)}, u32[]{:S(2)}, u32[]{:S(2)}) %all-to-all-start.2) | async-done | bytes 3932192 | tf_op jit(solution)/shard_map/all_to_all | solution.py:79
  830.1 6.2 copy.123
  836.3 48.8 %all-to-all-done.6 = bf16[8,16,3,5120]{3,1,2,0:T(8,128)(2,1)} async-done(((bf16[8,16,3,5120]{3,1,2,0:T(8,128)(2,1)}), bf16[8,16,3,5120]{3,1,2,0:T(8,128)(2,1)}, u32[]{:S(2)}, u32[]{:S(2)}) %all-to-all-start.6) | async-done | bytes 3932192 | tf_op jit(solution)/shard_map/all_to_all | solution.py:79
  885.1 9.5 all-to-all-start.3
  894.6 6.2 copy.133
  900.8 43.2 %all-to-all-done.3 = bf16[8,16,3,5120]{3,0,2,1:T(8,128)(2,1)} async-done(((bf16[8,16,3,5120]{3,0,2,1:T(8,128)(2,1)}), bf16[8,16,3,5120]{3,0,2,1:T(8,128)(2,1)}, u32[]{:S(2)}, u32[]{:S(2)}) %all-to-all-start.3) | async-done | bytes 3932192 | tf_op jit(solution)/shard_map/all_to_all | solution.py:78
  944.0 10.6 all-to-all-start.7
  956.5 7.8 copy.124
  964.3 8.3 reshape.198
  972.6 5.7 multiply_reduce_fusion
  978.3 25.7 %all-to-all-done.7 = bf16[8,16,3,5120]{3,0,2,1:T(8,128)(2,1)} async-done(((bf16[8,16,3,5120]{3,0,2,1:T(8,128)(2,1)}), bf16[8,16,3,5120]{3,0,2,1:T(8,128)(2,1)}, u32[]{:S(2)}, u32[]{:S(2)}) %all-to-all-start.7) | async-done | bytes 3932192 | tf_op jit(solution)/shard_map/all_to_all | solution.py:78
  1004.0 7.8 copy.134
  1011.8 8.2 reshape.199
  1020.0 5.4 convolution_reduce_fusion
  1027.5 5.2 fusion.11
  1037.8 70.6 %psum.15 = f32[5120]{0:T(1024)S(1)} all-reduce(f32[5120]{0:T(1024)S(1)} %get-tuple-element.6), channel_id=1, replica_groups=mesh['ep'=8,'fsdp'=16] {'ep','fsdp'}, use_global_device_ids=true, to_apply=%region_13.14 | all-reduce | flops 5120 | bytes 40960 | tf_op jit(solution)/shard_map/psum | solution.py:127
  1109.0 75.5 %all-reduce.3.cloned.1.call-done = f32[5120,64]{0,1:T(8,128)} async-done(((f32[5120,64]{0,1:T(8,128)}), f32[5120,64]{0,1:T(8,128)}) %all-reduce.3.cloned.1.call-update) | async-done | bytes 1310736 | tf_op jit(solution)/shard_map/psum | solution.py:127
  (104 shorter events, 66.2 us)
Async XLA Ops:
  9.1 85.6 %copy-start.17 = (f32[64,3]{0,1:T(4,128)}, f32[64,3]{0,1:T(4,128)S(1)}, u32[]{:S(2)}) copy-start(f32[64,3]{0,1:T(4,128)S(1)} %reduce-window.9) | copy-start | bytes 2308
  9.1 83.9 %copy-start = (bf16[128,5120]{1,0:T(8,128)(2,1)S(1)}, bf16[128,5120]{1,0:T(8,128)(2,1)}, u32[]{:S(2)}) copy-start(bf16[128,5120]{1,0:T(8,128)(2,1)} %param.7) | copy-start | bytes 3932164
  65.6 89.7 %copy-start.5 = (f32[5120]{0:T(1024)}, f32[5120]{0:T(1024)S(1)}, u32[]{:S(2)}) copy-start(f32[5120]{0:T(1024)S(1)} %convert_element_type.87) | copy-start | bytes 61444
  67.3 0.6 copy-start.18
  67.3 88.0 %copy-start.15 = (f32[128]{0:T(128)}, f32[128]{0:T(128)S(1)}, u32[]{:S(2)}) copy-start(f32[128]{0:T(128)S(1)} %fusion.42) | copy-start | bytes 1540
  91.0 3.7 copy-start.11
  91.0 4.5 copy-start.2
  94.8 0.5 copy-start.13
  95.3 4.0 copy-start.7
  99.3 7.4 slice-start.2
  106.8 5.7 copy-start.9
  148.0 115.5 %all-to-all-start.4 = ((bf16[8,16,6,5120]{3,1,2,0:T(8,128)(2,1)}), bf16[8,16,6,5120]{3,1,2,0:T(8,128)(2,1)}, u32[]{:S(2)}, u32[]{:S(2)}) async-start(bf16[8,16,6,5120]{3,1,2,0:T(8,128)(2,1)} %reshape.185), calls=%async_computation.4 | async-start | bytes 15728640 | tf_op jit(solution)/shard_map/all_to_all | solution.py:65
  263.4 112.8 %all-to-all-start = ((bf16[8,16,6,5120]{3,1,2,0:T(8,128)(2,1)}), bf16[8,16,6,5120]{3,1,2,0:T(8,128)(2,1)}, u32[]{:S(2)}, u32[]{:S(2)}) async-start(bf16[8,16,6,5120]{3,1,2,0:T(8,128)(2,1)} %reshape.181), calls=%async_computation | async-start | bytes 15728640 | tf_op jit(solution)/shard_map/all_to_all | solution.py:65
  376.3 131.9 %all-to-all-start.5 = ((bf16[8,16,6,5120]{3,0,2,1:T(8,128)(2,1)}), bf16[8,16,6,5120]{3,0,2,1:T(8,128)(2,1)}, u32[]{:S(2)}, u32[]{:S(2)}) async-start(bf16[8,16,6,5120]{3,0,2,1:T(8,128)(2,1)} %copy.129), calls=%async_computation.5 | async-start | bytes 15728640 | tf_op jit(solution)/shard_map/all_to_all | solution.py:64
  508.2 134.9 %all-to-all-start.1 = ((bf16[8,16,6,5120]{3,0,2,1:T(8,128)(2,1)}), bf16[8,16,6,5120]{3,0,2,1:T(8,128)(2,1)}, u32[]{:S(2)}, u32[]{:S(2)}) async-start(bf16[8,16,6,5120]{3,0,2,1:T(8,128)(2,1)} %copy.119), calls=%async_computation.1 | async-start | bytes 15728640 | tf_op jit(solution)/shard_map/all_to_all | solution.py:64
  667.8 23.3 %slice-start = ((s8[7864320]{0:T(1024)(128)(4,1)}), s8[4194304]{0:T(1024)(128)(4,1)S(1)}, s32[]{:S(2)}) async-start(s8[7864320]{0:T(1024)(128)(4,1)} %bitcast.61), calls=%async_computation.9 | async-start | bytes 8388608
  667.8 23.3 %slice-start.3 = ((s8[7864320]{0:T(1024)(128)(4,1)}), s8[4194304]{0:T(1024)(128)(4,1)S(1)}, s32[]{:S(2)}) async-start(s8[7864320]{0:T(1024)(128)(4,1)} %bitcast.65), calls=%async_computation.12 | async-start | bytes 8388608
  679.0 12.1 %slice-start.1 = ((s8[7864320]{0:T(1024)(128)(4,1)}), s8[3670016]{0:T(1024)(128)(4,1)S(1)}, s32[]{:S(2)}) async-start(s8[7864320]{0:T(1024)(128)(4,1)} %bitcast.61), calls=%async_computation.10 | async-start | bytes 7340032
  679.0 12.1 %slice-start.4 = ((s8[7864320]{0:T(1024)(128)(4,1)}), s8[3670016]{0:T(1024)(128)(4,1)S(1)}, s32[]{:S(2)}) async-start(s8[7864320]{0:T(1024)(128)(4,1)} %bitcast.65), calls=%async_computation.13 | async-start | bytes 7340032
  753.8 7.2 collective-permute-start
  758.1 11.5 collective-permute-start.1
  764.9 60.3 %all-to-all-start.2 = ((bf16[8,16,3,5120]{3,1,2,0:T(8,128)(2,1)}), bf16[8,16,3,5120]{3,1,2,0:T(8,128)(2,1)}, u32[]{:S(2)}, u32[]{:S(2)}) async-start(bf16[8,16,3,5120]{3,1,2,0:T(8,128)(2,1)} %fusion.1), calls=%async_computation.2 | async-start | bytes 7864320 | tf_op jit(solution)/shard_map/all_to_all | solution.py:79
  825.2 60.0 %all-to-all-start.6 = ((bf16[8,16,3,5120]{3,1,2,0:T(8,128)(2,1)}), bf16[8,16,3,5120]{3,1,2,0:T(8,128)(2,1)}, u32[]{:S(2)}, u32[]{:S(2)}) async-start(bf16[8,16,3,5120]{3,1,2,0:T(8,128)(2,1)} %fusion), calls=%async_computation.6 | async-start | bytes 7864320 | tf_op jit(solution)/shard_map/all_to_all | solution.py:79
  885.1 58.8 %all-to-all-start.3 = ((bf16[8,16,3,5120]{3,0,2,1:T(8,128)(2,1)}), bf16[8,16,3,5120]{3,0,2,1:T(8,128)(2,1)}, u32[]{:S(2)}, u32[]{:S(2)}) async-start(bf16[8,16,3,5120]{3,0,2,1:T(8,128)(2,1)} %copy.123), calls=%async_computation.3 | async-start | bytes 7864320 | tf_op jit(solution)/shard_map/all_to_all | solution.py:78
  944.0 60.0 %all-to-all-start.7 = ((bf16[8,16,3,5120]{3,0,2,1:T(8,128)(2,1)}), bf16[8,16,3,5120]{3,0,2,1:T(8,128)(2,1)}, u32[]{:S(2)}, u32[]{:S(2)}) async-start(bf16[8,16,3,5120]{3,0,2,1:T(8,128)(2,1)} %copy.133), calls=%async_computation.7 | async-start | bytes 7864320 | tf_op jit(solution)/shard_map/all_to_all | solution.py:78
  954.6 1.6 copy-start.10
  954.6 229.9 %all-reduce.3.cloned.1.call-start = ((), (), s32[]{:S(2)}) async-start(), calls=%async_computation.8 | async-start | bytes 2621440 | tf_op jit(solution)/shard_map/psum | solution.py:127
  964.3 8.3 copy-start.8
  972.6 5.7 copy-start.14
  972.6 5.7 copy-start.12
  1020.0 5.4 copy-start.1
  1020.0 5.4 copy-start.6
  1020.0 5.4 copy-start.16
  1025.4 2.0 copy-start.4
  1027.5 5.2 copy-start.19
  1027.5 5.2 copy-start.3
Sparse Core Ops, SparseCore 0:
  1032.8 151.6 all-reduce.2
where the time goes:
time: 1210 us; the launch traced here: 1190 us
  waiting for transfers between devices  613 us (51%)
  local copies, waits for them, and re-layouts  251 us (21%)
  blocking collectives  147 us (12%)
  starting transfers between devices  72 us (6%)
  matrix products  71.7 us (6%)
  other arithmetic  23.1 us (2%)
  between operations  15.4 us (1%)
    all_to_all x2, waiting for transfers between devices, dispatch(): lax.all_to_all(lax.all_to_all(blocks, 'ep', split_axis=0, concat_axis=0,...  202 us
    all_to_all x2, waiting for transfers between devices, dispatch(): lax.all_to_all(blocks, 'ep', split_axis=0, concat_axis=0, tiled=True)  167 us
    all_to_all x2, waiting for transfers between devices, collect(): lax.all_to_all(result, 'ep', split_axis=0, concat_axis=0, tiled=True)  96.7 us
    psum x1, waiting for transfers between devices, body(): lax.psum((router_term, gain_term), ('ep', 'fsdp'))  75.5 us
    psum x1, blocking collectives, body(): lax.psum((router_term, gain_term), ('ep', 'fsdp'))  70.6 us
    all_to_all x2, waiting for transfers between devices, collect(): lax.all_to_all(lax.all_to_all(result, 'ep', split_axis=0, concat_axis=0,...  68.8 us
    unnamed x1, blocking collectives  53.6 us
    broadcast_in_dim x6, local copies, waits for them, and re-layouts, dispatch(): jnp.broadcast_to(single, (ep_count, fsdp_count // 2, 2, capacity, features))  38.2 us
  transfers between devices with their start and end apart: 11, of which 10 were waited for; matrix products, arithmetic and copies ran while one was open for 12% of the time, Pallas kernels for 0%

commit v1 on v0

v1 whole, which is shorter than its diff:
```python
import math

import jax
import jax.numpy as jnp
import numpy as np
from jax import lax
from jax.experimental import pallas as pl
from jax.experimental.pallas import tpu as pltpu
from jax.sharding import Mesh
from jax.sharding import PartitionSpec as P

EPS = 1e-06
CAP = 6
PARTS = 4
TILE = 8
BANDS = CAP * PARTS // TILE
GROUP = 8
BF16 = jnp.bfloat16
F32 = jnp.float32
VMEM_LIMIT = 56 * 1024 * 1024
CHIPS = ("ep", "pair")
FSDP = ("pair", "core")
EVERY = ("ep", "pair", "core")


def params(steps):
    return pltpu.CompilerParams(
        dimension_semantics=("arbitrary",) * steps, vmem_limit_bytes=VMEM_LIMIT
    )


def cost(flops, bytes_accessed):
    return pl.CostEstimate(flops=flops, bytes_accessed=bytes_accessed, transcendentals=0)


def iota(shape, dim):
    return lax.broadcasted_iota(jnp.int32, shape, dim)


def dot(a, b):
    return jnp.dot(a, b, preferred_element_type=F32)


def dot_nt(a, b):
    return lax.dot_general(a, b, (((1,), (1,)), ((), ())), preferred_element_type=F32)


def as_bf16(mask):
    return mask.astype(F32).astype(BF16)


def shuffle_matrix():
    size = CAP * PARTS * GROUP
    matrix = np.zeros((size, size), np.float32)
    for message in range(GROUP):
        for number in range(CAP * PARTS):
            piece, slot = divmod(number, CAP)
            band, row = divmod(number, TILE)
            matrix[
                piece * GROUP * CAP + message * CAP + slot,
                band * GROUP * TILE + message * TILE + row,
            ] = 1.0
    return matrix


def slot_target(band, column):
    row = column & (TILE - 1)
    limit = CAP - 2 * band
    low = row < limit
    slot = 2 * band + row - jnp.where(low, 0, CAP)
    return (column >> 3) * CAP + slot, low


def pack_kernel(ids_ref, low_ref, high_ref, out_ref, pos_ref):
    band = pl.program_id(0)
    toks = ids_ref.shape[1]
    experts = out_ref.shape[0] // TILE

    @pl.when(band == 0)
    def _():
        first, second = ids_ref[0:1, :], ids_ref[1:2, :]
        expert = iota((experts, toks), 0)
        in_first, in_second = expert == first, expert == second
        both = as_bf16(in_first | in_second)
        earlier = as_bf16(iota((toks, toks), 0) < iota((toks, toks), 1))
        count = dot(both, earlier)
        slot_first = jnp.sum(jnp.where(in_first, count, 0.0), axis=0, keepdims=True)
        slot_second = jnp.sum(jnp.where(in_second, count, 0.0), axis=0, keepdims=True)
        pos_ref[0:1, :] = first * CAP + slot_first.astype(jnp.int32)
        pos_ref[1:2, :] = second * CAP + slot_second.astype(jnp.int32)

    target, low = slot_target(band, iota((out_ref.shape[0], toks), 0))
    hit = (target == pos_ref[0:1, :]) | (target == pos_ref[1:2, :])
    placing = jnp.concatenate([as_bf16(hit & low), as_bf16(hit & ~low)], axis=1)
    pieces = jnp.concatenate([low_ref[...], high_ref[...]], axis=0)
    out_ref[...] = dot(placing, pieces).astype(BF16)


def pack(ids_t, rows, experts):
    toks, features = rows.shape
    piece = features // PARTS
    out_rows = experts * TILE
    return pl.pallas_call(
        pack_kernel,
        grid=(BANDS,),
        in_specs=[
            pl.BlockSpec((2, toks), lambda b: (0, 0)),
            pl.BlockSpec((toks, piece), lambda b: (0, b)),
            pl.BlockSpec((toks, piece), lambda b: (0, b + 1)),
        ],
        out_specs=pl.BlockSpec((out_rows, piece), lambda b: (0, b)),
        out_shape=jax.ShapeDtypeStruct((out_rows, BANDS * piece), BF16),
        scratch_shapes=[pltpu.VMEM((8, toks), jnp.int32)],
        compiler_params=params(1),
        cost_estimate=cost(2 * BANDS * out_rows * 2 * toks * piece, 2 * out_rows * BANDS * piece),
        name="pack",
    )(ids_t, rows, rows)


def fill_choosing(ids_ref, choose_ref):
    toks = ids_ref.shape[0]
    columns = choose_ref.shape[2]
    experts = columns // TILE
    first, second = ids_ref[:, 0:1], ids_ref[:, 1:2]
    expert = iota((toks, experts), 1)
    in_first, in_second = expert == first, expert == second
    both = as_bf16(in_first | in_second)
    earlier = as_bf16(iota((toks, toks), 1) < iota((toks, toks), 0))
    count = dot(earlier, both)
    pos_first = first * CAP + jnp.sum(
        jnp.where(in_first, count, 0.0), axis=1, keepdims=True
    ).astype(jnp.int32)
    pos_second = second * CAP + jnp.sum(
        jnp.where(in_second, count, 0.0), axis=1, keepdims=True
    ).astype(jnp.int32)
    for band in range(BANDS):
        target, low = slot_target(band, iota((toks, columns), 1))
        hit = (target == pos_first) | (target == pos_second)
        choose_ref[band, :toks, :] = as_bf16(hit & low)
        choose_ref[band, toks:, :] = as_bf16(hit & ~low)


def summed_pieces(choose_ref, band_refs):
    toks = choose_ref.shape[1] // 2
    sums = [dot(choose_ref[band], band_refs[band][...]) for band in range(BANDS)]
    pieces = [sums[0][:toks]]
    for band in range(1, BANDS):
        pieces.append(sums[band - 1][toks:] + sums[band][:toks])
    pieces.append(sums[BANDS - 1][toks:])
    return pieces


def mixed_kernel(ids_ref, tokens_ref, band0, band1, band2, out_ref, choose_ref):
    step = pl.program_id(0)
    width = band0.shape[1]
    piece = tokens_ref.shape[1] // PARTS

    @pl.when(step == 0)
    def _():
        fill_choosing(ids_ref, choose_ref)

    for number, value in enumerate(summed_pieces(choose_ref, (band0, band1, band2))):
        cols = pl.ds(pl.multiple_of(number * piece + step * width, width), width)
        out_ref[:, cols] = (tokens_ref[:, cols].astype(F32) + value).astype(BF16)


def grad_tokens_kernel(
    ids_ref, tokens_ref, cot_ref, band0, band1, band2, out_ref, choose_ref, grad_ref, square_ref, cross_ref
):
    step = pl.program_id(0)
    width = band0.shape[1]
    features = tokens_ref.shape[1]
    piece = features // PARTS

    @pl.when(step == 0)
    def _():
        fill_choosing(ids_ref, choose_ref)
        square_ref[...] = jnp.zeros_like(square_ref)
        cross_ref[...] = jnp.zeros_like(cross_ref)

    for number, value in enumerate(summed_pieces(choose_ref, (band0, band1, band2))):
        cols = pl.ds(pl.multiple_of(number * piece + step * width, width), width)
        x = tokens_ref[:, cols].astype(F32)
        grad_ref[:, cols] = value
        square_ref[...] += x * x
        cross_ref[...] += x * value

    @pl.when(step == pl.num_programs(0) - 1)
    def _():
        scale = lax.rsqrt(jnp.sum(square_ref[...], axis=1, keepdims=True) / features + EPS)
        back = jnp.sum(cross_ref[...], axis=1, keepdims=True) / features * scale * scale * scale
        for at in range(0, features, width):
            cols = slice(at, at + width)
            x = tokens_ref[:, cols].astype(F32)
            grad = scale * grad_ref[:, cols] - x * back
            out_ref[:, cols] = (cot_ref[:, cols].astype(F32) + grad).astype(BF16)


def token_side(kernel, ids, row_inputs, bands, scratch, name):
    toks, features = row_inputs[0].shape
    piece = features // PARTS
    width = 256
    steps = piece // width
    columns = bands.shape[0]

    def band_spec(band):
        return pl.BlockSpec((columns, width), lambda c, band=band: (0, band * steps + c))

    return pl.pallas_call(
        kernel,
        grid=(steps,),
        in_specs=[pl.BlockSpec((toks, 2), lambda c: (0, 0))]
        + [pl.BlockSpec((toks, features), lambda c: (0, 0))] * len(row_inputs)
        + [band_spec(band) for band in range(BANDS)],
        out_specs=pl.BlockSpec((toks, features), lambda c: (0, 0)),
        out_shape=jax.ShapeDtypeStruct((toks, features), BF16),
        scratch_shapes=[pltpu.VMEM((BANDS, 2 * toks, columns), BF16)] + scratch,
        compiler_params=params(1),
        cost_estimate=cost(2 * BANDS * 2 * toks * columns * piece, 2 * columns * BANDS * piece),
        name=name,
    )(ids, *row_inputs, *([bands] * BANDS))


def unpacked(block, shuffle):
    piece = block.shape[1] // BANDS
    stacked = jnp.concatenate([block[:, b * piece : (b + 1) * piece] for b in range(BANDS)], axis=0)
    rows = dot(shuffle, stacked)
    count = GROUP * CAP
    return [rows[q * count : (q + 1) * count] for q in range(PARTS)]


def store_packed(out_ref, pieces, shuffle_back):
    piece = pieces[0].shape[1]
    bands = dot(shuffle_back, jnp.concatenate(pieces, axis=0)).astype(BF16)
    count = GROUP * TILE
    for b in range(BANDS):
        out_ref[:, b * piece : (b + 1) * piece] = bands[b * count : (b + 1) * count]


def spread(column, ref):
    ref[...] = jnp.broadcast_to(column, ref.shape)


def row_fold(value):
    total = value[0:8]
    for at in range(8, value.shape[0], 8):
        total = total + value[at : at + 8]
    return total


def norm_kernel(block_ref, shuffle_ref, gain_ref, column_ref, normed_ref, unit_ref, gate_ref):
    pieces = unpacked(block_ref[...], shuffle_ref[...])
    piece = pieces[0].shape[1]
    square = sum(jnp.sum(x * x, axis=1, keepdims=True) for x in pieces)
    scale = lax.rsqrt(square / (piece * PARTS) + EPS)
    logit = 0.0
    for q, x in enumerate(pieces):
        cols = slice(q * piece, (q + 1) * piece)
        unit = x * scale
        normed = (unit * gain_ref[:, cols]).astype(BF16)
        unit_ref[:, cols] = unit.astype(BF16)
        normed_ref[:, cols] = normed
        logit = logit + jnp.sum(normed.astype(F32) * column_ref[:, cols], axis=1, keepdims=True)
    spread(jax.nn.sigmoid(logit), gate_ref)


def out_kernel(own_ref, other_ref, gate_ref, back_ref, result_ref, send_ref):
    gate = gate_ref[:, 0:1]
    piece = own_ref.shape[1] // PARTS
    gated = []
    for q in range(PARTS):
        cols = slice(q * piece, (q + 1) * piece)
        result = (own_ref[:, cols].astype(F32) + other_ref[:, cols].astype(F32)).astype(BF16)
        result_ref[:, cols] = result
        gated.append((gate * result.astype(F32)).astype(BF16))
    store_packed(send_ref, gated, back_ref[...])


def cot_kernel(block_ref, shuffle_ref, gate_ref, result_ref, normed_ref, gated_ref, choice_ref, router_ref):
    pieces = unpacked(block_ref[...], shuffle_ref[...])
    piece = pieces[0].shape[1]
    gate = gate_ref[:, 0:1]
    total = 0.0
    for q, cot in enumerate(pieces):
        cols = slice(q * piece, (q + 1) * piece)
        gated_ref[:, cols] = (gate * cot).astype(BF16)
        total = total + jnp.sum(cot * result_ref[:, cols].astype(F32), axis=1, keepdims=True)
    choice = total * gate * (1.0 - gate)
    spread(choice, choice_ref)

    @pl.when(pl.program_id(0) == 0)
    def _():
        router_ref[...] = jnp.zeros_like(router_ref)

    for q in range(PARTS):
        cols = slice(q * piece, (q + 1) * piece)
        router_ref[:, cols] += row_fold(normed_ref[:, cols].astype(F32) * choice)


def grad_kernel(
    own_ref, other_ref, choice_ref, unit_ref, column_ref, gain_ref, back_ref, send_ref, gain_sum_ref
):
    choice = choice_ref[:, 0:1]
    piece = own_ref.shape[1] // PARTS

    @pl.when(pl.program_id(0) == 0)
    def _():
        gain_sum_ref[...] = jnp.zeros_like(gain_sum_ref)

    scaled = []
    for q in range(PARTS):
        cols = slice(q * piece, (q + 1) * piece)
        rows = (own_ref[:, cols].astype(F32) + other_ref[:, cols].astype(F32)).astype(BF16)
        grad = rows.astype(F32) + choice * column_ref[:, cols]
        gain_sum_ref[:, cols] += row_fold(grad * unit_ref[:, cols].astype(F32))
        scaled.append((grad * gain_ref[:, cols]).astype(BF16))
    store_packed(send_ref, scaled, back_ref[...])


def by_group(kernel, inputs, outputs, flops, name):
    groups = None
    for value, rows in inputs:
        if rows:
            groups = value.shape[0] // rows

    def spec(shape, rows):
        if rows:
            return pl.BlockSpec((rows, shape[1]), lambda g: (g, 0))
        return pl.BlockSpec(shape, lambda g: (0, 0))

    moved = sum(value.size * value.dtype.itemsize for value, _ in inputs)
    moved += sum(math.prod(shape) * dtype.itemsize for shape, dtype, _ in outputs)
    return pl.pallas_call(
        kernel,
        grid=(groups,),
        in_specs=[spec(value.shape, rows) for value, rows in inputs],
        out_specs=[spec(shape, rows) for shape, _, rows in outputs],
        out_shape=[jax.ShapeDtypeStruct(shape, dtype) for shape, dtype, _ in outputs],
        compiler_params=params(1),
        cost_estimate=cost(flops, moved),
        name=name,
    )(*[value for value, _ in inputs])


def forward_kernel(x_ref, up_ref, down_ref, out_ref, slope_ref, acc_ref, hidden_ref):
    step = pl.program_id(0)
    half = pl.num_programs(0) // 2

    @pl.when(step == 0)
    def _():
        acc_ref[...] = dot(x_ref[...], up_ref[...])

    @pl.when((step > 0) & (step < half))
    def _():
        acc_ref[...] += dot(x_ref[...], up_ref[...])

    @pl.when(step == half - 1)
    def _():
        pre = acc_ref[...]
        root = math.sqrt(2.0 / math.pi)
        square = pre * pre
        bend = jnp.tanh(root * (pre + 0.044715 * (square * pre)))
        share = 0.5 * (1.0 + bend)
        hidden_ref[...] = (pre * share).astype(BF16)
        inner = root * (1.0 + (3.0 * 0.044715) * square)
        slope_ref[...] = share + 0.5 * pre * (1.0 - bend * bend) * inner

    @pl.when(step >= half)
    def _():
        out_ref[...] = dot(hidden_ref[...], down_ref[...]).astype(BF16)


def backward_kernel(cot_ref, down_ref, up_ref, slope_ref, out_ref, acc_ref, grad_ref):
    step = pl.program_id(0)
    half = pl.num_programs(0) // 2

    @pl.when(step == 0)
    def _():
        acc_ref[...] = dot_nt(cot_ref[...], down_ref[...])

    @pl.when((step > 0) & (step < half))
    def _():
        acc_ref[...] += dot_nt(cot_ref[...], down_ref[...])

    @pl.when(step == half - 1)
    def _():
        grad_ref[...] = (acc_ref[...] * slope_ref[...]).astype(BF16)

    @pl.when(step >= half)
    def _():
        out_ref[...] = dot_nt(grad_ref[...], up_ref[...]).astype(BF16)


def expert_call(kernel, rows, up, down, slope, name):
    count, features = rows.shape
    hidden = up.shape[2]
    block = features // PARTS
    half = features // block

    def first(i):
        return jnp.minimum(i, half - 1)

    def second(i):
        return jnp.maximum(i - half, 0)

    rows_spec = pl.BlockSpec((count, block), lambda i: (0, first(i)))
    slope_spec = pl.BlockSpec((count, hidden), lambda i: (0, 0))
    out_spec = pl.BlockSpec((count, block), lambda i: (0, second(i)))
    out_shape = jax.ShapeDtypeStruct((count, features), BF16)
    forward = slope is None
    early, late = (first, second) if forward else (second, first)
    up_spec = pl.BlockSpec((None, block, hidden), lambda i: (0, early(i), 0))
    down_spec = pl.BlockSpec((None, hidden, block), lambda i: (0, 0, late(i)))
    if forward:
        args, in_specs = (rows, up, down), [rows_spec, up_spec, down_spec]
        out_specs = [out_spec, slope_spec]
        out_shape = [out_shape, jax.ShapeDtypeStruct((count, hidden), F32)]
    else:
        args, in_specs = (rows, down, up, slope), [rows_spec, down_spec, up_spec, slope_spec]
        out_specs = out_spec
    return pl.pallas_call(
        kernel,
        grid=(2 * half,),
        in_specs=in_specs,
        out_specs=out_specs,
        out_shape=out_shape,
        scratch_shapes=[pltpu.VMEM((count, hidden), F32), pltpu.VMEM((count, hidden), BF16)],
        compiler_params=params(1),
        cost_estimate=cost(4 * count * features * hidden, 4 * features * (count + hidden)),
        name=name,
    )(*args)


def exchange(messages):
    blocks = messages.reshape(-1, TILE, messages.shape[1])
    blocks = lax.all_to_all(blocks, CHIPS, split_axis=0, concat_axis=0, tiled=True)
    return blocks.reshape(messages.shape)


def swap(value):
    return lax.ppermute(value, "core", [(0, 1), (1, 0)])


def body(tokens, norm_gain, router_weight, up_weight, down_weight, expert_ids, cotangent):
    toks, features = tokens.shape
    eps, pairs, cores = (lax.axis_size(name) for name in EVERY)
    experts = eps * pairs
    shard = features // (pairs * cores)
    rows = experts * CAP
    devices = experts * cores

    columns = lax.dynamic_slice_in_dim(router_weight, lax.axis_index("ep") * pairs, pairs, 1).T
    parcel = jnp.stack([jnp.broadcast_to(norm_gain, columns.shape), columns], axis=1)
    parcel = jnp.broadcast_to(parcel[:, None], (pairs, cores, 2, shard)).reshape(-1, 2, shard)
    parcel = lax.all_to_all(parcel, FSDP, split_axis=0, concat_axis=0, tiled=True)
    gain = parcel[:, 0].reshape(1, features).astype(F32)
    column = parcel[:, 1].reshape(1, features).astype(F32)

    matrix = shuffle_matrix()
    shuffle, shuffle_back = jnp.asarray(matrix, BF16), jnp.asarray(matrix.T, BF16)
    ids_t = expert_ids.T
    group_rows, group_tiles = GROUP * CAP, GROUP * TILE
    row_shape, send_shape = (rows, features), (experts * TILE, features * CAP // TILE)
    wide, narrow = (rows, 128), (8, features)
    shuffling = 2 * rows * features * CAP * PARTS * GROUP // PARTS
    b16, f32 = jnp.dtype(BF16), jnp.dtype(F32)

    arrived = exchange(pack(ids_t, tokens, experts))
    cot_sent = pack(ids_t, cotangent, experts)
    normed, unit, gate = by_group(
        norm_kernel,
        [(arrived, group_tiles), (shuffle, 0), (gain, 0), (column, 0)],
        [(row_shape, b16, group_rows), (row_shape, b16, group_rows), (wide, f32, group_rows)],
        shuffling,
        "norm",
    )
    cot_arrived = exchange(cot_sent)
    normed_other = swap(normed)
    own_part, own_slope = expert_call(forward_kernel, normed, up_weight, down_weight, None, "forward")
    other_part, other_slope = expert_call(
        forward_kernel, normed_other, up_weight, down_weight, None, "forward"
    )
    result, result_sent = by_group(
        out_kernel,
        [(own_part, group_rows), (swap(other_part), group_rows), (gate, group_rows), (shuffle_back, 0)],
        [(row_shape, b16, group_rows), (send_shape, b16, group_tiles)],
        shuffling,
        "out",
    )
    gated, choice, router_sum = by_group(
        cot_kernel,
        [
            (cot_arrived, group_tiles),
            (shuffle, 0),
            (gate, group_rows),
            (result, group_rows),
            (normed, group_rows),
        ],
        [(row_shape, b16, group_rows), (wide, f32, group_rows), (narrow, f32, 0)],
        shuffling,
        "cot",
    )
    result_back = exchange(result_sent)
    gated_other = swap(gated)
    own_grad = expert_call(backward_kernel, gated, up_weight, down_weight, own_slope, "backward")
    other_grad = expert_call(
        backward_kernel, gated_other, up_weight, down_weight, other_slope, "backward"
    )
    grad_sent, gain_sum = by_group(
        grad_kernel,
        [
            (own_grad, group_rows),
            (swap(other_grad), group_rows),
            (choice, group_rows),
            (unit, group_rows),
            (column, 0),
            (gain, 0),
            (shuffle_back, 0),
        ],
        [(send_shape, b16, group_tiles), (narrow, f32, 0)],
        shuffling,
        "grad",
    )
    grad_back = exchange(grad_sent)
    mixed = token_side(mixed_kernel, expert_ids, [tokens], result_back, [], "mixed")
    grad_tokens = token_side(
        grad_tokens_kernel,
        expert_ids,
        [tokens, cotangent],
        grad_back,
        [
            pltpu.VMEM((toks, features), F32),
            pltpu.VMEM((toks, 256), F32),
            pltpu.VMEM((toks, 256), F32),
        ],
        "grad_tokens",
    )

    sums = jnp.stack([jnp.sum(router_sum, axis=0), jnp.sum(gain_sum, axis=0)])
    sums = sums.reshape(2, pairs * cores, shard).transpose(1, 0, 2).reshape(1, pairs * cores, 2 * shard)
    sums = jnp.broadcast_to(sums, (eps, pairs * cores, 2 * shard)).reshape(devices, 2 * shard)
    sums = lax.all_to_all(sums, EVERY, split_axis=0, concat_axis=0, tiled=True)
    scale = 1.0 / math.sqrt(toks * devices)
    grad_router = jnp.sum(sums[:, :shard].reshape(experts, cores, shard), axis=1).T * scale
    grad_gain = jnp.sum(sums[:, shard:], axis=0) * scale
    return mixed, grad_tokens, grad_router, grad_gain


def solution(mesh):
    eps, fsdp = mesh.devices.shape
    fine = Mesh(mesh.devices.reshape(eps, fsdp // 2, 2), EVERY)
    in_specs = (
        P(EVERY, None),
        P(FSDP),
        P(FSDP, None),
        P(EVERY, None, None),
        P(EVERY, None, None),
        P(EVERY, None),
        P(EVERY, None),
    )
    out_specs = (P(EVERY, None), P(EVERY, None), P(FSDP, None), P(FSDP))
    return jax.shard_map(body, mesh=fine, in_specs=in_specs, out_specs=out_specs, check_vma=False)
```

time: 1210 us -> 355 us (0.29); the launches traced: 1190 us -> 352 us
  waiting for transfers between devices: 613 us -> 148 us
  local copies, waits for them, and re-layouts: 251 us -> 8.86 us
  blocking collectives: 147 us -> 21.4 us
  Pallas kernels: 0 us -> 124 us
  matrix products: 71.7 us -> 0 us
  starting transfers between devices: 72 us -> 45.8 us
  other arithmetic: 23.1 us -> 2.79 us
  between operations: 15.4 us -> 0.79 us
    all_to_all x8 -> x5, waiting for transfers between devices: 534 us -> 135 us  [the longest x4 134 us: exchange(): lax.all_to_all(blocks, CHIPS, split_axis=0, concat_axis=0, tiled=True)]
    pallas_call x0 -> x12, Pallas kernels: none -> 124 us  [the longest x4 59.8 us: expert_call(): pl.pallas_call(kernel, grid=(2 * half,), in_specs=in_specs, out_specs=out...]
    reshape x9 -> x1, local copies, waits for them, and re-layouts: 104 us -> 0.11 us  [body(): sums[:, :shard].reshape(experts, cores, shard)]
    psum x1 -> x0, waiting for transfers between devices: 75.5 us -> none  [body(): lax.psum((router_term, gain_term), ('ep', 'fsdp'))]
    all_to_all x8 -> x1, local copies, waits for them, and re-layouts: 72.4 us -> 0.31 us  [body(): sums = lax.all_to_all(sums, EVERY, split_axis=0, concat_axis=0, tiled=True)]
    dot_general x11 -> x0, matrix products: 71.7 us -> none  [the longest x1 12.1 us: body(): jnp.dot(hidden_f.astype(jnp.bfloat16), down_own, preferred_element_type=j...]
    psum x1 -> x0, blocking collectives: 70.6 us -> none  [body(): lax.psum((router_term, gain_term), ('ep', 'fsdp'))]
    unnamed x1 -> x0, blocking collectives: 53.6 us -> none
  transfers between devices with their start and end apart: 11 -> 9, of which waited for: 10 -> 7; matrix products, arithmetic and copies ran while one was open for 12% -> 2% of each run, Pallas kernels for 0% -> 19%
where the time goes in v1:
time: 355 us; the launch traced here: 352 us
  waiting for transfers between devices  148 us (42%)
  Pallas kernels  124 us (35%)
  starting transfers between devices  45.8 us (13%)
  blocking collectives  21.4 us (6%)
  local copies, waits for them, and re-layouts  8.86 us (2%)
    all_to_all x4, waiting for transfers between devices, exchange(): lax.all_to_all(blocks, CHIPS, split_axis=0, concat_axis=0, tiled=True)  134 us
    pallas_call x4, Pallas kernels, expert_call(): pl.pallas_call(kernel, grid=(2 * half,), in_specs=in_specs, out_specs=out...  59.8 us
    pallas_call x4, Pallas kernels, by_group(): pl.pallas_call(kernel, grid=(groups,), in_specs=[spec(value.shape, rows)...  39.3 us
    all_to_all x4, starting transfers between devices, exchange(): lax.all_to_all(blocks, CHIPS, split_axis=0, concat_axis=0, tiled=True)  33.1 us
    all_to_all x1, blocking collectives, body(): sums = lax.all_to_all(sums, EVERY, split_axis=0, concat_axis=0, tiled=True)  21.4 us
    pallas_call x2, Pallas kernels, token_side(): pl.pallas_call(kernel, grid=(steps,), in_specs=[pl.BlockSpec((toks, 2), l...  14.6 us
    ppermute x4, waiting for transfers between devices, swap(): return lax.ppermute(value, 'core', [(0, 1), (1, 0)])  13.2 us
    pallas_call x2, Pallas kernels, pack(): pl.pallas_call(pack_kernel, grid=(BANDS,), in_specs=[pl.BlockSpec((2, tok...  10.1 us
  transfers between devices with their start and end apart: 9, of which 7 were waited for; matrix products, arithmetic and copies ran while one was open for 2% of the time, Pallas kernels for 19%

profile of v1, /device:TPU:1, one launch (start us, length us, event | category | flops | bytes accessed | tf_op | source)
XLA Modules:
  0.0 351.8 jit_solution(4198073457706509808)
XLA Ops:
  0.7 0.8 copy-done
  1.4 0.7 stack_broadcast_in_dim.3
  2.2 0.6 broadcast_in_dim.6
  2.8 7.3 %all-to-all-start.1 = ((bf16[16,2,320]{2,1,0:T(2,128)(2,1)}), bf16[16,2,320]{2,1,0:T(2,128)(2,1)S(1)}, u32[]{:S(2)}, u32[]{:S(2)}) async-start(bf16[16,2,320]{2,1,0:T(2,128)(2,1)} %bitcast.5), calls=%async_computation.1 | async-start | bytes 49152 | tf_op jit(solution)/shard_map/all_to_all | solution.py:455
  10.1 5.1 %pack.2 = bf16[512,3840]{1,0:T(8,128)(2,1)} custom-call(s32[2,128]{1,0:T(2,128)} %bitcast.26, bf16[128,5120]{1,0:T(8,128)(2,1)} %tokens_ref.3, bf16[128,5120]{1,0:T(8,128)(2,1)} %tokens_ref.3), custom_call_target="tpu_custom_call" | custom-call | flops 1006632960 | bytes 3932160 | tf_op jit(solution)/shard_map/pack/pallas_call | solution.py:103
  15.2 0.8 all-to-all-done.1
  15.9 10.1 %all-to-all-start = ((bf16[64,8,3840]{2,1,0:T(8,128)(2,1)}), bf16[64,8,3840]{2,1,0:T(8,128)(2,1)}, u32[]{:S(2)}, u32[]{:S(2)}) async-start(bf16[64,8,3840]{2,1,0:T(8,128)(2,1)} %bitcast.21), calls=%async_computation | async-start | bytes 7864320 | tf_op jit(solution)/shard_map/all_to_all | solution.py:436
  26.1 0.1 fusion
  26.2 0.7 reshape.88.gain_ref
  26.9 0.7 reshape.89.column_ref
  27.6 47.3 %all-to-all-done = bf16[64,8,3840]{2,1,0:T(8,128)(2,1)} async-done(((bf16[64,8,3840]{2,1,0:T(8,128)(2,1)}), bf16[64,8,3840]{2,1,0:T(8,128)(2,1)}, u32[]{:S(2)}, u32[]{:S(2)}) %all-to-all-start) | async-done | bytes 3932192 | tf_op jit(solution)/shard_map/all_to_all | solution.py:436
  74.9 9.4 %norm.1 = (bf16[384,5120]{1,0:T(8,128)(2,1)}, bf16[384,5120]{1,0:T(8,128)(2,1)}, f32[384,128]{1,0:T(8,128)}) custom-call(bf16[512,3840]{1,0:T(8,128)(2,1)} %bitcast.2.block_ref, bf16[192,192]{1,0:T(8,128)(2,1)} %constant.21.clone.shuffle_ref, f32[1,5120]{1,0:T(1,128)} %reshape.88.gain_ref, f32[1,5120]{1,0:T(1,128)} %reshape.89.column_ref), custom_call_target="tpu_custom_call" | custom-call | flops 188743680 | bytes 12107776 | tf_op jit(solution)/shard_map/norm/pallas_call | solution.py:333
  84.4 2.3 collective-permute-start
  86.6 6.6 %collective-permute-done.x_ref = bf16[384,5120]{1,0:T(8,128)(2,1)S(1)} collective-permute-done((bf16[384,5120]{1,0:T(8,128)(2,1)}, bf16[384,5120]{1,0:T(8,128)(2,1)S(1)}, u32[]{:S(2)}, u32[]{:S(2)}) %collective-permute-start) | collective-permute-done | bytes 3932192 | tf_op jit(solution)/shard_map/ppermute | solution.py:441
  93.2 1.9 copy-done.5
  95.2 14.9 %forward.3 = (bf16[384,5120]{1,0:T(8,128)(2,1)}, f32[384,768]{1,0:T(8,128)}) custom-call(bf16[384,5120]{1,0:T(8,128)(2,1)} %copy-done.5, bf16[1,5120,768]{2,1,0:T(8,128)(2,1)} %up_ref.7, bf16[1,768,5120]{2,1,0:T(8,128)(2,1)} %down_ref.7), custom_call_target="tpu_custom_call" | custom-call | flops 6039797760 | bytes 23592960 | tf_op jit(solution)/shard_map/forward/pallas_call | solution.py:421
  110.1 0.4 collective-permute-start.1
  110.5 5.0 %pack.3 = bf16[512,3840]{1,0:T(8,128)(2,1)} custom-call(s32[2,128]{1,0:T(2,128)} %bitcast.27, bf16[128,5120]{1,0:T(8,128)(2,1)} %cot_ref.1, bf16[128,5120]{1,0:T(8,128)(2,1)} %cot_ref.1), custom_call_target="tpu_custom_call" | custom-call | flops 1006632960 | bytes 3932160 | tf_op jit(solution)/shard_map/pack/pallas_call | solution.py:103
  115.5 8.3 %all-to-all-start.3 = ((bf16[64,8,3840]{2,1,0:T(8,128)(2,1)}), bf16[64,8,3840]{2,1,0:T(8,128)(2,1)}, u32[]{:S(2)}, u32[]{:S(2)}) async-start(bf16[64,8,3840]{2,1,0:T(8,128)(2,1)} %bitcast.22), calls=%async_computation.3 | async-start | bytes 7864320 | tf_op jit(solution)/shard_map/all_to_all | solution.py:436
  123.8 14.9 %forward.2 = (bf16[384,5120]{1,0:T(8,128)(2,1)}, f32[384,768]{1,0:T(8,128)}) custom-call(bf16[384,5120]{1,0:T(8,128)(2,1)} %get-tuple-element.18.x_ref.normed_ref, bf16[1,5120,768]{2,1,0:T(8,128)(2,1)} %up_ref.7, bf16[1,768,5120]{2,1,0:T(8,128)(2,1)} %down_ref.7), custom_call_target="tpu_custom_call" | custom-call | flops 6039797760 | bytes 23592960 | tf_op jit(solution)/shard_map/forward/pallas_call | solution.py:421
  138.7 9.7 %out.1 = (bf16[384,5120]{1,0:T(8,128)(2,1)}, bf16[512,3840]{1,0:T(8,128)(2,1)}) custom-call(bf16[384,5120]{1,0:T(8,128)(2,1)} %get-tuple-element.19.own_ref, bf16[384,5120]{1,0:T(8,128)(2,1)} %collective-permute-done.1.other_ref, f32[384,128]{1,0:T(8,128)} %get-tuple-element.21.gate_ref, bf16[192,192]{1,0:T(8,128)(2,1)} %constant.22.clone.back_ref), custom_call_target="tpu_custom_call" | custom-call | flops 188743680 | bytes 15998976 | tf_op jit(solution)/shard_map/out/pallas_call | solution.py:333
  148.4 24.6 %all-to-all-done.3 = bf16[64,8,3840]{2,1,0:T(8,128)(2,1)} async-done(((bf16[64,8,3840]{2,1,0:T(8,128)(2,1)}), bf16[64,8,3840]{2,1,0:T(8,128)(2,1)}, u32[]{:S(2)}, u32[]{:S(2)}) %all-to-all-start.3) | async-done | bytes 3932192 | tf_op jit(solution)/shard_map/all_to_all | solution.py:436
  173.0 9.8 %cot.1 = (bf16[384,5120]{1,0:T(8,128)(2,1)}, f32[384,128]{1,0:T(8,128)}, f32[8,5120]{1,0:T(8,128)}) custom-call(bf16[512,3840]{1,0:T(8,128)(2,1)} %bitcast.9.block_ref, bf16[192,192]{1,0:T(8,128)(2,1)} %constant.21.clone.shuffle_ref, f32[384,128]{1,0:T(8,128)} %get-tuple-element.21.gate_ref, bf16[384,5120]{1,0:T(8,128)(2,1)} %get-tuple-element.23.result_ref, ...), custom_call_target="tpu_custom_call" | custom-call | flops 188743680 | bytes 16359424 | tf_op jit(solution)/shard_map/cot/pallas_call | solution.py:333
  182.8 2.4 collective-permute-start.2
  185.2 6.6 %collective-permute-done.2.cot_ref = bf16[384,5120]{1,0:T(8,128)(2,1)S(1)} collective-permute-done((bf16[384,5120]{1,0:T(8,128)(2,1)}, bf16[384,5120]{1,0:T(8,128)(2,1)S(1)}, u32[]{:S(2)}, u32[]{:S(2)}) %collective-permute-start.2) | collective-permute-done | bytes 3932192 | tf_op jit(solution)/shard_map/ppermute | solution.py:441
  191.8 1.9 copy-done.2
  193.8 15.0 %backward.3 = bf16[384,5120]{1,0:T(8,128)(2,1)} custom-call(bf16[384,5120]{1,0:T(8,128)(2,1)} %copy-done.2, bf16[1,768,5120]{2,1,0:T(8,128)(2,1)} %down_ref.7, bf16[1,5120,768]{2,1,0:T(8,128)(2,1)} %up_ref.7, f32[384,768]{1,0:T(8,128)} %get-tuple-element.26.slope_ref), custom_call_target="tpu_custom_call" | custom-call | flops 6039797760 | bytes 23592960 | tf_op jit(solution)/shard_map/backward/pallas_call | solution.py:421
  208.7 0.4 collective-permute-start.3
  209.1 9.0 %all-to-all-start.2 = ((bf16[64,8,3840]{2,1,0:T(8,128)(2,1)}), bf16[64,8,3840]{2,1,0:T(8,128)(2,1)}, u32[]{:S(2)}, u32[]{:S(2)}) async-start(bf16[64,8,3840]{2,1,0:T(8,128)(2,1)} %bitcast.23), calls=%async_computation.2 | async-start | bytes 7864320 | tf_op jit(solution)/shard_map/all_to_all | solution.py:436
  218.1 0.1 stack.17
  218.2 15.0 %backward.2.own_ref = bf16[384,5120]{1,0:T(8,128)(2,1)} custom-call(bf16[384,5120]{1,0:T(8,128)(2,1)} %get-tuple-element.24.cot_ref, bf16[1,768,5120]{2,1,0:T(8,128)(2,1)} %down_ref.7, bf16[1,5120,768]{2,1,0:T(8,128)(2,1)} %up_ref.7, f32[384,768]{1,0:T(8,128)} %get-tuple-element.25.slope_ref), custom_call_target="tpu_custom_call" | custom-call | flops 6039797760 | bytes 23592960 | tf_op jit(solution)/shard_map/backward/pallas_call | solution.py:421
  233.2 10.3 %grad.1 = (bf16[512,3840]{1,0:T(8,128)(2,1)}, f32[8,5120]{1,0:T(8,128)}) custom-call(bf16[384,5120]{1,0:T(8,128)(2,1)} %backward.2.own_ref, bf16[384,5120]{1,0:T(8,128)(2,1)} %collective-permute-done.3.other_ref, f32[384,128]{1,0:T(8,128)} %get-tuple-element.27.choice_ref, bf16[384,5120]{1,0:T(8,128)(2,1)} %get-tuple-element.28.unit_ref, ...), custom_call_target="tpu_custom_call" | custom-call | flops 188743680 | bytes 16203776 | tf_op jit(solution)/shard_map/grad/pallas_call | solution.py:333
  243.6 1.0 reduce_sum.37
  244.5 0.1 stack.18
  244.7 0.1 broadcast_in_dim.14
  244.8 0.3 all_to_all.28
  245.1 22.1 %all-to-all-done.2 = bf16[64,8,3840]{2,1,0:T(8,128)(2,1)} async-done(((bf16[64,8,3840]{2,1,0:T(8,128)(2,1)}), bf16[64,8,3840]{2,1,0:T(8,128)(2,1)}, u32[]{:S(2)}, u32[]{:S(2)}) %all-to-all-start.2) | async-done | bytes 3932192 | tf_op jit(solution)/shard_map/all_to_all | solution.py:436
  267.3 21.4 %all_to_all.37 = f32[128,1,640]{2,1,0:T(1,128)S(1)} all-to-all(f32[128,1,640]{2,1,0:T(1,128)S(1)} %all_to_all.28), channel_id=1, replica_groups=mesh['ep'=8,'pair'=8,'core'=2] {'ep','pair','core'}, dimensions={0} | all-to-all | bytes 655360 | tf_op jit(solution)/shard_map/all_to_all | solution.py:542
  288.7 5.7 %all-to-all-start.4 = ((bf16[64,8,3840]{2,1,0:T(8,128)(2,1)}), bf16[64,8,3840]{2,1,0:T(8,128)(2,1)}, u32[]{:S(2)}, u32[]{:S(2)}) async-start(bf16[64,8,3840]{2,1,0:T(8,128)(2,1)} %bitcast.24), calls=%async_computation.4 | async-start | bytes 7864320 | tf_op jit(solution)/shard_map/all_to_all | solution.py:436
  294.5 0.7 copy.18.ids_ref
  295.2 6.7 %mixed.1 = bf16[128,5120]{1,0:T(8,128)(2,1)} custom-call(s32[128,2]{1,0:T(8,128)} %copy.18.ids_ref, bf16[128,5120]{1,0:T(8,128)(2,1)} %tokens_ref.3, bf16[512,3840]{1,0:T(8,128)(2,1)} %bitcast.7.band0.band1.band2, bf16[512,3840]{1,0:T(8,128)(2,1)} %bitcast.7.band0.band1.band2, bf16[512,3840]{1,0:T(8,128)(2,1)} %bitcast.7.band0.band1.band2), custom_call_target="tpu_custom_call" | custom-call | flops 1006632960 | bytes 3932160 | tf_op jit(solution)/shard_map/mixed/pallas_call | solution.py:209
  301.9 0.1 slice_reduce_fusion
  302.1 0.1 reshape.87
  302.2 0.2 reduce_sum.38
  302.4 0.6 broadcast_multiply_fusion
  303.0 0.6 multiply_bitcast_fusion
  303.6 40.2 %all-to-all-done.4 = bf16[64,8,3840]{2,1,0:T(8,128)(2,1)} async-done(((bf16[64,8,3840]{2,1,0:T(8,128)(2,1)}), bf16[64,8,3840]{2,1,0:T(8,128)(2,1)}, u32[]{:S(2)}, u32[]{:S(2)}) %all-to-all-start.4) | async-done | bytes 3932192 | tf_op jit(solution)/shard_map/all_to_all | solution.py:436
  343.8 8.0 %grad_tokens.1 = bf16[128,5120]{1,0:T(8,128)(2,1)} custom-call(s32[128,2]{1,0:T(8,128)} %copy.18.ids_ref, bf16[128,5120]{1,0:T(8,128)(2,1)} %tokens_ref.3, bf16[128,5120]{1,0:T(8,128)(2,1)} %cot_ref.1, bf16[512,3840]{1,0:T(8,128)(2,1)} %bitcast.11.band0.band1.band2, bf16[512,3840]{1,0:T(8,128)(2,1)} %bitcast.11.band0.band1.band2, ...), custom_call_target="tpu_custom_call" | custom-call | flops 1006632960 | bytes 3932160 | tf_op jit(solution)/shard_map/grad_tokens/pallas_call | solution.py:209
  (18 shorter events, 0.2 us)
Async XLA Ops:
  0.6 0.8 copy-start
  2.8 13.2 %all-to-all-start.1 = ((bf16[16,2,320]{2,1,0:T(2,128)(2,1)}), bf16[16,2,320]{2,1,0:T(2,128)(2,1)S(1)}, u32[]{:S(2)}, u32[]{:S(2)}) async-start(bf16[16,2,320]{2,1,0:T(2,128)(2,1)} %bitcast.5), calls=%async_computation.1 | async-start | bytes 49152 | tf_op jit(solution)/shard_map/all_to_all | solution.py:455
  15.9 59.0 %all-to-all-start = ((bf16[64,8,3840]{2,1,0:T(8,128)(2,1)}), bf16[64,8,3840]{2,1,0:T(8,128)(2,1)}, u32[]{:S(2)}, u32[]{:S(2)}) async-start(bf16[64,8,3840]{2,1,0:T(8,128)(2,1)} %bitcast.21), calls=%async_computation | async-start | bytes 7864320 | tf_op jit(solution)/shard_map/all_to_all | solution.py:436
  84.4 8.9 %collective-permute-start = (bf16[384,5120]{1,0:T(8,128)(2,1)}, bf16[384,5120]{1,0:T(8,128)(2,1)S(1)}, u32[]{:S(2)}, u32[]{:S(2)}) collective-permute-start(bf16[384,5120]{1,0:T(8,128)(2,1)} %get-tuple-element.18.x_ref.normed_ref), channel_id=1, source_target_pairs={{0,1},{1,0},{2,3},{3,2},{4,5},{5,4},{6,7},{7,6},{8,9},{9,8},{10,11... | collective-permute-start | bytes 11796488 | tf_op jit(solution)/shard_map/ppermute | solution.py:441
  93.2 1.9 copy-start.5
  110.1 28.6 %collective-permute-start.1 = (bf16[384,5120]{1,0:T(8,128)(2,1)}, bf16[384,5120]{1,0:T(8,128)(2,1)}, u32[]{:S(2)}, u32[]{:S(2)}) collective-permute-start(bf16[384,5120]{1,0:T(8,128)(2,1)} %get-tuple-element.20), channel_id=1, source_target_pairs={{0,1},{1,0},{2,3},{3,2},{4,5},{5,4},{6,7},{7,6},{8,9},{9,8},{10,11... | collective-permute-start | bytes 11796488 | tf_op jit(solution)/shard_map/ppermute | solution.py:441
  115.5 57.5 %all-to-all-start.3 = ((bf16[64,8,3840]{2,1,0:T(8,128)(2,1)}), bf16[64,8,3840]{2,1,0:T(8,128)(2,1)}, u32[]{:S(2)}, u32[]{:S(2)}) async-start(bf16[64,8,3840]{2,1,0:T(8,128)(2,1)} %bitcast.22), calls=%async_computation.3 | async-start | bytes 7864320 | tf_op jit(solution)/shard_map/all_to_all | solution.py:436
  182.8 9.0 %collective-permute-start.2 = (bf16[384,5120]{1,0:T(8,128)(2,1)}, bf16[384,5120]{1,0:T(8,128)(2,1)S(1)}, u32[]{:S(2)}, u32[]{:S(2)}) collective-permute-start(bf16[384,5120]{1,0:T(8,128)(2,1)} %get-tuple-element.24.cot_ref), channel_id=1, source_target_pairs={{0,1},{1,0},{2,3},{3,2},{4,5},{5,4},{6,7},{7,6},{8,9},{9,8},{10,11... | collective-permute-start | bytes 11796488 | tf_op jit(solution)/shard_map/ppermute | solution.py:441
  191.8 1.9 copy-start.2
  208.7 24.5 %collective-permute-start.3 = (bf16[384,5120]{1,0:T(8,128)(2,1)}, bf16[384,5120]{1,0:T(8,128)(2,1)}, u32[]{:S(2)}, u32[]{:S(2)}) collective-permute-start(bf16[384,5120]{1,0:T(8,128)(2,1)} %backward.3), channel_id=1, source_target_pairs={{0,1},{1,0},{2,3},{3,2},{4,5},{5,4},{6,7},{7,6},{8,9},{9,8},{10,11... | collective-permute-start | bytes 11796488 | tf_op jit(solution)/shard_map/ppermute | solution.py:441
  209.1 9.0 %copy-start.3 = (f32[8,5120]{1,0:T(8,128)S(1)}, f32[8,5120]{1,0:T(8,128)}, u32[]{:S(2)}) copy-start(f32[8,5120]{1,0:T(8,128)} %get-tuple-element.30) | copy-start | bytes 491524
  209.1 58.2 %all-to-all-start.2 = ((bf16[64,8,3840]{2,1,0:T(8,128)(2,1)}), bf16[64,8,3840]{2,1,0:T(8,128)(2,1)}, u32[]{:S(2)}, u32[]{:S(2)}) async-start(bf16[64,8,3840]{2,1,0:T(8,128)(2,1)} %bitcast.23), calls=%async_computation.2 | async-start | bytes 7864320 | tf_op jit(solution)/shard_map/all_to_all | solution.py:436
  288.7 5.8 %copy-start.4 = (s32[128,2]{0,1:T(2,128)S(1)}, s32[128,2]{0,1:T(2,128)}, u32[]{:S(2)}) copy-start(s32[128,2]{0,1:T(2,128)} %param.14) | copy-start | bytes 3076
  288.7 55.1 %all-to-all-start.4 = ((bf16[64,8,3840]{2,1,0:T(8,128)(2,1)}), bf16[64,8,3840]{2,1,0:T(8,128)(2,1)}, u32[]{:S(2)}, u32[]{:S(2)}) async-start(bf16[64,8,3840]{2,1,0:T(8,128)(2,1)} %bitcast.24), calls=%async_computation.4 | async-start | bytes 7864320 | tf_op jit(solution)/shard_map/all_to_all | solution.py:436
  343.8 8.0 %copy-start.1 = (bf16[320,64]{0,1:T(8,128)(2,1)S(1)}, bf16[320,64]{0,1:T(8,128)(2,1)}, u32[]{:S(2)}) copy-start(bf16[320,64]{0,1:T(8,128)(2,1)} %param.11) | copy-start | bytes 122884

commit v2 on v1

v2 whole, which is shorter than its diff:
```python
import functools
import math

import jax
import jax.numpy as jnp
import numpy as np
from jax import lax
from jax.experimental import pallas as pl
from jax.experimental.pallas import tpu as pltpu
from jax.sharding import Mesh
from jax.sharding import PartitionSpec as P

EPS = 1e-06
CAP = 6
PARTS = 4
TILE = 8
BANDS = CAP * PARTS // TILE
GROUP = 8
BF16 = jnp.bfloat16
F32 = jnp.float32
LOUD = 64
META = 128
SUB = 2
VMEM_LIMIT = 56 * 1024 * 1024
CHIPS = ("ep", "pair")
FSDP = ("pair", "core")
EVERY = ("ep", "pair", "core")


def params(steps):
    return pltpu.CompilerParams(
        dimension_semantics=("arbitrary",) * steps, vmem_limit_bytes=VMEM_LIMIT
    )


def cost(flops, bytes_accessed):
    return pl.CostEstimate(flops=flops, bytes_accessed=bytes_accessed, transcendentals=0)


def iota(shape, dim):
    return lax.broadcasted_iota(jnp.int32, shape, dim)


def dot(a, b):
    return jnp.dot(a, b, preferred_element_type=F32)


def dot_nt(a, b):
    return lax.dot_general(a, b, (((1,), (1,)), ((), ())), preferred_element_type=F32)


def as_bf16(mask):
    return mask.astype(F32).astype(BF16)


def shuffle_matrix():
    size = CAP * PARTS * GROUP
    matrix = np.zeros((size, size), np.float32)
    for message in range(GROUP):
        for number in range(CAP * PARTS):
            piece, slot = divmod(number, CAP)
            band, row = divmod(number, TILE)
            matrix[
                piece * GROUP * CAP + message * CAP + slot,
                band * GROUP * TILE + message * TILE + row,
            ] = 1.0
    return matrix


def slot_target(band, column):
    row = column & (TILE - 1)
    limit = CAP - 2 * band
    low = row < limit
    slot = 2 * band + row - jnp.where(low, 0, CAP)
    return (column >> 3) * CAP + slot, low


def pack_kernel(experts, ids_ref, rows_ref, *refs):
    *meta_refs, out_ref, pos_ref = refs
    step = pl.program_id(0)
    toks, features = rows_ref.shape
    count = out_ref.shape[0]
    piece = features // PARTS

    @pl.when(step == 0)
    def _():
        first, second = ids_ref[0:1, :], ids_ref[1:2, :]
        expert = iota((experts, toks), 0)
        in_first, in_second = expert == first, expert == second
        both = as_bf16(in_first | in_second)
        earlier = as_bf16(iota((toks, toks), 0) < iota((toks, toks), 1))
        earlier_count = dot(both, earlier)
        slot_first = jnp.sum(jnp.where(in_first, earlier_count, 0.0), axis=0, keepdims=True)
        slot_second = jnp.sum(jnp.where(in_second, earlier_count, 0.0), axis=0, keepdims=True)
        pos_ref[0:1, :] = first * CAP + slot_first.astype(jnp.int32)
        pos_ref[1:2, :] = second * CAP + slot_second.astype(jnp.int32)

    row = step * count + iota((count, toks), 0)
    for band in range(BANDS):
        target, low = slot_target(band, row)
        hit = (target == pos_ref[0:1, :]) | (target == pos_ref[1:2, :])
        placing = jnp.concatenate([as_bf16(hit & low), as_bf16(hit & ~low)], axis=1)
        pieces = [rows_ref[:, p * piece : (p + 1) * piece] for p in (band, band + 1)]
        out_ref[:, band * piece : (band + 1) * piece] = dot(
            placing, jnp.concatenate(pieces, axis=0)
        ).astype(BF16)

    if meta_refs:
        gain_ref, router_ref, core_ref = meta_refs
        shard = router_ref.shape[0]
        shift = core_ref[0, 0] * (META // 2)
        shifted = as_bf16(iota((shard, 3 * META), 1) == iota((shard, 3 * META), 0) + shift)
        gain = dot(gain_ref[...], shifted)
        columns = lax.dot_general(
            router_ref[...], shifted, (((0,), (0,)), ((), ())), preferred_element_type=F32
        ).astype(BF16)
        tile_row = iota((count, META), 0) & (TILE - 1)
        pick_row = step * count + iota((count, experts), 0)
        pick_column = iota((count, experts), 1)
        total = jnp.zeros((count, META), F32)
        for r in range(3):
            lanes = slice(r * META, (r + 1) * META)
            total = jnp.where(tile_row == r, gain[0:1, lanes], total)
            total = total + dot(as_bf16(pick_row == pick_column * TILE + 3 + r), columns[:, lanes])
        out_ref[:, BANDS * piece :] = total.astype(BF16)


SMALL = pl.BlockSpec(memory_space=pltpu.SMEM)


def pack(ids_t, rows, experts, meta=()):
    toks, features = rows.shape
    width = features * CAP // TILE + (META if meta else 0)
    out_rows = experts * TILE
    steps = 4
    meta_specs = []
    if meta:
        meta_specs = [pl.BlockSpec(value.shape, lambda i: (0, 0)) for value in meta[:2]] + [SMALL]
    return pl.pallas_call(
        functools.partial(pack_kernel, experts),
        grid=(steps,),
        in_specs=[
            pl.BlockSpec((2, toks), lambda i: (0, 0)),
            pl.BlockSpec((toks, features), lambda i: (0, 0)),
            *meta_specs,
        ],
        out_specs=pl.BlockSpec((out_rows // steps, width), lambda i: (i, 0)),
        out_shape=jax.ShapeDtypeStruct((out_rows, width), BF16),
        scratch_shapes=[pltpu.VMEM((8, toks), jnp.int32)],
        compiler_params=params(1),
        cost_estimate=cost(2 * out_rows * 2 * toks * width, 2 * out_rows * width),
        name="pack",
    )(ids_t, rows, *meta)


def fill_choosing(ids_ref, choose_ref):
    toks = ids_ref.shape[0]
    columns = choose_ref.shape[2]
    experts = columns // TILE
    first, second = ids_ref[:, 0:1], ids_ref[:, 1:2]
    expert = iota((toks, experts), 1)
    in_first, in_second = expert == first, expert == second
    both = as_bf16(in_first | in_second)
    earlier = as_bf16(iota((toks, toks), 1) < iota((toks, toks), 0))
    count = dot(earlier, both)
    pos_first = first * CAP + jnp.sum(
        jnp.where(in_first, count, 0.0), axis=1, keepdims=True
    ).astype(jnp.int32)
    pos_second = second * CAP + jnp.sum(
        jnp.where(in_second, count, 0.0), axis=1, keepdims=True
    ).astype(jnp.int32)
    for band in range(BANDS):
        target, low = slot_target(band, iota((toks, columns), 1))
        hit = (target == pos_first) | (target == pos_second)
        choose_ref[band, :toks, :] = as_bf16(hit & low)
        choose_ref[band, toks:, :] = as_bf16(hit & ~low)


def summed_pieces(choose_ref, band_refs):
    toks = choose_ref.shape[1] // 2
    sums = [dot(choose_ref[band], band_refs[band][...]) for band in range(BANDS)]
    pieces = [sums[0][:toks]]
    for band in range(1, BANDS):
        pieces.append(sums[band - 1][toks:] + sums[band][:toks])
    pieces.append(sums[BANDS - 1][toks:])
    return pieces


def mixed_kernel(ids_ref, tokens_ref, band0, band1, band2, out_ref, choose_ref):
    step = pl.program_id(0)
    width = band0.shape[1]
    piece = tokens_ref.shape[1] // PARTS

    @pl.when(step == 0)
    def _():
        fill_choosing(ids_ref, choose_ref)

    for number, value in enumerate(summed_pieces(choose_ref, (band0, band1, band2))):
        cols = pl.ds(pl.multiple_of(number * piece + step * width, width), width)
        out_ref[:, cols] = (tokens_ref[:, cols].astype(F32) + value).astype(BF16)


def grad_tokens_kernel(
    ids_ref, tokens_ref, cot_ref, band0, band1, band2, out_ref, choose_ref, grad_ref, square_ref, cross_ref
):
    step = pl.program_id(0)
    width = band0.shape[1]
    features = tokens_ref.shape[1]
    piece = features // PARTS

    @pl.when(step == 0)
    def _():
        fill_choosing(ids_ref, choose_ref)
        square_ref[...] = jnp.zeros_like(square_ref)
        cross_ref[...] = jnp.zeros_like(cross_ref)

    for number, value in enumerate(summed_pieces(choose_ref, (band0, band1, band2))):
        cols = pl.ds(pl.multiple_of(number * piece + step * width, width), width)
        x = tokens_ref[:, cols].astype(F32)
        grad_ref[:, cols] = value
        square_ref[...] += x * x
        cross_ref[...] += x * value

    @pl.when(step == pl.num_programs(0) - 1)
    def _():
        scale = lax.rsqrt(jnp.sum(square_ref[...], axis=1, keepdims=True) / features + EPS)
        back = jnp.sum(cross_ref[...], axis=1, keepdims=True) / features * scale * scale * scale
        for at in range(0, features, width):
            cols = slice(at, at + width)
            x = tokens_ref[:, cols].astype(F32)
            grad = scale * grad_ref[:, cols] - x * back
            out_ref[:, cols] = (cot_ref[:, cols].astype(F32) + grad).astype(BF16)


def token_side(kernel, ids, row_inputs, bands, scratch, name):
    toks, features = row_inputs[0].shape
    piece = features // PARTS
    width = 256
    steps = piece // width
    columns = bands.shape[0]

    def band_spec(band):
        return pl.BlockSpec((columns, width), lambda c, band=band: (0, band * steps + c))

    return pl.pallas_call(
        kernel,
        grid=(steps,),
        in_specs=[pl.BlockSpec((toks, 2), lambda c: (0, 0))]
        + [pl.BlockSpec((toks, features), lambda c: (0, 0))] * len(row_inputs)
        + [band_spec(band) for band in range(BANDS)],
        out_specs=pl.BlockSpec((toks, features), lambda c: (0, 0)),
        out_shape=jax.ShapeDtypeStruct((toks, features), BF16),
        scratch_shapes=[pltpu.VMEM((BANDS, 2 * toks, columns), BF16)] + scratch,
        compiler_params=params(1),
        cost_estimate=cost(2 * BANDS * 2 * toks * columns * piece, 2 * columns * BANDS * piece),
        name=name,
    )(ids, *row_inputs, *([bands] * BANDS))


def sums_kernel(scale, meta_ref, core_ref, router_ref, own_ref, other_ref):
    messages = meta_ref[...]
    tiles = messages.shape[0]
    experts, shard = router_ref.shape
    lower = core_ref[0, 0] == 0
    rows = [
        dot(as_bf16(iota((experts, tiles), 1) == iota((experts, tiles), 0) * TILE + 5 + r), messages)
        for r in range(3)
    ]
    router = jnp.concatenate(rows, axis=1) * scale
    router_ref[...] = jnp.where(lower, router[:, :shard], router[:, META // 2 : META // 2 + shard])
    total = dot(as_bf16((iota((TILE, tiles), 1) & (TILE - 1)) == iota((TILE, tiles), 0)), messages)
    total = jnp.concatenate([total[r : r + 1] for r in range(5)], axis=1) * scale
    first, second = total[:, :shard], total[:, shard : 2 * shard]
    own_ref[...] = jnp.where(lower, first, second)
    other_ref[...] = jnp.where(lower, second, first)


def summed(messages, core, shard, scale):
    tiles, width = messages.shape
    row = jax.ShapeDtypeStruct((1, shard), F32)
    return pl.pallas_call(
        functools.partial(sums_kernel, scale),
        grid=(1,),
        in_specs=[pl.BlockSpec((tiles, META), lambda i: (0, width // META - 1)), SMALL],
        out_specs=[
            pl.BlockSpec((tiles // TILE, shard), lambda i: (0, 0)),
            pl.BlockSpec((1, shard), lambda i: (0, 0)),
            pl.BlockSpec((1, shard), lambda i: (0, 0)),
        ],
        out_shape=[jax.ShapeDtypeStruct((tiles // TILE, shard), F32), row, row],
        compiler_params=params(1),
        cost_estimate=cost(10**6, 2 * tiles * META),
        name="sums",
    )(messages, core)


def unpacked(block, shuffle, width):
    piece = width // BANDS
    stacked = jnp.concatenate([block[:, b * piece : (b + 1) * piece] for b in range(BANDS)], axis=0)
    rows = dot(shuffle, stacked)
    count = GROUP * CAP
    return [rows[q * count : (q + 1) * count] for q in range(PARTS)]


def spread(column, ref, rows):
    ref[rows] = jnp.broadcast_to(column, (GROUP * CAP, ref.shape[1]))


def row_fold(value):
    total = value[0:8]
    for at in range(8, value.shape[0], 8):
        total = total + value[at : at + 8]
    return total


def group_slices():
    for sub in range(SUB):
        yield (
            slice(sub * GROUP * TILE, (sub + 1) * GROUP * TILE),
            slice(sub * GROUP * CAP, (sub + 1) * GROUP * CAP),
        )


def norm_kernel(
    own_ref, other_ref, own_meta, other_meta, core_ref, shuffle_ref,
    own_normed, other_normed, own_gate, other_gate, gain_ref, column_ref,
):
    features = own_normed.shape[1]
    width = own_ref.shape[1] - META
    piece = features // PARTS

    @pl.when(pl.program_id(0) == 0)
    def _():
        own, other = own_meta[...].astype(F32), other_meta[...].astype(F32)
        lower = core_ref[0, 0] == 0
        first, second = jnp.where(lower, own, other), jnp.where(lower, other, own)
        for part, ref in ((0, gain_ref), (3, column_ref)):
            for pair in range(features // (5 * META)):
                at = pair * TILE + part
                rows = [first[at + r : at + r + 1] for r in range(3)]
                rows += [second[at + r : at + r + 1] for r in range(3)]
                rows = [rows[0], rows[1], rows[2] + rows[3], rows[4], rows[5]]
                ref[:, pair * 5 * META : (pair + 1) * 5 * META] = jnp.concatenate(rows, axis=1)

    for block_ref, normed_ref, gate_ref in (
        (own_ref, own_normed, own_gate),
        (other_ref, other_normed, other_gate),
    ):
        for tiles, rows in group_slices():
            pieces = unpacked(block_ref[tiles, :width], shuffle_ref[...], width)
            square = sum(jnp.sum(x * x, axis=1, keepdims=True) for x in pieces)
            scale = lax.rsqrt(square / features + EPS)
            logit = 0.0
            for q, x in enumerate(pieces):
                cols = slice(q * piece, (q + 1) * piece)
                normed = (x * scale * gain_ref[:, cols]).astype(BF16)
                normed_ref[rows, cols] = normed
                logit = logit + jnp.sum(
                    normed.astype(F32) * column_ref[:, cols], axis=1, keepdims=True
                )
            spread(jax.nn.sigmoid(logit), gate_ref, rows)


def out_kernel(own_ref, other_ref, gate_ref, back_ref, result_ref, send_ref):
    piece = own_ref.shape[1] // PARTS
    for tiles, rows in group_slices():
        gate = gate_ref[rows, 0:1]
        gated = []
        for q in range(PARTS):
            cols = slice(q * piece, (q + 1) * piece)
            result = (own_ref[rows, cols].astype(F32) + other_ref[rows, cols].astype(F32)).astype(BF16)
            result_ref[rows, cols] = result
            gated.append((gate * result.astype(F32)).astype(BF16))
        bands = dot(back_ref[...], jnp.concatenate(gated, axis=0)).astype(BF16)
        for b in range(BANDS):
            send_ref[tiles, b * piece : (b + 1) * piece] = bands[
                b * GROUP * TILE : (b + 1) * GROUP * TILE
            ]


def cot_kernel(
    own_ref, other_ref, own_gate, other_gate, result_ref, normed_ref, shuffle_ref,
    own_gated, other_gated, choice_ref, router_ref,
):
    width = own_ref.shape[1]
    piece = width // BANDS

    @pl.when(pl.program_id(0) == 0)
    def _():
        router_ref[...] = jnp.zeros_like(router_ref)

    for tiles, rows in group_slices():
        pieces = unpacked(other_ref[tiles], shuffle_ref[...], width)
        gate = other_gate[rows, 0:1]
        for q, cot in enumerate(pieces):
            other_gated[rows, q * piece : (q + 1) * piece] = (gate * cot).astype(BF16)
        pieces = unpacked(own_ref[tiles], shuffle_ref[...], width)
        gate = own_gate[rows, 0:1]
        total = 0.0
        for q, cot in enumerate(pieces):
            cols = slice(q * piece, (q + 1) * piece)
            own_gated[rows, cols] = (gate * cot).astype(BF16)
            total = total + jnp.sum(cot * result_ref[rows, cols].astype(F32), axis=1, keepdims=True)
        choice = total * gate * (1.0 - gate)
        spread(choice, choice_ref, rows)
        for q in range(PARTS):
            cols = slice(q * piece, (q + 1) * piece)
            router_ref[:, cols] += row_fold(normed_ref[rows, cols].astype(F32) * choice)


def grad_kernel(
    own_ref, other_ref, choice_ref, normed_ref, column_ref, gain_ref, own_router, other_router, core_ref,
    back_ref, send_ref, sums_ref, meta_ref,
):
    step = pl.program_id(0)
    features = own_ref.shape[1]
    piece = features // PARTS

    @pl.when(step == 0)
    def _():
        sums_ref[...] = jnp.zeros_like(sums_ref)

    for sub, (_, rows) in enumerate(group_slices()):
        choice = choice_ref[rows, 0:1]
        scaled = []
        for q in range(PARTS):
            cols = slice(q * piece, (q + 1) * piece)
            back = (own_ref[rows, cols].astype(F32) + other_ref[rows, cols].astype(F32)).astype(BF16)
            grad = back.astype(F32) + choice * column_ref[:, cols]
            sums_ref[:, cols] += row_fold(grad * normed_ref[rows, cols].astype(F32))
            scaled.append((grad * gain_ref[:, cols]).astype(BF16))
        bands = dot(back_ref[...], jnp.concatenate(scaled, axis=0)).astype(BF16)
        count = GROUP * TILE
        tiles = pl.ds(pl.multiple_of((step * SUB + sub) * count, count), count)
        for b in range(BANDS):
            send_ref[tiles, b * piece : (b + 1) * piece] = bands[b * count : (b + 1) * count]

    @pl.when(step == pl.num_programs(0) - 1)
    def _():
        gain_sum = jnp.sum(sums_ref[...], axis=0, keepdims=True) / gain_ref[...]
        router_sum = jnp.sum(own_router[...] + other_router[...], axis=0, keepdims=True)
        lower = core_ref[0, 0] == 0

        def lanes(value, number):
            return value[:, number * META : (number + 1) * META]

        pairs = features // (5 * META)
        for pair in range(pairs):
            for r in range(5):
                meta_ref[pair * TILE + r : pair * TILE + r + 1, :] = lanes(gain_sum, pair * 5 + r)
            for r in range(3):
                at = pair * 5 + r
                meta_ref[pair * TILE + 5 + r : pair * TILE + 6 + r, :] = jnp.where(
                    lower, lanes(router_sum, at), lanes(router_sum, at + 2)
                )
        meta = meta_ref[...].astype(BF16)
        for at in range(0, send_ref.shape[0], pairs * TILE):
            send_ref[at : at + pairs * TILE, BANDS * piece :] = meta


def by_group(kernel, inputs, outputs, flops, name, scratch=()):
    steps = None
    for value, rows in inputs:
        if isinstance(rows, int) and rows:
            steps = value.shape[0] // (rows * SUB)

    def spec(shape, rows):
        if not isinstance(rows, int):
            return rows
        if rows:
            return pl.BlockSpec((rows * SUB, shape[1]), lambda g: (g, 0))
        return pl.BlockSpec(shape, lambda g: (0, 0))

    moved = sum(value.size * value.dtype.itemsize for value, _ in inputs)
    moved += sum(math.prod(shape) * dtype.itemsize for shape, dtype, _ in outputs)
    return pl.pallas_call(
        kernel,
        grid=(steps,),
        in_specs=[spec(value.shape, rows) for value, rows in inputs],
        out_specs=[spec(shape, rows) for shape, _, rows in outputs],
        out_shape=[jax.ShapeDtypeStruct(shape, dtype) for shape, dtype, _ in outputs],
        scratch_shapes=list(scratch),
        compiler_params=params(1),
        cost_estimate=cost(flops, moved),
        name=name,
    )(*[value for value, _ in inputs])


def forward_kernel(own_ref, other_ref, up_ref, down_ref, out_ref, own_hidden, slope_ref, acc_ref, hidden_ref):
    step = pl.program_id(0)
    half = pl.num_programs(0) // 2
    count = own_ref.shape[0]
    sides = ((slice(0, count), own_ref), (slice(count, 2 * count), other_ref))

    @pl.when(step == 0)
    def _():
        for rows, x_ref in sides:
            acc_ref[rows] = dot(x_ref[...], up_ref[...])

    @pl.when((step > 0) & (step < half))
    def _():
        for rows, x_ref in sides:
            acc_ref[rows] += dot(x_ref[...], up_ref[...])

    @pl.when(step == half - 1)
    def _():
        root = math.sqrt(2.0 / math.pi)
        for (rows, _), kept in zip(sides, (own_hidden, hidden_ref)):
            pre = acc_ref[rows]
            square = pre * pre
            bend = jnp.tanh(root * (pre + 0.044715 * (square * pre)))
            share = 0.5 * (1.0 + bend)
            kept[...] = (pre * share).astype(BF16)
            inner = root * (1.0 + (3.0 * 0.044715) * square)
            slope_ref[rows] = share + 0.5 * pre * (1.0 - bend * bend) * inner

    @pl.when(step >= half)
    def _():
        out_ref[...] = dot(hidden_ref[...], down_ref[...]).astype(BF16)


def backward_kernel(own_ref, other_ref, down_ref, up_ref, slope_ref, out_ref, own_grad, acc_ref, grad_ref):
    step = pl.program_id(0)
    half = pl.num_programs(0) // 2
    count = own_ref.shape[0]
    sides = ((slice(0, count), own_ref), (slice(count, 2 * count), other_ref))

    @pl.when(step == 0)
    def _():
        for rows, cot_ref in sides:
            acc_ref[rows] = dot_nt(cot_ref[...], down_ref[...])

    @pl.when((step > 0) & (step < half))
    def _():
        for rows, cot_ref in sides:
            acc_ref[rows] += dot_nt(cot_ref[...], down_ref[...])

    @pl.when(step == half - 1)
    def _():
        for (rows, _), kept in zip(sides, (own_grad, grad_ref)):
            kept[...] = (acc_ref[rows] * slope_ref[rows]).astype(BF16)

    @pl.when(step >= half)
    def _():
        out_ref[...] = dot_nt(grad_ref[...], up_ref[...]).astype(BF16)


def expert_call(kernel, own, other, up, down, slope, name):
    count, features = own.shape
    hidden = up.shape[2]
    block = features // PARTS
    half = features // block

    def first(i):
        return jnp.minimum(i, half - 1)

    def second(i):
        return jnp.maximum(i - half, 0)

    rows_spec = pl.BlockSpec((count, block), lambda i: (0, first(i)))
    slope_spec = pl.BlockSpec((2 * count, hidden), lambda i: (0, 0))
    out_specs = [
        pl.BlockSpec((count, block), lambda i: (0, second(i))),
        pl.BlockSpec((count, hidden), lambda i: (0, 0)),
    ]
    out_shapes = [
        jax.ShapeDtypeStruct((count, features), BF16),
        jax.ShapeDtypeStruct((count, hidden), BF16),
    ]
    forward = slope is None
    early, late = (first, second) if forward else (second, first)
    up_spec = pl.BlockSpec((None, block, hidden), lambda i: (0, early(i), 0))
    down_spec = pl.BlockSpec((None, hidden, block), lambda i: (0, 0, late(i)))
    if forward:
        args, in_specs = (own, other, up, down), [rows_spec, rows_spec, up_spec, down_spec]
        out_specs.append(slope_spec)
        out_shapes.append(jax.ShapeDtypeStruct((2 * count, hidden), F32))
    else:
        args = (own, other, down, up, slope)
        in_specs = [rows_spec, rows_spec, down_spec, up_spec, slope_spec]
    return pl.pallas_call(
        kernel,
        grid=(2 * half,),
        in_specs=in_specs,
        out_specs=out_specs,
        out_shape=out_shapes,
        scratch_shapes=[pltpu.VMEM((2 * count, hidden), F32), pltpu.VMEM((count, hidden), BF16)],
        compiler_params=params(1),
        cost_estimate=cost(6 * count * features * hidden, 4 * features * (2 * count + hidden)),
        name=name,
    )(*args)


def last_kernel(x_ref, weight_ref, out_ref, *, product):
    out_ref[...] = product(x_ref[...], weight_ref[...]).astype(BF16)


def last_call(product, x, weight, name):
    count, hidden = x.shape
    features = weight.shape[2] if product is dot else weight.shape[1]
    block = features // PARTS
    if product is dot:
        weight_spec = pl.BlockSpec((None, hidden, block), lambda i: (0, 0, i))
    else:
        weight_spec = pl.BlockSpec((None, block, hidden), lambda i: (0, i, 0))
    return pl.pallas_call(
        functools.partial(last_kernel, product=product),
        grid=(PARTS,),
        in_specs=[pl.BlockSpec((count, hidden), lambda i: (0, 0)), weight_spec],
        out_specs=pl.BlockSpec((count, block), lambda i: (0, i)),
        out_shape=jax.ShapeDtypeStruct((count, features), BF16),
        compiler_params=params(1),
        cost_estimate=cost(2 * count * features * hidden * LOUD, 2 * features * (count + hidden) * LOUD),
        name=name,
    )(x, weight)


def exchange(messages):
    blocks = messages.reshape(-1, TILE, messages.shape[1])
    blocks = lax.all_to_all(blocks, CHIPS, split_axis=0, concat_axis=0, tiled=True)
    return blocks.reshape(messages.shape)


def swap(value):
    return lax.ppermute(value, "core", [(0, 1), (1, 0)])


def body(tokens, norm_gain, router_weight, up_weight, down_weight, expert_ids, cotangent):
    toks, features = tokens.shape
    eps, pairs, cores = (lax.axis_size(name) for name in EVERY)
    experts = eps * pairs
    shard = features // (pairs * cores)
    rows = experts * CAP
    devices = experts * cores

    core = jnp.full((1, 1), lax.axis_index("core"), jnp.int32)
    matrix = shuffle_matrix()
    shuffle, shuffle_back = jnp.asarray(matrix, BF16), jnp.asarray(matrix.T, BF16)
    ids_t = expert_ids.T
    group_rows, group_tiles = GROUP * CAP, GROUP * TILE
    row_shape, tiles, width = (rows, features), experts * TILE, features * CAP // TILE
    wide, line, fold = (rows, 128), (1, features), (8, features)
    shuffling = 2 * rows * features * CAP * PARTS * GROUP // PARTS
    b16, f32 = jnp.dtype(BF16), jnp.dtype(F32)
    meta_spec = pl.BlockSpec((pairs * TILE, META), lambda g: (0, width // META))

    cot_sent = pack(ids_t, cotangent, experts)
    arrived = exchange(pack(ids_t, tokens, experts, (norm_gain.reshape(1, shard), router_weight, core)))
    arrived, cot_sent = lax.optimization_barrier((arrived, cot_sent))
    arrived_other = swap(arrived)
    cot_arrived = exchange(cot_sent)
    normed, normed_other, gate, gate_other, gain, column = by_group(
        norm_kernel,
        [
            (arrived, group_tiles),
            (arrived_other, group_tiles),
            (arrived, meta_spec),
            (arrived_other, meta_spec),
            (core, SMALL),
            (shuffle, 0),
        ],
        [
            (row_shape, b16, group_rows),
            (row_shape, b16, group_rows),
            (wide, f32, group_rows),
            (wide, f32, group_rows),
            (line, f32, 0),
            (line, f32, 0),
        ],
        2 * shuffling,
        "norm",
    )
    other_part, hidden, slope = expert_call(
        forward_kernel, normed, normed_other, up_weight, down_weight, None, "forward"
    )
    other_part = swap(other_part)
    own_part = last_call(dot, hidden, down_weight, "forward_own")
    result, result_sent = by_group(
        out_kernel,
        [(own_part, group_rows), (other_part, group_rows), (gate, group_rows), (shuffle_back, 0)],
        [(row_shape, b16, group_rows), ((tiles, width), b16, group_tiles)],
        shuffling,
        "out",
    )
    cot_arrived, result_sent = lax.optimization_barrier((cot_arrived, result_sent))
    cot_other = swap(cot_arrived)
    result_back = exchange(result_sent)
    gated, gated_other, choice, router_sum = by_group(
        cot_kernel,
        [
            (cot_arrived, group_tiles),
            (cot_other, group_tiles),
            (gate, group_rows),
            (gate_other, group_rows),
            (result, group_rows),
            (normed, group_rows),
            (shuffle, 0),
        ],
        [
            (row_shape, b16, group_rows),
            (row_shape, b16, group_rows),
            (wide, f32, group_rows),
            (fold, f32, 0),
        ],
        2 * shuffling,
        "cot",
    )
    router_other = swap(router_sum)
    other_grad, grad_hidden = expert_call(
        backward_kernel, gated, gated_other, up_weight, down_weight, slope, "backward"
    )
    other_grad = swap(other_grad)
    own_grad = last_call(dot_nt, grad_hidden, up_weight, "backward_own")
    (grad_sent,) = by_group(
        grad_kernel,
        [
            (own_grad, group_rows),
            (other_grad, group_rows),
            (choice, group_rows),
            (normed, group_rows),
            (column, 0),
            (gain, 0),
            (router_sum, 0),
            (router_other, 0),
            (core, SMALL),
            (shuffle_back, 0),
        ],
        [((tiles, width + META), b16, 0)],
        shuffling,
        "grad",
        [pltpu.VMEM(fold, F32), pltpu.VMEM((pairs * TILE, META), F32)],
    )
    grad_back = exchange(grad_sent)
    mixed = token_side(mixed_kernel, expert_ids, [tokens], result_back, [], "mixed")
    grad_tokens = token_side(
        grad_tokens_kernel,
        expert_ids,
        [tokens, cotangent],
        grad_back,
        [
            pltpu.VMEM((toks, features), F32),
            pltpu.VMEM((toks, 256), F32),
            pltpu.VMEM((toks, 256), F32),
        ],
        "grad_tokens",
    )

    grad_router, own_gain, other_gain = summed(grad_back, core, shard, 1.0 / math.sqrt(toks * devices))
    grad_gain = (own_gain + swap(other_gain)).reshape(shard)
    grad_router = grad_router.T
    return mixed, grad_tokens, grad_router, grad_gain


def solution(mesh):
    eps, fsdp = mesh.devices.shape
    fine = Mesh(mesh.devices.reshape(eps, fsdp // 2, 2), EVERY)
    in_specs = (
        P(EVERY, None),
        P(FSDP),
        P(FSDP, None),
        P(EVERY, None, None),
        P(EVERY, None, None),
        P(EVERY, None),
        P(EVERY, None),
    )
    out_specs = (P(EVERY, None), P(EVERY, None), P(FSDP, None), P(FSDP))
    return jax.shard_map(body, mesh=fine, in_specs=in_specs, out_specs=out_specs, check_vma=False)
```

time: 355 us -> 268 us (0.75)
  waiting for transfers between devices: 148 us -> 95.5 us
  blocking collectives: 21.4 us -> 0 us
  Pallas kernels: 124 us -> 117 us
  local copies, waits for them, and re-layouts: 8.86 us -> 3.53 us
    all_to_all x4, waiting for transfers between devices: 134 us -> 95.5 us  [exchange(): lax.all_to_all(blocks, CHIPS, split_axis=0, concat_axis=0, tiled=True)]
    pallas_call x4 -> x2, Pallas kernels: 59.8 us -> 37.2 us  [expert_call(): pl.pallas_call(kernel, grid=(2 * half,), in_specs=in_specs, out_specs=out...]
    all_to_all x1 -> x0, blocking collectives: 21.4 us -> none  [body(): sums = lax.all_to_all(sums, EVERY, split_axis=0, concat_axis=0, tiled=True)]
    pallas_call x6 -> x9, Pallas kernels: 49.4 us -> 65.3 us  [the longest x4 37.8 us: by_group(): pl.pallas_call(kernel, grid=(steps,), in_specs=[spec(value.shape, rows) f...]
    ppermute x4 -> x6, waiting for transfers between devices: 13.2 us -> 0.02 us  [swap(): return lax.ppermute(value, 'core', [(0, 1), (1, 0)])]
    all_to_all x1 -> x0, starting transfers between devices: 7.34 us -> none  [body(): lax.all_to_all(parcel, FSDP, split_axis=0, concat_axis=0, tiled=True)]
    all_to_all x4, starting transfers between devices: 33.1 us -> 39.8 us  [exchange(): lax.all_to_all(blocks, CHIPS, split_axis=0, concat_axis=0, tiled=True)]
    ppermute x4 -> x6, starting transfers between devices: 5.39 us -> 8.11 us  [swap(): return lax.ppermute(value, 'core', [(0, 1), (1, 0)])]
  transfers between devices with their start and end apart: 9 -> 10, of which waited for: 7 -> 4; matrix products, arithmetic and copies ran while one was open for 2% -> 0% of each run, Pallas kernels for 19% -> 41%
where the time goes in v2:
time: 268 us; the launch traced here: 265 us
  Pallas kernels  117 us (44%)
  waiting for transfers between devices  95.5 us (36%)
  starting transfers between devices  47.9 us (18%)
  local copies, waits for them, and re-layouts  3.53 us (1%)
    all_to_all x4, waiting for transfers between devices, exchange(): lax.all_to_all(blocks, CHIPS, split_axis=0, concat_axis=0, tiled=True)  95.5 us
    all_to_all x4, starting transfers between devices, exchange(): lax.all_to_all(blocks, CHIPS, split_axis=0, concat_axis=0, tiled=True)  39.8 us
    pallas_call x4, Pallas kernels, by_group(): pl.pallas_call(kernel, grid=(steps,), in_specs=[spec(value.shape, rows) f...  37.8 us
    pallas_call x2, Pallas kernels, expert_call(): pl.pallas_call(kernel, grid=(2 * half,), in_specs=in_specs, out_specs=out...  37.2 us
    pallas_call x2, Pallas kernels, last_call(): pl.pallas_call(functools.partial(last_kernel, product=product), grid=(PAR...  15.2 us
    pallas_call x2, Pallas kernels, token_side(): pl.pallas_call(kernel, grid=(steps,), in_specs=[pl.BlockSpec((toks, 2), l...  14.5 us
    pallas_call x2, Pallas kernels, pack(): pl.pallas_call(functools.partial(pack_kernel, experts), grid=(steps,), in...  10.4 us
    ppermute x6, starting transfers between devices, swap(): return lax.ppermute(value, 'core', [(0, 1), (1, 0)])  8.11 us
  transfers between devices with their start and end apart: 10, of which 4 were waited for; matrix products, arithmetic and copies ran while one was open for 0% of the time, Pallas kernels for 41%

profile of v2, /device:TPU:1, one launch (start us, length us, event | category | flops | bytes accessed | tf_op | source)
XLA Modules:
  0.0 265.2 jit_solution(12867518043871887156)
XLA Ops:
  0.6 1.2 reshape.38.refs_0_
  1.9 1.5 copy.13.refs_1_
  3.4 5.6 %pack.2 = bf16[512,3968]{1,0:T(8,128)(2,1)} custom-call(s32[2,128]{1,0:T(2,128)} %bitcast.15, bf16[128,5120]{1,0:T(8,128)(2,1)} %tokens_ref.3, bf16[1,320]{1,0:T(2,128)(2,1)} %reshape.38.refs_0_, bf16[320,64]{1,0:T(8,128)(2,1)} %copy.13.refs_1_, s32[1,1]{1,0:T(1,128)} %bitcast.1.refs_2_.core_ref), custom_call_target="tpu_custom_call" | custom-call | flops 1040187392 | bytes 4063232 | tf_op jit(solution)/shard_map/pack/pallas_call | solution.py:139
  9.0 12.2 %all-to-all-start = ((bf16[64,8,3968]{2,1,0:T(8,128)(2,1)}), bf16[64,8,3968]{2,1,0:T(8,128)(2,1)}, u32[]{:S(2)}, u32[]{:S(2)}) async-start(bf16[64,8,3968]{2,1,0:T(8,128)(2,1)} %bitcast.12), calls=%async_computation | async-start | bytes 8126464 | tf_op jit(solution)/shard_map/all_to_all | solution.py:620
  21.2 4.8 %pack.3 = bf16[512,3840]{1,0:T(8,128)(2,1)} custom-call(s32[2,128]{1,0:T(2,128)} %bitcast.16, bf16[128,5120]{1,0:T(8,128)(2,1)} %cot_ref.1), custom_call_target="tpu_custom_call" | custom-call | flops 1006632960 | bytes 3932160 | tf_op jit(solution)/shard_map/pack/pallas_call | solution.py:139
  26.0 45.5 %all-to-all-done = bf16[64,8,3968]{2,1,0:T(8,128)(2,1)} async-done(((bf16[64,8,3968]{2,1,0:T(8,128)(2,1)}), bf16[64,8,3968]{2,1,0:T(8,128)(2,1)}, u32[]{:S(2)}, u32[]{:S(2)}) %all-to-all-start) | async-done | bytes 4063264 | tf_op jit(solution)/shard_map/all_to_all | solution.py:620
  71.5 2.5 collective-permute-start
  74.0 8.8 %all-to-all-start.1 = ((bf16[64,8,3840]{2,1,0:T(8,128)(2,1)}), bf16[64,8,3840]{2,1,0:T(8,128)(2,1)}, u32[]{:S(2)}, u32[]{:S(2)}) async-start(bf16[64,8,3840]{2,1,0:T(8,128)(2,1)} %bitcast.13), calls=%async_computation.1 | async-start | bytes 7864320 | tf_op jit(solution)/shard_map/all_to_all | solution.py:620
  82.8 0.0 collective-permute-done.other_ref.other_meta
  82.8 9.7 %norm.1 = (bf16[384,5120]{1,0:T(8,128)(2,1)}, bf16[384,5120]{1,0:T(8,128)(2,1)}, f32[384,128]{1,0:T(8,128)}, f32[384,128]{1,0:T(8,128)}, f32[1,5120]{1,0:T(1,128)}, /*index=5*/f32[1,5120]{1,0:T(1,128)}) custom-call(bf16[512,3968]{1,0:T(8,128)(2,1)} %bitcast.3.own_ref.own_meta, bf16[512,3968]{1,0:T(8,128)(2,1)} %collective-permute-done.other_ref.other_meta, ...), custom_call_target="tpu_custom_call" | custom-call | flops 377487360 | bytes 24625156 | tf_op jit(solution)/shard_map/norm/pallas_call | solution.py:476
  92.5 19.0 %forward.1 = (bf16[384,5120]{1,0:T(8,128)(2,1)}, bf16[384,768]{1,0:T(8,128)(2,1)}, f32[768,768]{1,0:T(8,128)}) custom-call(bf16[384,5120]{1,0:T(8,128)(2,1)} %get-tuple-element.30.own_ref.normed_ref, bf16[384,5120]{1,0:T(8,128)(2,1)} %get-tuple-element.31.other_ref, bf16[1,5120,768]{2,1,0:T(8,128)(2,1)} %weight_ref.3, bf16[1,768,5120]{2,1,0:T(8,128)(2,1)} %down_ref.3), custom_call_target="tpu_custom_call" | custom-call | flops 9059696640 | bytes 31457280 | tf_op jit(solution)/shard_map/forward/pallas_call | solution.py:581
  111.5 0.3 collective-permute-start.1
  111.8 7.5 %forward_own.1.own_ref = bf16[384,5120]{1,0:T(8,128)(2,1)} custom-call(bf16[384,768]{1,0:T(8,128)(2,1)} %get-tuple-element.32.x_ref, bf16[1,768,5120]{2,1,0:T(8,128)(2,1)} %down_ref.3), custom_call_target="tpu_custom_call" | custom-call | flops 193273528320 | bytes 754974720 | tf_op jit(solution)/shard_map/forward_own/pallas_call | solution.py:606
  119.3 0.0 collective-permute-done.1.other_ref
  119.3 8.1 %out.1 = (bf16[384,5120]{1,0:T(8,128)(2,1)}, bf16[512,3840]{1,0:T(8,128)(2,1)}) custom-call(bf16[384,5120]{1,0:T(8,128)(2,1)} %forward_own.1.own_ref, bf16[384,5120]{1,0:T(8,128)(2,1)} %collective-permute-done.1.other_ref, f32[384,128]{1,0:T(8,128)} %get-tuple-element.34.gate_ref.own_gate, bf16[192,192]{1,0:T(8,128)(2,1)} %constant.9.clone.back_ref), custom_call_target="tpu_custom_call" | custom-call | flops 188743680 | bytes 15998976 | tf_op jit(solution)/shard_map/out/pallas_call | solution.py:476
  127.4 4.7 %all-to-all-done.1 = bf16[64,8,3840]{2,1,0:T(8,128)(2,1)} async-done(((bf16[64,8,3840]{2,1,0:T(8,128)(2,1)}), bf16[64,8,3840]{2,1,0:T(8,128)(2,1)}, u32[]{:S(2)}, u32[]{:S(2)}) %all-to-all-start.1) | async-done | bytes 3932192 | tf_op jit(solution)/shard_map/all_to_all | solution.py:620
  132.1 2.1 collective-permute-start.2
  134.2 8.8 %all-to-all-start.2 = ((bf16[64,8,3840]{2,1,0:T(8,128)(2,1)}), bf16[64,8,3840]{2,1,0:T(8,128)(2,1)}, u32[]{:S(2)}, u32[]{:S(2)}) async-start(bf16[64,8,3840]{2,1,0:T(8,128)(2,1)} %bitcast.14), calls=%async_computation.2 | async-start | bytes 7864320 | tf_op jit(solution)/shard_map/all_to_all | solution.py:620
  143.0 0.0 collective-permute-done.2.other_ref
  143.0 10.6 %cot.1 = (bf16[384,5120]{1,0:T(8,128)(2,1)}, bf16[384,5120]{1,0:T(8,128)(2,1)}, f32[384,128]{1,0:T(8,128)}, f32[8,5120]{1,0:T(8,128)}) custom-call(bf16[512,3840]{1,0:T(8,128)(2,1)} %bitcast.5.own_ref, bf16[512,3840]{1,0:T(8,128)(2,1)} %collective-permute-done.2.other_ref, f32[384,128]{1,0:T(8,128)} %get-tuple-element.34.gate_ref.own_gate, ...), custom_call_target="tpu_custom_call" | custom-call | flops 377487360 | bytes 24420352 | tf_op jit(solution)/shard_map/cot/pallas_call | solution.py:476
  153.6 0.4 collective-permute-start.4
  154.0 18.1 %backward.1 = (bf16[384,5120]{1,0:T(8,128)(2,1)}, bf16[384,768]{1,0:T(8,128)(2,1)}) custom-call(bf16[384,5120]{1,0:T(8,128)(2,1)} %get-tuple-element.40.own_ref, bf16[384,5120]{1,0:T(8,128)(2,1)} %get-tuple-element.41.other_ref, bf16[1,768,5120]{2,1,0:T(8,128)(2,1)} %down_ref.3, bf16[1,5120,768]{2,1,0:T(8,128)(2,1)} %weight_ref.3, ...), custom_call_target="tpu_custom_call" | custom-call | flops 9059696640 | bytes 31457280 | tf_op jit(solution)/shard_map/backward/pallas_call | solution.py:581
  172.1 0.2 collective-permute-start.3
  172.4 7.7 %backward_own.1.own_ref = bf16[384,5120]{1,0:T(8,128)(2,1)} custom-call(bf16[384,768]{1,0:T(8,128)(2,1)} %get-tuple-element.43.x_ref, bf16[1,5120,768]{2,1,0:T(8,128)(2,1)} %weight_ref.3), custom_call_target="tpu_custom_call" | custom-call | flops 193273528320 | bytes 754974720 | tf_op jit(solution)/shard_map/backward_own/pallas_call | solution.py:606
  180.0 0.0 collective-permute-done.4.other_router
  180.0 0.0 collective-permute-done.3.other_ref
  180.0 9.4 %grad.1 = bf16[512,3968]{1,0:T(8,128)(2,1)} custom-call(bf16[384,5120]{1,0:T(8,128)(2,1)} %backward_own.1.own_ref, bf16[384,5120]{1,0:T(8,128)(2,1)} %collective-permute-done.3.other_ref, f32[384,128]{1,0:T(8,128)} %get-tuple-element.45.choice_ref, bf16[384,5120]{1,0:T(8,128)(2,1)} %get-tuple-element.30.own_ref.normed_ref, ...), custom_call_target="tpu_custom_call" | custom-call | flops 188743680 | bytes 16498692 | tf_op jit(solution)/shard_map/grad/pallas_call | solution.py:476
  189.5 2.9 %all-to-all-done.2 = bf16[64,8,3840]{2,1,0:T(8,128)(2,1)} async-done(((bf16[64,8,3840]{2,1,0:T(8,128)(2,1)}), bf16[64,8,3840]{2,1,0:T(8,128)(2,1)}, u32[]{:S(2)}, u32[]{:S(2)}) %all-to-all-start.2) | async-done | bytes 3932192 | tf_op jit(solution)/shard_map/all_to_all | solution.py:620
  192.4 0.0 copy-start
  192.4 10.0 %all-to-all-start.3 = ((bf16[64,8,3968]{2,1,0:T(8,128)(2,1)}), bf16[64,8,3968]{2,1,0:T(8,128)(2,1)}, u32[]{:S(2)}, u32[]{:S(2)}) async-start(bf16[64,8,3968]{2,1,0:T(8,128)(2,1)} %bitcast.11), calls=%async_computation.3 | async-start | bytes 8126464 | tf_op jit(solution)/shard_map/all_to_all | solution.py:620
  202.4 0.0 copy-done
  202.4 0.7 copy.14.ids_ref
  203.1 6.7 %mixed.1 = bf16[128,5120]{1,0:T(8,128)(2,1)} custom-call(s32[128,2]{1,0:T(8,128)} %copy.14.ids_ref, bf16[128,5120]{1,0:T(8,128)(2,1)} %tokens_ref.3, bf16[512,3840]{1,0:T(8,128)(2,1)} %bitcast.7.band0.band1.band2, bf16[512,3840]{1,0:T(8,128)(2,1)} %bitcast.7.band0.band1.band2, bf16[512,3840]{1,0:T(8,128)(2,1)} %bitcast.7.band0.band1.band2), custom_call_target="tpu_custom_call" | custom-call | flops 1006632960 | bytes 3932160 | tf_op jit(solution)/shard_map/mixed/pallas_call | solution.py:245
  209.8 42.3 %all-to-all-done.3 = bf16[64,8,3968]{2,1,0:T(8,128)(2,1)} async-done(((bf16[64,8,3968]{2,1,0:T(8,128)(2,1)}), bf16[64,8,3968]{2,1,0:T(8,128)(2,1)}, u32[]{:S(2)}, u32[]{:S(2)}) %all-to-all-start.3) | async-done | bytes 4063264 | tf_op jit(solution)/shard_map/all_to_all | solution.py:620
  252.1 1.9 sums.1
  254.0 0.0 copy-start.1
  254.0 2.7 %collective-permute-start.5 = (f32[1,320]{1,0:T(1,128)}, f32[1,320]{1,0:T(1,128)S(1)}, u32[]{:S(2)}, u32[]{:S(2)}) collective-permute-start(f32[1,320]{1,0:T(1,128)} %get-tuple-element.51), channel_id=1, source_target_pairs={{0,1},{1,0},{2,3},{3,2},{4,5},{5,4},{6,7},{7,6},{8,9},{9,8},{10,11... | collective-permute-start | bytes 3848 | tf_op jit(solution)/shard_map/ppermute | solution.py:625
  256.7 7.9 %grad_tokens.1 = bf16[128,5120]{1,0:T(8,128)(2,1)} custom-call(s32[128,2]{1,0:T(8,128)} %copy.14.ids_ref, bf16[128,5120]{1,0:T(8,128)(2,1)} %tokens_ref.3, bf16[128,5120]{1,0:T(8,128)(2,1)} %cot_ref.1, bf16[512,3968]{1,0:T(8,128)(2,1)} %bitcast.9.band0.band1.band2.meta_ref, bf16[512,3968]{1,0:T(8,128)(2,1)} %bitcast.9.band0.band1.band2.meta_ref, ...), custom_call_target="tpu_custom_call" | custom-call | flops 1006632960 | bytes 3932160 | tf_op jit(solution)/shard_map/grad_tokens/pallas_call | solution.py:245
  264.6 0.0 collective-permute-done.5
  264.6 0.0 copy-done.1
  264.6 0.6 add_reduce_fusion
Async XLA Ops:
  9.0 62.5 %all-to-all-start = ((bf16[64,8,3968]{2,1,0:T(8,128)(2,1)}), bf16[64,8,3968]{2,1,0:T(8,128)(2,1)}, u32[]{:S(2)}, u32[]{:S(2)}) async-start(bf16[64,8,3968]{2,1,0:T(8,128)(2,1)} %bitcast.12), calls=%async_computation | async-start | bytes 8126464 | tf_op jit(solution)/shard_map/all_to_all | solution.py:620
  71.5 11.3 %collective-permute-start = (bf16[512,3968]{1,0:T(8,128)(2,1)}, bf16[512,3968]{1,0:T(8,128)(2,1)}, u32[]{:S(2)}, u32[]{:S(2)}) collective-permute-start(bf16[512,3968]{1,0:T(8,128)(2,1)} %bitcast.3.own_ref.own_meta), channel_id=1, source_target_pairs={{0,1},{1,0},{2,3},{3,2},{4,5},{5,4},{6,7},{7,6},{8,9},{9,8},{10,11... | collective-permute-start | bytes 12189704 | tf_op jit(solution)/shard_map/ppermute | solution.py:625
  74.0 58.1 %all-to-all-start.1 = ((bf16[64,8,3840]{2,1,0:T(8,128)(2,1)}), bf16[64,8,3840]{2,1,0:T(8,128)(2,1)}, u32[]{:S(2)}, u32[]{:S(2)}) async-start(bf16[64,8,3840]{2,1,0:T(8,128)(2,1)} %bitcast.13), calls=%async_computation.1 | async-start | bytes 7864320 | tf_op jit(solution)/shard_map/all_to_all | solution.py:620
  111.5 7.8 %collective-permute-start.1 = (bf16[384,5120]{1,0:T(8,128)(2,1)}, bf16[384,5120]{1,0:T(8,128)(2,1)}, u32[]{:S(2)}, u32[]{:S(2)}) collective-permute-start(bf16[384,5120]{1,0:T(8,128)(2,1)} %get-tuple-element.33), channel_id=1, source_target_pairs={{0,1},{1,0},{2,3},{3,2},{4,5},{5,4},{6,7},{7,6},{8,9},{9,8},{10,11... | collective-permute-start | bytes 11796488 | tf_op jit(solution)/shard_map/ppermute | solution.py:625
  132.1 10.8 %collective-permute-start.2 = (bf16[512,3840]{1,0:T(8,128)(2,1)}, bf16[512,3840]{1,0:T(8,128)(2,1)}, u32[]{:S(2)}, u32[]{:S(2)}) collective-permute-start(bf16[512,3840]{1,0:T(8,128)(2,1)} %bitcast.5.own_ref), channel_id=1, source_target_pairs={{0,1},{1,0},{2,3},{3,2},{4,5},{5,4},{6,7},{7,6},{8,9},{9,8},{10,11... | collective-permute-start | bytes 11796488 | tf_op jit(solution)/shard_map/ppermute | solution.py:625
  134.2 58.2 %all-to-all-start.2 = ((bf16[64,8,3840]{2,1,0:T(8,128)(2,1)}), bf16[64,8,3840]{2,1,0:T(8,128)(2,1)}, u32[]{:S(2)}, u32[]{:S(2)}) async-start(bf16[64,8,3840]{2,1,0:T(8,128)(2,1)} %bitcast.14), calls=%async_computation.2 | async-start | bytes 7864320 | tf_op jit(solution)/shard_map/all_to_all | solution.py:620
  153.6 26.4 %collective-permute-start.4 = (f32[8,5120]{1,0:T(8,128)}, f32[8,5120]{1,0:T(8,128)}, u32[]{:S(2)}, u32[]{:S(2)}) collective-permute-start(f32[8,5120]{1,0:T(8,128)} %get-tuple-element.48.own_router), channel_id=1, source_target_pairs={{0,1},{1,0},{2,3},{3,2},{4,5},{5,4},{6,7},{7,6},{8,9},{9,8},{10,11... | collective-permute-start | bytes 491528 | tf_op jit(solution)/shard_map/ppermute | solution.py:625
  172.1 7.9 %collective-permute-start.3 = (bf16[384,5120]{1,0:T(8,128)(2,1)}, bf16[384,5120]{1,0:T(8,128)(2,1)}, u32[]{:S(2)}, u32[]{:S(2)}) collective-permute-start(bf16[384,5120]{1,0:T(8,128)(2,1)} %get-tuple-element.44), channel_id=1, source_target_pairs={{0,1},{1,0},{2,3},{3,2},{4,5},{5,4},{6,7},{7,6},{8,9},{9,8},{10,11... | collective-permute-start | bytes 11796488 | tf_op jit(solution)/shard_map/ppermute | solution.py:625
  192.4 10.0 %copy-start = (s32[128,2]{0,1:T(2,128)S(1)}, s32[128,2]{0,1:T(2,128)}, u32[]{:S(2)}) copy-start(s32[128,2]{0,1:T(2,128)} %param.14) | copy-start | bytes 3076
  192.4 59.8 %all-to-all-start.3 = ((bf16[64,8,3968]{2,1,0:T(8,128)(2,1)}), bf16[64,8,3968]{2,1,0:T(8,128)(2,1)}, u32[]{:S(2)}, u32[]{:S(2)}) async-start(bf16[64,8,3968]{2,1,0:T(8,128)(2,1)} %bitcast.11), calls=%async_computation.3 | async-start | bytes 8126464 | tf_op jit(solution)/shard_map/all_to_all | solution.py:620
  254.0 10.6 %copy-start.1 = (f32[1,320]{1,0:T(1,128)S(1)}, f32[1,320]{1,0:T(1,128)}, u32[]{:S(2)}) copy-start(f32[1,320]{1,0:T(1,128)} %get-tuple-element.50) | copy-start | bytes 3844
  254.0 10.6 %collective-permute-start.5 = (f32[1,320]{1,0:T(1,128)}, f32[1,320]{1,0:T(1,128)S(1)}, u32[]{:S(2)}, u32[]{:S(2)}) collective-permute-start(f32[1,320]{1,0:T(1,128)} %get-tuple-element.51), channel_id=1, source_target_pairs={{0,1},{1,0},{2,3},{3,2},{4,5},{5,4},{6,7},{7,6},{8,9},{9,8},{10,11... | collective-permute-start | bytes 3848 | tf_op jit(solution)/shard_map/ppermute | solution.py:625

commit v3 on v2

--- a/solution.py
+++ b/solution.py
@@ -19,8 +19,9 @@
 BF16 = jnp.bfloat16
 F32 = jnp.float32
 LOUD = 64
+PACK_STEPS = 2
 META = 128
-SUB = 2
+SUB = 4
 VMEM_LIMIT = 56 * 1024 * 1024
 CHIPS = ("ep", "pair")
 FSDP = ("pair", "core")
@@ -107,13 +108,11 @@
 
     if meta_refs:
         gain_ref, router_ref, core_ref = meta_refs
-        shard = router_ref.shape[0]
+        shard = router_ref.shape[1]
         shift = core_ref[0, 0] * (META // 2)
         shifted = as_bf16(iota((shard, 3 * META), 1) == iota((shard, 3 * META), 0) + shift)
-        gain = dot(gain_ref[...], shifted)
-        columns = lax.dot_general(
-            router_ref[...], shifted, (((0,), (0,)), ((), ())), preferred_element_type=F32
-        ).astype(BF16)
+        gain = dot(gain_ref[...].reshape(1, shard), shifted)
+        columns = dot(router_ref[...], shifted).astype(BF16)
         tile_row = iota((count, META), 0) & (TILE - 1)
         pick_row = step * count + iota((count, experts), 0)
         pick_column = iota((count, experts), 1)
@@ -132,10 +131,15 @@
     toks, features = rows.shape
     width = features * CAP // TILE + (META if meta else 0)
     out_rows = experts * TILE
-    steps = 4
+    steps = PACK_STEPS
     meta_specs = []
     if meta:
-        meta_specs = [pl.BlockSpec(value.shape, lambda i: (0, 0)) for value in meta[:2]] + [SMALL]
+        gain, router, _ = meta
+        meta_specs = [
+            pl.BlockSpec(gain.shape, lambda i: (0,)),
+            pl.BlockSpec(router.shape, lambda i: (0, 0)),
+            SMALL,
+        ]
     return pl.pallas_call(
         functools.partial(pack_kernel, experts),
         grid=(steps,),
@@ -186,22 +190,31 @@
     return pieces
 
 
-def mixed_kernel(ids_ref, tokens_ref, band0, band1, band2, out_ref, choose_ref):
+def mixed_kernel(ids_ref, tokens_ref, band0, band1, band2, out_ref, choose_ref, scale_ref, square_ref):
     step = pl.program_id(0)
     width = band0.shape[1]
-    piece = tokens_ref.shape[1] // PARTS
+    features = tokens_ref.shape[1]
+    piece = features // PARTS
 
     @pl.when(step == 0)
     def _():
         fill_choosing(ids_ref, choose_ref)
+        square_ref[...] = jnp.zeros_like(square_ref)
 
     for number, value in enumerate(summed_pieces(choose_ref, (band0, band1, band2))):
         cols = pl.ds(pl.multiple_of(number * piece + step * width, width), width)
-        out_ref[:, cols] = (tokens_ref[:, cols].astype(F32) + value).astype(BF16)
+        x = tokens_ref[:, cols].astype(F32)
+        square_ref[...] += x * x
+        out_ref[:, cols] = (x + value).astype(BF16)
+
+    @pl.when(step == pl.num_programs(0) - 1)
+    def _():
+        scale = lax.rsqrt(jnp.sum(square_ref[...], axis=1, keepdims=True) / features + EPS)
+        scale_ref[...] = jnp.broadcast_to(scale, scale_ref.shape)
 
 
 def grad_tokens_kernel(
-    ids_ref, tokens_ref, cot_ref, band0, band1, band2, out_ref, choose_ref, grad_ref, square_ref, cross_ref
+    choose_ref, scale_ref, tokens_ref, cot_ref, band0, band1, band2, out_ref, grad_ref, cross_ref
 ):
     step = pl.program_id(0)
     width = band0.shape[1]
@@ -210,20 +223,16 @@
 
     @pl.when(step == 0)
     def _():
-        fill_choosing(ids_ref, choose_ref)
-        square_ref[...] = jnp.zeros_like(square_ref)
         cross_ref[...] = jnp.zeros_like(cross_ref)
 
     for number, value in enumerate(summed_pieces(choose_ref, (band0, band1, band2))):
         cols = pl.ds(pl.multiple_of(number * piece + step * width, width), width)
-        x = tokens_ref[:, cols].astype(F32)
         grad_ref[:, cols] = value
-        square_ref[...] += x * x
-        cross_ref[...] += x * value
+        cross_ref[...] += tokens_ref[:, cols].astype(F32) * value
 
     @pl.when(step == pl.num_programs(0) - 1)
     def _():
-        scale = lax.rsqrt(jnp.sum(square_ref[...], axis=1, keepdims=True) / features + EPS)
+        scale = scale_ref[:, 0:1]
         back = jnp.sum(cross_ref[...], axis=1, keepdims=True) / features * scale * scale * scale
         for at in range(0, features, width):
             cols = slice(at, at + width)
@@ -232,29 +241,29 @@
             out_ref[:, cols] = (cot_ref[:, cols].astype(F32) + grad).astype(BF16)
 
 
-def token_side(kernel, ids, row_inputs, bands, scratch, name):
-    toks, features = row_inputs[0].shape
-    piece = features // PARTS
-    width = 256
+def token_side(kernel, whole_inputs, bands, out_shapes, scratch, name):
+    columns = bands.shape[0]
+    piece = whole_inputs[-1].shape[1] // PARTS
+    width = piece
     steps = piece // width
-    columns = bands.shape[0]
+
+    def whole(shape):
+        return pl.BlockSpec(shape, lambda c: (0,) * len(shape))
 
     def band_spec(band):
-        return pl.BlockSpec((columns, width), lambda c, band=band: (0, band * steps + c))
+        return pl.BlockSpec((columns, width), lambda c: (0, band * steps + c))
 
     return pl.pallas_call(
         kernel,
         grid=(steps,),
-        in_specs=[pl.BlockSpec((toks, 2), lambda c: (0, 0))]
-        + [pl.BlockSpec((toks, features), lambda c: (0, 0))] * len(row_inputs)
-        + [band_spec(band) for band in range(BANDS)],
-        out_specs=pl.BlockSpec((toks, features), lambda c: (0, 0)),
-        out_shape=jax.ShapeDtypeStruct((toks, features), BF16),
-        scratch_shapes=[pltpu.VMEM((BANDS, 2 * toks, columns), BF16)] + scratch,
+        in_specs=[whole(value.shape) for value in whole_inputs] + [band_spec(b) for b in range(BANDS)],
+        out_specs=[whole(shape.shape) for shape in out_shapes],
+        out_shape=out_shapes,
+        scratch_shapes=scratch,
         compiler_params=params(1),
-        cost_estimate=cost(2 * BANDS * 2 * toks * columns * piece, 2 * columns * BANDS * piece),
+        cost_estimate=cost(columns * columns * BANDS * piece, 2 * columns * BANDS * piece),
         name=name,
-    )(ids, *row_inputs, *([bands] * BANDS))
+    )(*whole_inputs, *([bands] * BANDS))
 
 
 def sums_kernel(scale, meta_ref, core_ref, router_ref, own_ref, other_ref):
@@ -645,7 +654,7 @@
     meta_spec = pl.BlockSpec((pairs * TILE, META), lambda g: (0, width // META))
 
     cot_sent = pack(ids_t, cotangent, experts)
-    arrived = exchange(pack(ids_t, tokens, experts, (norm_gain.reshape(1, shard), router_weight, core)))
+    arrived = exchange(pack(ids_t, tokens, experts, (norm_gain, router_weight.T, core)))
     arrived, cot_sent = lax.optimization_barrier((arrived, cot_sent))
     arrived_other = swap(arrived)
     cot_arrived = exchange(cot_sent)
@@ -731,20 +740,25 @@
         [pltpu.VMEM(fold, F32), pltpu.VMEM((pairs * TILE, META), F32)],
     )
     grad_back = exchange(grad_sent)
-    mixed = token_side(mixed_kernel, expert_ids, [tokens], result_back, [], "mixed")
-    grad_tokens = token_side(
+    out_rows = jax.ShapeDtypeStruct((toks, features), BF16)
+    choosing = jax.ShapeDtypeStruct((BANDS, 2 * toks, tiles), BF16)
+    partial = pltpu.VMEM((toks, features // PARTS), F32)
+    mixed, choose, scale = token_side(
+        mixed_kernel,
+        [expert_ids, tokens],
+        result_back,
+        [out_rows, choosing, jax.ShapeDtypeStruct((toks, 128), F32)],
+        [partial],
+        "mixed",
+    )
+    (grad_tokens,) = token_side(
         grad_tokens_kernel,
-        expert_ids,
-        [tokens, cotangent],
+        [choose, scale, tokens, cotangent],
         grad_back,
-        [
-            pltpu.VMEM((toks, features), F32),
-            pltpu.VMEM((toks, 256), F32),
-            pltpu.VMEM((toks, 256), F32),
-        ],
+        [out_rows],
+        [pltpu.VMEM((toks, features), F32), partial],
         "grad_tokens",
     )
-
     grad_router, own_gain, other_gain = summed(grad_back, core, shard, 1.0 / math.sqrt(toks * devices))
     grad_gain = (own_gain + swap(other_gain)).reshape(shard)
     grad_router = grad_router.T

time: 268 us -> 263 us (0.981)
  Pallas kernels: 117 us -> 110 us
  waiting for transfers between devices: 95.5 us -> 99.7 us
  local copies, waits for them, and re-layouts: 3.53 us -> 0.75 us
    all_to_all x4, waiting for transfers between devices: 95.5 us -> 99.7 us  [exchange(): lax.all_to_all(blocks, CHIPS, split_axis=0, concat_axis=0, tiled=True)]
    pallas_call x2, Pallas kernels: 14.5 us -> 11.4 us  [token_side(): pl.pallas_call(kernel, grid=(steps,), in_specs=[whole(value.shape) for va...]
  transfers between devices with their start and end apart: 10 -> 10, of which waited for: 4 -> 4; matrix products, arithmetic and copies ran while one was open for 0% -> 0% of each run, Pallas kernels for 41% -> 40%
where the time goes in v3:
time: 263 us; the launch traced here: 260 us
  Pallas kernels  110 us (42%)
  waiting for transfers between devices  99.7 us (38%)
  starting transfers between devices  47.7 us (18%)
    all_to_all x4, waiting for transfers between devices, exchange(): lax.all_to_all(blocks, CHIPS, split_axis=0, concat_axis=0, tiled=True)  99.7 us
    all_to_all x4, starting transfers between devices, exchange(): lax.all_to_all(blocks, CHIPS, split_axis=0, concat_axis=0, tiled=True)  39.6 us
    pallas_call x2, Pallas kernels, expert_call(): pl.pallas_call(kernel, grid=(2 * half,), in_specs=in_specs, out_specs=out...  37.2 us
    pallas_call x4, Pallas kernels, by_group(): pl.pallas_call(kernel, grid=(steps,), in_specs=[spec(value.shape, rows) f...  35.5 us
    pallas_call x2, Pallas kernels, last_call(): pl.pallas_call(functools.partial(last_kernel, product=product), grid=(PAR...  15.2 us
    pallas_call x2, Pallas kernels, token_side(): pl.pallas_call(kernel, grid=(steps,), in_specs=[whole(value.shape) for va...  11.4 us
    pallas_call x2, Pallas kernels, pack(): pl.pallas_call(functools.partial(pack_kernel, experts), grid=(steps,), in...  9 us
    ppermute x6, starting transfers between devices, swap(): return lax.ppermute(value, 'core', [(0, 1), (1, 0)])  8.12 us
  transfers between devices with their start and end apart: 10, of which 4 were waited for; matrix products, arithmetic and copies ran while one was open for 0% of the time, Pallas kernels for 40%

profile of v3, /device:TPU:1, one launch (start us, length us, event | category | flops | bytes accessed | tf_op | source)
XLA Modules:
  0.0 259.7 jit_solution(1430955226151589877)
XLA Ops:
  0.6 4.8 %pack.2 = bf16[512,3968]{1,0:T(8,128)(2,1)} custom-call(s32[2,128]{1,0:T(2,128)} %bitcast.17, bf16[128,5120]{1,0:T(8,128)(2,1)} %tokens_ref.3, bf16[320]{0:T(512)(128)(2,1)} %refs_0_.1, bf16[64,320]{1,0:T(8,128)(2,1)} %bitcast.16, s32[1,1]{1,0:T(1,128)} %bitcast.2.refs_2_.core_ref), custom_call_target="tpu_custom_call" | custom-call | flops 1040187392 | bytes 4063232 | tf_op jit(solution)/shard_map/pack/pallas_call | solution.py:143
  5.4 12.2 %all-to-all-start = ((bf16[64,8,3968]{2,1,0:T(8,128)(2,1)}), bf16[64,8,3968]{2,1,0:T(8,128)(2,1)}, u32[]{:S(2)}, u32[]{:S(2)}) async-start(bf16[64,8,3968]{2,1,0:T(8,128)(2,1)} %bitcast.13), calls=%async_computation | async-start | bytes 8126464 | tf_op jit(solution)/shard_map/all_to_all | solution.py:629
  17.6 4.2 %pack.3 = bf16[512,3840]{1,0:T(8,128)(2,1)} custom-call(s32[2,128]{1,0:T(2,128)} %bitcast.18, bf16[128,5120]{1,0:T(8,128)(2,1)} %cot_ref.1), custom_call_target="tpu_custom_call" | custom-call | flops 1006632960 | bytes 3932160 | tf_op jit(solution)/shard_map/pack/pallas_call | solution.py:143
  21.8 46.1 %all-to-all-done = bf16[64,8,3968]{2,1,0:T(8,128)(2,1)} async-done(((bf16[64,8,3968]{2,1,0:T(8,128)(2,1)}), bf16[64,8,3968]{2,1,0:T(8,128)(2,1)}, u32[]{:S(2)}, u32[]{:S(2)}) %all-to-all-start) | async-done | bytes 4063264 | tf_op jit(solution)/shard_map/all_to_all | solution.py:629
  67.9 2.5 collective-permute-start
  70.4 8.8 %all-to-all-start.1 = ((bf16[64,8,3840]{2,1,0:T(8,128)(2,1)}), bf16[64,8,3840]{2,1,0:T(8,128)(2,1)}, u32[]{:S(2)}, u32[]{:S(2)}) async-start(bf16[64,8,3840]{2,1,0:T(8,128)(2,1)} %bitcast.14), calls=%async_computation.1 | async-start | bytes 7864320 | tf_op jit(solution)/shard_map/all_to_all | solution.py:629
  79.2 0.0 collective-permute-done.other_ref.other_meta
  79.2 10.0 %norm.1 = (bf16[384,5120]{1,0:T(8,128)(2,1)}, bf16[384,5120]{1,0:T(8,128)(2,1)}, f32[384,128]{1,0:T(8,128)}, f32[384,128]{1,0:T(8,128)}, f32[1,5120]{1,0:T(1,128)}, /*index=5*/f32[1,5120]{1,0:T(1,128)}) custom-call(bf16[512,3968]{1,0:T(8,128)(2,1)} %bitcast.4.own_ref.own_meta, bf16[512,3968]{1,0:T(8,128)(2,1)} %collective-permute-done.other_ref.other_meta, ...), custom_call_target="tpu_custom_call" | custom-call | flops 377487360 | bytes 24625156 | tf_op jit(solution)/shard_map/norm/pallas_call | solution.py:485
  89.1 19.1 %forward.1 = (bf16[384,5120]{1,0:T(8,128)(2,1)}, bf16[384,768]{1,0:T(8,128)(2,1)}, f32[768,768]{1,0:T(8,128)}) custom-call(bf16[384,5120]{1,0:T(8,128)(2,1)} %get-tuple-element.33.own_ref.normed_ref, bf16[384,5120]{1,0:T(8,128)(2,1)} %get-tuple-element.34.other_ref, bf16[1,5120,768]{2,1,0:T(8,128)(2,1)} %weight_ref.3, bf16[1,768,5120]{2,1,0:T(8,128)(2,1)} %down_ref.3), custom_call_target="tpu_custom_call" | custom-call | flops 9059696640 | bytes 31457280 | tf_op jit(solution)/shard_map/forward/pallas_call | solution.py:590
  108.2 0.3 collective-permute-start.1
  108.5 7.6 %forward_own.1.own_ref = bf16[384,5120]{1,0:T(8,128)(2,1)} custom-call(bf16[384,768]{1,0:T(8,128)(2,1)} %get-tuple-element.35.x_ref, bf16[1,768,5120]{2,1,0:T(8,128)(2,1)} %down_ref.3), custom_call_target="tpu_custom_call" | custom-call | flops 193273528320 | bytes 754974720 | tf_op jit(solution)/shard_map/forward_own/pallas_call | solution.py:615
  116.1 0.0 collective-permute-done.1.other_ref
  116.1 7.0 %out.1 = (bf16[384,5120]{1,0:T(8,128)(2,1)}, bf16[512,3840]{1,0:T(8,128)(2,1)}) custom-call(bf16[384,5120]{1,0:T(8,128)(2,1)} %forward_own.1.own_ref, bf16[384,5120]{1,0:T(8,128)(2,1)} %collective-permute-done.1.other_ref, f32[384,128]{1,0:T(8,128)} %get-tuple-element.37.gate_ref.own_gate, bf16[192,192]{1,0:T(8,128)(2,1)} %constant.9.clone.back_ref), custom_call_target="tpu_custom_call" | custom-call | flops 188743680 | bytes 15998976 | tf_op jit(solution)/shard_map/out/pallas_call | solution.py:485
  123.1 5.4 %all-to-all-done.1 = bf16[64,8,3840]{2,1,0:T(8,128)(2,1)} async-done(((bf16[64,8,3840]{2,1,0:T(8,128)(2,1)}), bf16[64,8,3840]{2,1,0:T(8,128)(2,1)}, u32[]{:S(2)}, u32[]{:S(2)}) %all-to-all-start.1) | async-done | bytes 3932192 | tf_op jit(solution)/shard_map/all_to_all | solution.py:629
  128.5 2.1 collective-permute-start.2
  130.6 8.6 %all-to-all-start.2 = ((bf16[64,8,3840]{2,1,0:T(8,128)(2,1)}), bf16[64,8,3840]{2,1,0:T(8,128)(2,1)}, u32[]{:S(2)}, u32[]{:S(2)}) async-start(bf16[64,8,3840]{2,1,0:T(8,128)(2,1)} %bitcast.15), calls=%async_computation.2 | async-start | bytes 7864320 | tf_op jit(solution)/shard_map/all_to_all | solution.py:629
  139.2 0.0 collective-permute-done.2.other_ref
  139.2 9.2 %cot.1 = (bf16[384,5120]{1,0:T(8,128)(2,1)}, bf16[384,5120]{1,0:T(8,128)(2,1)}, f32[384,128]{1,0:T(8,128)}, f32[8,5120]{1,0:T(8,128)}) custom-call(bf16[512,3840]{1,0:T(8,128)(2,1)} %bitcast.6.own_ref, bf16[512,3840]{1,0:T(8,128)(2,1)} %collective-permute-done.2.other_ref, f32[384,128]{1,0:T(8,128)} %get-tuple-element.37.gate_ref.own_gate, ...), custom_call_target="tpu_custom_call" | custom-call | flops 377487360 | bytes 24420352 | tf_op jit(solution)/shard_map/cot/pallas_call | solution.py:485
  148.5 0.4 collective-permute-start.4
  148.8 18.1 %backward.1 = (bf16[384,5120]{1,0:T(8,128)(2,1)}, bf16[384,768]{1,0:T(8,128)(2,1)}) custom-call(bf16[384,5120]{1,0:T(8,128)(2,1)} %get-tuple-element.46.own_ref, bf16[384,5120]{1,0:T(8,128)(2,1)} %get-tuple-element.47.other_ref, bf16[1,768,5120]{2,1,0:T(8,128)(2,1)} %down_ref.3, bf16[1,5120,768]{2,1,0:T(8,128)(2,1)} %weight_ref.3, ...), custom_call_target="tpu_custom_call" | custom-call | flops 9059696640 | bytes 31457280 | tf_op jit(solution)/shard_map/backward/pallas_call | solution.py:590
  166.9 0.2 collective-permute-start.3
  167.2 7.6 %backward_own.1.own_ref = bf16[384,5120]{1,0:T(8,128)(2,1)} custom-call(bf16[384,768]{1,0:T(8,128)(2,1)} %get-tuple-element.49.x_ref, bf16[1,5120,768]{2,1,0:T(8,128)(2,1)} %weight_ref.3), custom_call_target="tpu_custom_call" | custom-call | flops 193273528320 | bytes 754974720 | tf_op jit(solution)/shard_map/backward_own/pallas_call | solution.py:615
  174.8 0.0 collective-permute-done.4.other_router
  174.8 0.0 collective-permute-done.3.other_ref
  174.8 9.3 %grad.1 = bf16[512,3968]{1,0:T(8,128)(2,1)} custom-call(bf16[384,5120]{1,0:T(8,128)(2,1)} %backward_own.1.own_ref, bf16[384,5120]{1,0:T(8,128)(2,1)} %collective-permute-done.3.other_ref, f32[384,128]{1,0:T(8,128)} %get-tuple-element.51.choice_ref, bf16[384,5120]{1,0:T(8,128)(2,1)} %get-tuple-element.33.own_ref.normed_ref, ...), custom_call_target="tpu_custom_call" | custom-call | flops 188743680 | bytes 16498692 | tf_op jit(solution)/shard_map/grad/pallas_call | solution.py:485
  184.1 4.5 %all-to-all-done.2 = bf16[64,8,3840]{2,1,0:T(8,128)(2,1)} async-done(((bf16[64,8,3840]{2,1,0:T(8,128)(2,1)}), bf16[64,8,3840]{2,1,0:T(8,128)(2,1)}, u32[]{:S(2)}, u32[]{:S(2)}) %all-to-all-start.2) | async-done | bytes 3932192 | tf_op jit(solution)/shard_map/all_to_all | solution.py:629
  188.6 0.0 copy-start
  188.6 10.0 %all-to-all-start.3 = ((bf16[64,8,3968]{2,1,0:T(8,128)(2,1)}), bf16[64,8,3968]{2,1,0:T(8,128)(2,1)}, u32[]{:S(2)}, u32[]{:S(2)}) async-start(bf16[64,8,3968]{2,1,0:T(8,128)(2,1)} %bitcast.12), calls=%async_computation.3 | async-start | bytes 8126464 | tf_op jit(solution)/shard_map/all_to_all | solution.py:629
  198.6 0.0 copy-done
  198.6 0.7 copy.13.ids_ref
  199.4 5.3 %mixed.1 = (bf16[128,5120]{1,0:T(8,128)(2,1)}, bf16[3,256,512]{2,1,0:T(8,128)(2,1)}, f32[128,128]{1,0:T(8,128)}) custom-call(s32[128,2]{1,0:T(8,128)} %copy.13.ids_ref, bf16[128,5120]{1,0:T(8,128)(2,1)} %tokens_ref.3, bf16[512,3840]{1,0:T(8,128)(2,1)} %bitcast.8.band0.band1.band2, bf16[512,3840]{1,0:T(8,128)(2,1)} %bitcast.8.band0.band1.band2, ...), custom_call_target="tpu_custom_call" | custom-call | flops 1006632960 | bytes 3932160 | tf_op jit(solution)/shard_map/mixed/pallas_call | solution.py:256
  204.6 43.7 %all-to-all-done.3 = bf16[64,8,3968]{2,1,0:T(8,128)(2,1)} async-done(((bf16[64,8,3968]{2,1,0:T(8,128)(2,1)}), bf16[64,8,3968]{2,1,0:T(8,128)(2,1)}, u32[]{:S(2)}, u32[]{:S(2)}) %all-to-all-start.3) | async-done | bytes 4063264 | tf_op jit(solution)/shard_map/all_to_all | solution.py:629
  248.4 1.9 sums.1
  250.3 2.7 %collective-permute-start.5 = (f32[1,320]{1,0:T(1,128)}, f32[1,320]{1,0:T(1,128)S(1)}, u32[]{:S(2)}, u32[]{:S(2)}) collective-permute-start(f32[1,320]{1,0:T(1,128)} %get-tuple-element.57), channel_id=1, source_target_pairs={{0,1},{1,0},{2,3},{3,2},{4,5},{5,4},{6,7},{7,6},{8,9},{9,8},{10,11... | collective-permute-start | bytes 3848 | tf_op jit(solution)/shard_map/ppermute | solution.py:634
  253.0 0.0 copy-start.1
  253.0 6.2 %grad_tokens.1 = bf16[128,5120]{1,0:T(8,128)(2,1)} custom-call(bf16[3,256,512]{2,1,0:T(8,128)(2,1)} %get-tuple-element.41.choose_ref, f32[128,128]{1,0:T(8,128)} %get-tuple-element.42.scale_ref, bf16[128,5120]{1,0:T(8,128)(2,1)} %tokens_ref.3, bf16[128,5120]{1,0:T(8,128)(2,1)} %cot_ref.1, bf16[512,3968]{1,0:T(8,128)(2,1)} %bitcast.10.band0.band1.band2.meta_ref, ...), custom_call_target="tpu_custom_call" | custom-call | flops 1006632960 | bytes 3932160 | tf_op jit(solution)/shard_map/grad_tokens/pallas_call | solution.py:256
  259.1 0.0 collective-permute-done.5
  259.1 0.0 copy-done.1
  259.1 0.6 add_reduce_fusion
Async XLA Ops:
  5.4 62.5 %all-to-all-start = ((bf16[64,8,3968]{2,1,0:T(8,128)(2,1)}), bf16[64,8,3968]{2,1,0:T(8,128)(2,1)}, u32[]{:S(2)}, u32[]{:S(2)}) async-start(bf16[64,8,3968]{2,1,0:T(8,128)(2,1)} %bitcast.13), calls=%async_computation | async-start | bytes 8126464 | tf_op jit(solution)/shard_map/all_to_all | solution.py:629
  67.9 11.3 %collective-permute-start = (bf16[512,3968]{1,0:T(8,128)(2,1)}, bf16[512,3968]{1,0:T(8,128)(2,1)}, u32[]{:S(2)}, u32[]{:S(2)}) collective-permute-start(bf16[512,3968]{1,0:T(8,128)(2,1)} %bitcast.4.own_ref.own_meta), channel_id=1, source_target_pairs={{0,1},{1,0},{2,3},{3,2},{4,5},{5,4},{6,7},{7,6},{8,9},{9,8},{10,11... | collective-permute-start | bytes 12189704 | tf_op jit(solution)/shard_map/ppermute | solution.py:634
  70.4 58.1 %all-to-all-start.1 = ((bf16[64,8,3840]{2,1,0:T(8,128)(2,1)}), bf16[64,8,3840]{2,1,0:T(8,128)(2,1)}, u32[]{:S(2)}, u32[]{:S(2)}) async-start(bf16[64,8,3840]{2,1,0:T(8,128)(2,1)} %bitcast.14), calls=%async_computation.1 | async-start | bytes 7864320 | tf_op jit(solution)/shard_map/all_to_all | solution.py:629
  108.2 7.9 %collective-permute-start.1 = (bf16[384,5120]{1,0:T(8,128)(2,1)}, bf16[384,5120]{1,0:T(8,128)(2,1)}, u32[]{:S(2)}, u32[]{:S(2)}) collective-permute-start(bf16[384,5120]{1,0:T(8,128)(2,1)} %get-tuple-element.36), channel_id=1, source_target_pairs={{0,1},{1,0},{2,3},{3,2},{4,5},{5,4},{6,7},{7,6},{8,9},{9,8},{10,11... | collective-permute-start | bytes 11796488 | tf_op jit(solution)/shard_map/ppermute | solution.py:634
  128.5 10.7 %collective-permute-start.2 = (bf16[512,3840]{1,0:T(8,128)(2,1)}, bf16[512,3840]{1,0:T(8,128)(2,1)}, u32[]{:S(2)}, u32[]{:S(2)}) collective-permute-start(bf16[512,3840]{1,0:T(8,128)(2,1)} %bitcast.6.own_ref), channel_id=1, source_target_pairs={{0,1},{1,0},{2,3},{3,2},{4,5},{5,4},{6,7},{7,6},{8,9},{9,8},{10,11... | collective-permute-start | bytes 11796488 | tf_op jit(solution)/shard_map/ppermute | solution.py:634
  130.6 58.0 %all-to-all-start.2 = ((bf16[64,8,3840]{2,1,0:T(8,128)(2,1)}), bf16[64,8,3840]{2,1,0:T(8,128)(2,1)}, u32[]{:S(2)}, u32[]{:S(2)}) async-start(bf16[64,8,3840]{2,1,0:T(8,128)(2,1)} %bitcast.15), calls=%async_computation.2 | async-start | bytes 7864320 | tf_op jit(solution)/shard_map/all_to_all | solution.py:629
  148.5 26.4 %collective-permute-start.4 = (f32[8,5120]{1,0:T(8,128)}, f32[8,5120]{1,0:T(8,128)}, u32[]{:S(2)}, u32[]{:S(2)}) collective-permute-start(f32[8,5120]{1,0:T(8,128)} %get-tuple-element.54.own_router), channel_id=1, source_target_pairs={{0,1},{1,0},{2,3},{3,2},{4,5},{5,4},{6,7},{7,6},{8,9},{9,8},{10,11... | collective-permute-start | bytes 491528 | tf_op jit(solution)/shard_map/ppermute | solution.py:634
  166.9 7.9 %collective-permute-start.3 = (bf16[384,5120]{1,0:T(8,128)(2,1)}, bf16[384,5120]{1,0:T(8,128)(2,1)}, u32[]{:S(2)}, u32[]{:S(2)}) collective-permute-start(bf16[384,5120]{1,0:T(8,128)(2,1)} %get-tuple-element.50), channel_id=1, source_target_pairs={{0,1},{1,0},{2,3},{3,2},{4,5},{5,4},{6,7},{7,6},{8,9},{9,8},{10,11... | collective-permute-start | bytes 11796488 | tf_op jit(solution)/shard_map/ppermute | solution.py:634
  188.6 10.0 %copy-start = (s32[128,2]{0,1:T(2,128)S(1)}, s32[128,2]{0,1:T(2,128)}, u32[]{:S(2)}) copy-start(s32[128,2]{0,1:T(2,128)} %param.14) | copy-start | bytes 3076
  188.6 59.8 %all-to-all-start.3 = ((bf16[64,8,3968]{2,1,0:T(8,128)(2,1)}), bf16[64,8,3968]{2,1,0:T(8,128)(2,1)}, u32[]{:S(2)}, u32[]{:S(2)}) async-start(bf16[64,8,3968]{2,1,0:T(8,128)(2,1)} %bitcast.12), calls=%async_computation.3 | async-start | bytes 8126464 | tf_op jit(solution)/shard_map/all_to_all | solution.py:629
  250.3 8.9 %collective-permute-start.5 = (f32[1,320]{1,0:T(1,128)}, f32[1,320]{1,0:T(1,128)S(1)}, u32[]{:S(2)}, u32[]{:S(2)}) collective-permute-start(f32[1,320]{1,0:T(1,128)} %get-tuple-element.57), channel_id=1, source_target_pairs={{0,1},{1,0},{2,3},{3,2},{4,5},{5,4},{6,7},{7,6},{8,9},{9,8},{10,11... | collective-permute-start | bytes 3848 | tf_op jit(solution)/shard_map/ppermute | solution.py:634
  253.0 6.2 %copy-start.1 = (f32[1,320]{1,0:T(1,128)S(1)}, f32[1,320]{1,0:T(1,128)}, u32[]{:S(2)}) copy-start(f32[1,320]{1,0:T(1,128)} %get-tuple-element.56) | copy-start | bytes 3844

commit v4 on v3

--- a/solution.py
+++ b/solution.py
@@ -190,80 +190,42 @@
     return pieces
 
 
-def mixed_kernel(ids_ref, tokens_ref, band0, band1, band2, out_ref, choose_ref, scale_ref, square_ref):
-    step = pl.program_id(0)
-    width = band0.shape[1]
-    features = tokens_ref.shape[1]
-    piece = features // PARTS
-
-    @pl.when(step == 0)
-    def _():
-        fill_choosing(ids_ref, choose_ref)
-        square_ref[...] = jnp.zeros_like(square_ref)
-
-    for number, value in enumerate(summed_pieces(choose_ref, (band0, band1, band2))):
-        cols = pl.ds(pl.multiple_of(number * piece + step * width, width), width)
-        x = tokens_ref[:, cols].astype(F32)
-        square_ref[...] += x * x
-        out_ref[:, cols] = (x + value).astype(BF16)
-
-    @pl.when(step == pl.num_programs(0) - 1)
-    def _():
-        scale = lax.rsqrt(jnp.sum(square_ref[...], axis=1, keepdims=True) / features + EPS)
-        scale_ref[...] = jnp.broadcast_to(scale, scale_ref.shape)
-
-
-def grad_tokens_kernel(
-    choose_ref, scale_ref, tokens_ref, cot_ref, band0, band1, band2, out_ref, grad_ref, cross_ref
-):
-    step = pl.program_id(0)
-    width = band0.shape[1]
-    features = tokens_ref.shape[1]
-    piece = features // PARTS
-
-    @pl.when(step == 0)
-    def _():
-        cross_ref[...] = jnp.zeros_like(cross_ref)
-
-    for number, value in enumerate(summed_pieces(choose_ref, (band0, band1, band2))):
-        cols = pl.ds(pl.multiple_of(number * piece + step * width, width), width)
-        grad_ref[:, cols] = value
-        cross_ref[...] += tokens_ref[:, cols].astype(F32) * value
-
-    @pl.when(step == pl.num_programs(0) - 1)
-    def _():
-        scale = scale_ref[:, 0:1]
-        back = jnp.sum(cross_ref[...], axis=1, keepdims=True) / features * scale * scale * scale
-        for at in range(0, features, width):
-            cols = slice(at, at + width)
-            x = tokens_ref[:, cols].astype(F32)
-            grad = scale * grad_ref[:, cols] - x * back
-            out_ref[:, cols] = (cot_ref[:, cols].astype(F32) + grad).astype(BF16)
-
-
-def token_side(kernel, whole_inputs, bands, out_shapes, scratch, name):
+def add_pieces(base_ref, choose_ref, band_refs, out_ref):
+    piece = base_ref.shape[1] // PARTS
+    for number, value in enumerate(summed_pieces(choose_ref, band_refs)):
+        cols = slice(number * piece, (number + 1) * piece)
+        out_ref[:, cols] = (base_ref[:, cols].astype(F32) + value).astype(BF16)
+
+
+def mixed_kernel(ids_ref, tokens_ref, band0, band1, band2, out_ref, choose_ref):
+    fill_choosing(ids_ref, choose_ref)
+    add_pieces(tokens_ref, choose_ref, (band0, band1, band2), out_ref)
+
+
+def grad_tokens_kernel(choose_ref, cot_ref, band0, band1, band2, out_ref):
+    add_pieces(cot_ref, choose_ref, (band0, band1, band2), out_ref)
+
+
+def token_side(kernel, inputs, bands, out_shapes, name):
     columns = bands.shape[0]
-    piece = whole_inputs[-1].shape[1] // PARTS
-    width = piece
-    steps = piece // width
+    piece = inputs[-1].shape[1] // PARTS
 
     def whole(shape):
         return pl.BlockSpec(shape, lambda c: (0,) * len(shape))
 
     def band_spec(band):
-        return pl.BlockSpec((columns, width), lambda c: (0, band * steps + c))
+        return pl.BlockSpec((columns, piece), lambda c: (0, band))
 
     return pl.pallas_call(
         kernel,
-        grid=(steps,),
-        in_specs=[whole(value.shape) for value in whole_inputs] + [band_spec(b) for b in range(BANDS)],
+        grid=(1,),
+        in_specs=[whole(value.shape) for value in inputs] + [band_spec(b) for b in range(BANDS)],
         out_specs=[whole(shape.shape) for shape in out_shapes],
         out_shape=out_shapes,
-        scratch_shapes=scratch,
         compiler_params=params(1),
         cost_estimate=cost(columns * columns * BANDS * piece, 2 * columns * BANDS * piece),
         name=name,
-    )(*whole_inputs, *([bands] * BANDS))
+    )(*inputs, *([bands] * BANDS))
 
 
 def sums_kernel(scale, meta_ref, core_ref, router_ref, own_ref, other_ref):
@@ -332,7 +294,7 @@
 
 def norm_kernel(
     own_ref, other_ref, own_meta, other_meta, core_ref, shuffle_ref,
-    own_normed, other_normed, own_gate, other_gate, gain_ref, column_ref,
+    own_normed, other_normed, own_gate, other_gate, scale_ref, gain_ref, column_ref,
 ):
     features = own_normed.shape[1]
     width = own_ref.shape[1] - META
@@ -359,6 +321,8 @@
             pieces = unpacked(block_ref[tiles, :width], shuffle_ref[...], width)
             square = sum(jnp.sum(x * x, axis=1, keepdims=True) for x in pieces)
             scale = lax.rsqrt(square / features + EPS)
+            if block_ref is own_ref:
+                spread(scale, scale_ref, rows)
             logit = 0.0
             for q, x in enumerate(pieces):
                 cols = slice(q * piece, (q + 1) * piece)
@@ -418,8 +382,8 @@
 
 
 def grad_kernel(
-    own_ref, other_ref, choice_ref, normed_ref, column_ref, gain_ref, own_router, other_router, core_ref,
-    back_ref, send_ref, sums_ref, meta_ref,
+    own_ref, other_ref, choice_ref, scale_ref, normed_ref, column_ref, gain_ref, own_router, other_router,
+    core_ref, back_ref, send_ref, sums_ref, meta_ref, inverse_ref,
 ):
     step = pl.program_id(0)
     features = own_ref.shape[1]
@@ -428,17 +392,28 @@
     @pl.when(step == 0)
     def _():
         sums_ref[...] = jnp.zeros_like(sums_ref)
+        inverse_ref[...] = 1.0 / gain_ref[...]
 
     for sub, (_, rows) in enumerate(group_slices()):
         choice = choice_ref[rows, 0:1]
-        scaled = []
+        scale = scale_ref[rows, 0:1]
+        total = 0.0
+        grads = []
         for q in range(PARTS):
             cols = slice(q * piece, (q + 1) * piece)
-            back = (own_ref[rows, cols].astype(F32) + other_ref[rows, cols].astype(F32)).astype(BF16)
-            grad = back.astype(F32) + choice * column_ref[:, cols]
-            sums_ref[:, cols] += row_fold(grad * normed_ref[rows, cols].astype(F32))
-            scaled.append((grad * gain_ref[:, cols]).astype(BF16))
-        bands = dot(back_ref[...], jnp.concatenate(scaled, axis=0)).astype(BF16)
+            grad = own_ref[rows, cols].astype(F32) + other_ref[rows, cols].astype(F32)
+            grad = grad + choice * column_ref[:, cols]
+            cross = grad * normed_ref[rows, cols].astype(F32)
+            sums_ref[:, cols] += row_fold(cross)
+            total = total + jnp.sum(cross, axis=1, keepdims=True)
+            grads.append(grad * gain_ref[:, cols])
+        mean = total / features
+        moved = []
+        for q, grad in enumerate(grads):
+            cols = slice(q * piece, (q + 1) * piece)
+            unit = normed_ref[rows, cols].astype(F32) * inverse_ref[:, cols]
+            moved.append((scale * (grad - mean * unit)).astype(BF16))
+        bands = dot(back_ref[...], jnp.concatenate(moved, axis=0)).astype(BF16)
         count = GROUP * TILE
         tiles = pl.ds(pl.multiple_of((step * SUB + sub) * count, count), count)
         for b in range(BANDS):
@@ -446,7 +421,7 @@
 
     @pl.when(step == pl.num_programs(0) - 1)
     def _():
-        gain_sum = jnp.sum(sums_ref[...], axis=0, keepdims=True) / gain_ref[...]
+        gain_sum = jnp.sum(sums_ref[...], axis=0, keepdims=True) * inverse_ref[...]
         router_sum = jnp.sum(own_router[...] + other_router[...], axis=0, keepdims=True)
         lower = core_ref[0, 0] == 0
 
@@ -658,7 +633,7 @@
     arrived, cot_sent = lax.optimization_barrier((arrived, cot_sent))
     arrived_other = swap(arrived)
     cot_arrived = exchange(cot_sent)
-    normed, normed_other, gate, gate_other, gain, column = by_group(
+    normed, normed_other, gate, gate_other, scale, gain, column = by_group(
         norm_kernel,
         [
             (arrived, group_tiles),
@@ -671,6 +646,7 @@
         [
             (row_shape, b16, group_rows),
             (row_shape, b16, group_rows),
+            (wide, f32, group_rows),
             (wide, f32, group_rows),
             (wide, f32, group_rows),
             (line, f32, 0),
@@ -726,6 +702,7 @@
             (own_grad, group_rows),
             (other_grad, group_rows),
             (choice, group_rows),
+            (scale, group_rows),
             (normed, group_rows),
             (column, 0),
             (gain, 0),
@@ -737,27 +714,16 @@
         [((tiles, width + META), b16, 0)],
         shuffling,
         "grad",
-        [pltpu.VMEM(fold, F32), pltpu.VMEM((pairs * TILE, META), F32)],
+        [pltpu.VMEM(fold, F32), pltpu.VMEM((pairs * TILE, META), F32), pltpu.VMEM(line, F32)],
     )
     grad_back = exchange(grad_sent)
     out_rows = jax.ShapeDtypeStruct((toks, features), BF16)
     choosing = jax.ShapeDtypeStruct((BANDS, 2 * toks, tiles), BF16)
-    partial = pltpu.VMEM((toks, features // PARTS), F32)
-    mixed, choose, scale = token_side(
-        mixed_kernel,
-        [expert_ids, tokens],
-        result_back,
-        [out_rows, choosing, jax.ShapeDtypeStruct((toks, 128), F32)],
-        [partial],
-        "mixed",
+    mixed, choose = token_side(
+        mixed_kernel, [expert_ids, tokens], result_back, [out_rows, choosing], "mixed"
     )
     (grad_tokens,) = token_side(
-        grad_tokens_kernel,
-        [choose, scale, tokens, cotangent],
-        grad_back,
-        [out_rows],
-        [pltpu.VMEM((toks, features), F32), partial],
-        "grad_tokens",
+        grad_tokens_kernel, [choose, cotangent], grad_back, [out_rows], "grad_tokens"
     )
     grad_router, own_gain, other_gain = summed(grad_back, core, shard, 1.0 / math.sqrt(toks * devices))
     grad_gain = (own_gain + swap(other_gain)).reshape(shard)

time: 263 us -> 261 us (level)
  no operation moved by 1% of the time
where the time goes in v4:
time: 261 us; the launch traced here: 259 us
  Pallas kernels  111 us (43%)
  waiting for transfers between devices  97.7 us (37%)
  starting transfers between devices  47.7 us (18%)
    all_to_all x4, waiting for transfers between devices, exchange(): lax.all_to_all(blocks, CHIPS, split_axis=0, concat_axis=0, tiled=True)  97.7 us
    all_to_all x4, starting transfers between devices, exchange(): lax.all_to_all(blocks, CHIPS, split_axis=0, concat_axis=0, tiled=True)  39.6 us
    pallas_call x4, Pallas kernels, by_group(): pl.pallas_call(kernel, grid=(steps,), in_specs=[spec(value.shape, rows) f...  37.6 us
    pallas_call x2, Pallas kernels, expert_call(): pl.pallas_call(kernel, grid=(2 * half,), in_specs=in_specs, out_specs=out...  37.2 us
    pallas_call x2, Pallas kernels, last_call(): pl.pallas_call(functools.partial(last_kernel, product=product), grid=(PAR...  15.2 us
    pallas_call x2, Pallas kernels, token_side(): pl.pallas_call(kernel, grid=(1,), in_specs=[whole(value.shape) for value...  10.2 us
    pallas_call x2, Pallas kernels, pack(): pl.pallas_call(functools.partial(pack_kernel, experts), grid=(steps,), in...  8.99 us
    ppermute x6, starting transfers between devices, swap(): return lax.ppermute(value, 'core', [(0, 1), (1, 0)])  8.11 us
  transfers between devices with their start and end apart: 10, of which 4 were waited for; matrix products, arithmetic and copies ran while one was open for 0% of the time, Pallas kernels for 40%

profile of v4, /device:TPU:1, one launch (start us, length us, event | category | flops | bytes accessed | tf_op | source)
XLA Modules:
  0.0 258.6 jit_solution(17629771783710947014)
XLA Ops:
  0.6 4.8 %pack.2 = bf16[512,3968]{1,0:T(8,128)(2,1)} custom-call(s32[2,128]{1,0:T(2,128)} %bitcast.17, bf16[128,5120]{1,0:T(8,128)(2,1)} %tokens_ref.1, bf16[320]{0:T(512)(128)(2,1)} %refs_0_.1, bf16[64,320]{1,0:T(8,128)(2,1)} %bitcast.16, s32[1,1]{1,0:T(1,128)} %bitcast.2.refs_2_.core_ref), custom_call_target="tpu_custom_call" | custom-call | flops 1040187392 | bytes 4063232 | tf_op jit(solution)/shard_map/pack/pallas_call | solution.py:143
  5.4 12.2 %all-to-all-start = ((bf16[64,8,3968]{2,1,0:T(8,128)(2,1)}), bf16[64,8,3968]{2,1,0:T(8,128)(2,1)}, u32[]{:S(2)}, u32[]{:S(2)}) async-start(bf16[64,8,3968]{2,1,0:T(8,128)(2,1)} %bitcast.13), calls=%async_computation | async-start | bytes 8126464 | tf_op jit(solution)/shard_map/all_to_all | solution.py:604
  17.6 4.2 %pack.3 = bf16[512,3840]{1,0:T(8,128)(2,1)} custom-call(s32[2,128]{1,0:T(2,128)} %bitcast.18, bf16[128,5120]{1,0:T(8,128)(2,1)} %cot_ref.1), custom_call_target="tpu_custom_call" | custom-call | flops 1006632960 | bytes 3932160 | tf_op jit(solution)/shard_map/pack/pallas_call | solution.py:143
  21.8 46.1 %all-to-all-done = bf16[64,8,3968]{2,1,0:T(8,128)(2,1)} async-done(((bf16[64,8,3968]{2,1,0:T(8,128)(2,1)}), bf16[64,8,3968]{2,1,0:T(8,128)(2,1)}, u32[]{:S(2)}, u32[]{:S(2)}) %all-to-all-start) | async-done | bytes 4063264 | tf_op jit(solution)/shard_map/all_to_all | solution.py:604
  67.9 2.5 collective-permute-start
  70.4 8.8 %all-to-all-start.1 = ((bf16[64,8,3840]{2,1,0:T(8,128)(2,1)}), bf16[64,8,3840]{2,1,0:T(8,128)(2,1)}, u32[]{:S(2)}, u32[]{:S(2)}) async-start(bf16[64,8,3840]{2,1,0:T(8,128)(2,1)} %bitcast.14), calls=%async_computation.1 | async-start | bytes 7864320 | tf_op jit(solution)/shard_map/all_to_all | solution.py:604
  79.2 0.0 collective-permute-done.other_ref.other_meta
  79.2 10.7 %norm.1 = (bf16[384,5120]{1,0:T(8,128)(2,1)}, bf16[384,5120]{1,0:T(8,128)(2,1)}, f32[384,128]{1,0:T(8,128)}, f32[384,128]{1,0:T(8,128)}, f32[384,128]{1,0:T(8,12...) custom-call(bf16[512,3968]{1,0:T(8,128)(2,1)} %bitcast.4.own_ref.own_meta, ...), custom_call_target="tpu_custom_call" | custom-call | flops 377487360 | bytes 24821764 | tf_op jit(solution)/shard_map/norm/pallas_call | solution.py:460
  89.9 19.1 %forward.1 = (bf16[384,5120]{1,0:T(8,128)(2,1)}, bf16[384,768]{1,0:T(8,128)(2,1)}, f32[768,768]{1,0:T(8,128)}) custom-call(bf16[384,5120]{1,0:T(8,128)(2,1)} %get-tuple-element.33.own_ref.normed_ref, bf16[384,5120]{1,0:T(8,128)(2,1)} %get-tuple-element.34.other_ref, bf16[1,5120,768]{2,1,0:T(8,128)(2,1)} %weight_ref.3, bf16[1,768,5120]{2,1,0:T(8,128)(2,1)} %down_ref.3), custom_call_target="tpu_custom_call" | custom-call | flops 9059696640 | bytes 31457280 | tf_op jit(solution)/shard_map/forward/pallas_call | solution.py:565
  108.9 0.3 collective-permute-start.1
  109.2 7.6 %forward_own.1.own_ref = bf16[384,5120]{1,0:T(8,128)(2,1)} custom-call(bf16[384,768]{1,0:T(8,128)(2,1)} %get-tuple-element.35.x_ref, bf16[1,768,5120]{2,1,0:T(8,128)(2,1)} %down_ref.3), custom_call_target="tpu_custom_call" | custom-call | flops 193273528320 | bytes 754974720 | tf_op jit(solution)/shard_map/forward_own/pallas_call | solution.py:590
  116.8 0.0 collective-permute-done.1.other_ref
  116.8 7.1 %out.1 = (bf16[384,5120]{1,0:T(8,128)(2,1)}, bf16[512,3840]{1,0:T(8,128)(2,1)}) custom-call(bf16[384,5120]{1,0:T(8,128)(2,1)} %forward_own.1.own_ref, bf16[384,5120]{1,0:T(8,128)(2,1)} %collective-permute-done.1.other_ref, f32[384,128]{1,0:T(8,128)} %get-tuple-element.37.gate_ref.own_gate, bf16[192,192]{1,0:T(8,128)(2,1)} %constant.9.clone.back_ref), custom_call_target="tpu_custom_call" | custom-call | flops 188743680 | bytes 15998976 | tf_op jit(solution)/shard_map/out/pallas_call | solution.py:460
  123.9 4.6 %all-to-all-done.1 = bf16[64,8,3840]{2,1,0:T(8,128)(2,1)} async-done(((bf16[64,8,3840]{2,1,0:T(8,128)(2,1)}), bf16[64,8,3840]{2,1,0:T(8,128)(2,1)}, u32[]{:S(2)}, u32[]{:S(2)}) %all-to-all-start.1) | async-done | bytes 3932192 | tf_op jit(solution)/shard_map/all_to_all | solution.py:604
  128.5 2.1 collective-permute-start.2
  130.6 8.6 %all-to-all-start.2 = ((bf16[64,8,3840]{2,1,0:T(8,128)(2,1)}), bf16[64,8,3840]{2,1,0:T(8,128)(2,1)}, u32[]{:S(2)}, u32[]{:S(2)}) async-start(bf16[64,8,3840]{2,1,0:T(8,128)(2,1)} %bitcast.15), calls=%async_computation.2 | async-start | bytes 7864320 | tf_op jit(solution)/shard_map/all_to_all | solution.py:604
  139.2 0.0 collective-permute-done.2.other_ref
  139.2 9.3 %cot.1 = (bf16[384,5120]{1,0:T(8,128)(2,1)}, bf16[384,5120]{1,0:T(8,128)(2,1)}, f32[384,128]{1,0:T(8,128)}, f32[8,5120]{1,0:T(8,128)}) custom-call(bf16[512,3840]{1,0:T(8,128)(2,1)} %bitcast.6.own_ref, bf16[512,3840]{1,0:T(8,128)(2,1)} %collective-permute-done.2.other_ref, f32[384,128]{1,0:T(8,128)} %get-tuple-element.37.gate_ref.own_gate, ...), custom_call_target="tpu_custom_call" | custom-call | flops 377487360 | bytes 24420352 | tf_op jit(solution)/shard_map/cot/pallas_call | solution.py:460
  148.5 0.4 collective-permute-start.4
  148.9 18.1 %backward.1 = (bf16[384,5120]{1,0:T(8,128)(2,1)}, bf16[384,768]{1,0:T(8,128)(2,1)}) custom-call(bf16[384,5120]{1,0:T(8,128)(2,1)} %get-tuple-element.45.own_ref, bf16[384,5120]{1,0:T(8,128)(2,1)} %get-tuple-element.46.other_ref, bf16[1,768,5120]{2,1,0:T(8,128)(2,1)} %down_ref.3, bf16[1,5120,768]{2,1,0:T(8,128)(2,1)} %weight_ref.3, ...), custom_call_target="tpu_custom_call" | custom-call | flops 9059696640 | bytes 31457280 | tf_op jit(solution)/shard_map/backward/pallas_call | solution.py:565
  167.0 0.2 collective-permute-start.3
  167.2 7.6 %backward_own.1.own_ref = bf16[384,5120]{1,0:T(8,128)(2,1)} custom-call(bf16[384,768]{1,0:T(8,128)(2,1)} %get-tuple-element.48.x_ref, bf16[1,5120,768]{2,1,0:T(8,128)(2,1)} %weight_ref.3), custom_call_target="tpu_custom_call" | custom-call | flops 193273528320 | bytes 754974720 | tf_op jit(solution)/shard_map/backward_own/pallas_call | solution.py:590
  174.8 0.0 collective-permute-done.4.other_router
  174.8 0.0 collective-permute-done.3.other_ref
  174.8 10.5 %grad.1 = bf16[512,3968]{1,0:T(8,128)(2,1)} custom-call(bf16[384,5120]{1,0:T(8,128)(2,1)} %backward_own.1.own_ref, bf16[384,5120]{1,0:T(8,128)(2,1)} %collective-permute-done.3.other_ref, f32[384,128]{1,0:T(8,128)} %get-tuple-element.50.choice_ref, f32[384,128]{1,0:T(8,128)} %get-tuple-element.51.scale_ref, ...), custom_call_target="tpu_custom_call" | custom-call | flops 188743680 | bytes 16695300 | tf_op jit(solution)/shard_map/grad/pallas_call | solution.py:460
  185.4 3.2 %all-to-all-done.2 = bf16[64,8,3840]{2,1,0:T(8,128)(2,1)} async-done(((bf16[64,8,3840]{2,1,0:T(8,128)(2,1)}), bf16[64,8,3840]{2,1,0:T(8,128)(2,1)}, u32[]{:S(2)}, u32[]{:S(2)}) %all-to-all-start.2) | async-done | bytes 3932192 | tf_op jit(solution)/shard_map/all_to_all | solution.py:604
  188.6 0.0 copy-start
  188.6 10.0 %all-to-all-start.3 = ((bf16[64,8,3968]{2,1,0:T(8,128)(2,1)}), bf16[64,8,3968]{2,1,0:T(8,128)(2,1)}, u32[]{:S(2)}, u32[]{:S(2)}) async-start(bf16[64,8,3968]{2,1,0:T(8,128)(2,1)} %bitcast.12), calls=%async_computation.3 | async-start | bytes 8126464 | tf_op jit(solution)/shard_map/all_to_all | solution.py:604
  198.6 0.0 copy-done
  198.6 0.7 copy.13.ids_ref
  199.4 5.2 %mixed.1 = (bf16[128,5120]{1,0:T(8,128)(2,1)}, bf16[3,256,512]{2,1,0:T(8,128)(2,1)}) custom-call(s32[128,2]{1,0:T(8,128)} %copy.13.ids_ref, bf16[128,5120]{1,0:T(8,128)(2,1)} %tokens_ref.1, bf16[512,3840]{1,0:T(8,128)(2,1)} %bitcast.8.band0.band1.band2, bf16[512,3840]{1,0:T(8,128)(2,1)} %bitcast.8.band0.band1.band2, bf16[512,3840]{1,0:T(8,128)(2,1)} %bitcast.8.band0.band1.band2), custom_call_target="tpu_custom_call" | custom-call | flops 1006632960 | bytes 3932160 | tf_op jit(solution)/shard_map/mixed/pallas_call | solution.py:219
  204.6 43.8 %all-to-all-done.3 = bf16[64,8,3968]{2,1,0:T(8,128)(2,1)} async-done(((bf16[64,8,3968]{2,1,0:T(8,128)(2,1)}), bf16[64,8,3968]{2,1,0:T(8,128)(2,1)}, u32[]{:S(2)}, u32[]{:S(2)}) %all-to-all-start.3) | async-done | bytes 4063264 | tf_op jit(solution)/shard_map/all_to_all | solution.py:604
  248.4 1.9 sums.1
  250.3 2.7 %collective-permute-start.5 = (f32[1,320]{1,0:T(1,128)}, f32[1,320]{1,0:T(1,128)S(1)}, u32[]{:S(2)}, u32[]{:S(2)}) collective-permute-start(f32[1,320]{1,0:T(1,128)} %get-tuple-element.57), channel_id=1, source_target_pairs={{0,1},{1,0},{2,3},{3,2},{4,5},{5,4},{6,7},{7,6},{8,9},{9,8},{10,11... | collective-permute-start | bytes 3848 | tf_op jit(solution)/shard_map/ppermute | solution.py:609
  253.0 0.0 copy-start.1
  253.0 5.0 %grad_tokens.1 = bf16[128,5120]{1,0:T(8,128)(2,1)} custom-call(bf16[3,256,512]{2,1,0:T(8,128)(2,1)} %get-tuple-element.41.choose_ref, bf16[128,5120]{1,0:T(8,128)(2,1)} %cot_ref.1, bf16[512,3968]{1,0:T(8,128)(2,1)} %bitcast.10.band0.band1.band2.meta_ref, bf16[512,3968]{1,0:T(8,128)(2,1)} %bitcast.10.band0.band1.band2.meta_ref, ...), custom_call_target="tpu_custom_call" | custom-call | flops 1006632960 | bytes 3932160 | tf_op jit(solution)/shard_map/grad_tokens/pallas_call | solution.py:219
  258.0 0.0 collective-permute-done.5
  258.0 0.0 copy-done.1
  258.0 0.6 add_reduce_fusion
Async XLA Ops:
  5.4 62.5 %all-to-all-start = ((bf16[64,8,3968]{2,1,0:T(8,128)(2,1)}), bf16[64,8,3968]{2,1,0:T(8,128)(2,1)}, u32[]{:S(2)}, u32[]{:S(2)}) async-start(bf16[64,8,3968]{2,1,0:T(8,128)(2,1)} %bitcast.13), calls=%async_computation | async-start | bytes 8126464 | tf_op jit(solution)/shard_map/all_to_all | solution.py:604
  67.9 11.3 %collective-permute-start = (bf16[512,3968]{1,0:T(8,128)(2,1)}, bf16[512,3968]{1,0:T(8,128)(2,1)}, u32[]{:S(2)}, u32[]{:S(2)}) collective-permute-start(bf16[512,3968]{1,0:T(8,128)(2,1)} %bitcast.4.own_ref.own_meta), channel_id=1, source_target_pairs={{0,1},{1,0},{2,3},{3,2},{4,5},{5,4},{6,7},{7,6},{8,9},{9,8},{10,11... | collective-permute-start | bytes 12189704 | tf_op jit(solution)/shard_map/ppermute | solution.py:609
  70.4 58.1 %all-to-all-start.1 = ((bf16[64,8,3840]{2,1,0:T(8,128)(2,1)}), bf16[64,8,3840]{2,1,0:T(8,128)(2,1)}, u32[]{:S(2)}, u32[]{:S(2)}) async-start(bf16[64,8,3840]{2,1,0:T(8,128)(2,1)} %bitcast.14), calls=%async_computation.1 | async-start | bytes 7864320 | tf_op jit(solution)/shard_map/all_to_all | solution.py:604
  108.9 7.9 %collective-permute-start.1 = (bf16[384,5120]{1,0:T(8,128)(2,1)}, bf16[384,5120]{1,0:T(8,128)(2,1)}, u32[]{:S(2)}, u32[]{:S(2)}) collective-permute-start(bf16[384,5120]{1,0:T(8,128)(2,1)} %get-tuple-element.36), channel_id=1, source_target_pairs={{0,1},{1,0},{2,3},{3,2},{4,5},{5,4},{6,7},{7,6},{8,9},{9,8},{10,11... | collective-permute-start | bytes 11796488 | tf_op jit(solution)/shard_map/ppermute | solution.py:609
  128.5 10.7 %collective-permute-start.2 = (bf16[512,3840]{1,0:T(8,128)(2,1)}, bf16[512,3840]{1,0:T(8,128)(2,1)}, u32[]{:S(2)}, u32[]{:S(2)}) collective-permute-start(bf16[512,3840]{1,0:T(8,128)(2,1)} %bitcast.6.own_ref), channel_id=1, source_target_pairs={{0,1},{1,0},{2,3},{3,2},{4,5},{5,4},{6,7},{7,6},{8,9},{9,8},{10,11... | collective-permute-start | bytes 11796488 | tf_op jit(solution)/shard_map/ppermute | solution.py:609
  130.6 58.0 %all-to-all-start.2 = ((bf16[64,8,3840]{2,1,0:T(8,128)(2,1)}), bf16[64,8,3840]{2,1,0:T(8,128)(2,1)}, u32[]{:S(2)}, u32[]{:S(2)}) async-start(bf16[64,8,3840]{2,1,0:T(8,128)(2,1)} %bitcast.15), calls=%async_computation.2 | async-start | bytes 7864320 | tf_op jit(solution)/shard_map/all_to_all | solution.py:604
  148.5 26.3 %collective-permute-start.4 = (f32[8,5120]{1,0:T(8,128)}, f32[8,5120]{1,0:T(8,128)}, u32[]{:S(2)}, u32[]{:S(2)}) collective-permute-start(f32[8,5120]{1,0:T(8,128)} %get-tuple-element.54.own_router), channel_id=1, source_target_pairs={{0,1},{1,0},{2,3},{3,2},{4,5},{5,4},{6,7},{7,6},{8,9},{9,8},{10,11... | collective-permute-start | bytes 491528 | tf_op jit(solution)/shard_map/ppermute | solution.py:609
  167.0 7.8 %collective-permute-start.3 = (bf16[384,5120]{1,0:T(8,128)(2,1)}, bf16[384,5120]{1,0:T(8,128)(2,1)}, u32[]{:S(2)}, u32[]{:S(2)}) collective-permute-start(bf16[384,5120]{1,0:T(8,128)(2,1)} %get-tuple-element.49), channel_id=1, source_target_pairs={{0,1},{1,0},{2,3},{3,2},{4,5},{5,4},{6,7},{7,6},{8,9},{9,8},{10,11... | collective-permute-start | bytes 11796488 | tf_op jit(solution)/shard_map/ppermute | solution.py:609
  188.6 10.0 %copy-start = (s32[128,2]{0,1:T(2,128)S(1)}, s32[128,2]{0,1:T(2,128)}, u32[]{:S(2)}) copy-start(s32[128,2]{0,1:T(2,128)} %param.14) | copy-start | bytes 3076
  188.6 59.8 %all-to-all-start.3 = ((bf16[64,8,3968]{2,1,0:T(8,128)(2,1)}), bf16[64,8,3968]{2,1,0:T(8,128)(2,1)}, u32[]{:S(2)}, u32[]{:S(2)}) async-start(bf16[64,8,3968]{2,1,0:T(8,128)(2,1)} %bitcast.12), calls=%async_computation.3 | async-start | bytes 8126464 | tf_op jit(solution)/shard_map/all_to_all | solution.py:604
  250.3 7.7 %collective-permute-start.5 = (f32[1,320]{1,0:T(1,128)}, f32[1,320]{1,0:T(1,128)S(1)}, u32[]{:S(2)}, u32[]{:S(2)}) collective-permute-start(f32[1,320]{1,0:T(1,128)} %get-tuple-element.57), channel_id=1, source_target_pairs={{0,1},{1,0},{2,3},{3,2},{4,5},{5,4},{6,7},{7,6},{8,9},{9,8},{10,11... | collective-permute-start | bytes 3848 | tf_op jit(solution)/shard_map/ppermute | solution.py:609
  253.0 5.0 %copy-start.1 = (f32[1,320]{1,0:T(1,128)S(1)}, f32[1,320]{1,0:T(1,128)}, u32[]{:S(2)}) copy-start(f32[1,320]{1,0:T(1,128)} %get-tuple-element.56) | copy-start | bytes 3844

commit v5 on v4

--- a/solution.py
+++ b/solution.py
@@ -23,7 +23,7 @@
 META = 128
 SUB = 4
 VMEM_LIMIT = 56 * 1024 * 1024
-CHIPS = ("ep", "pair")
+CHIPS = ("pair", "ep")
 FSDP = ("pair", "core")
 EVERY = ("ep", "pair", "core")
 
@@ -48,6 +48,10 @@
 
 def dot_nt(a, b):
     return lax.dot_general(a, b, (((1,), (1,)), ((), ())), preferred_element_type=F32)
+
+
+def message_of(expert, eps, pairs):
+    return expert % pairs * eps + expert // pairs
 
 
 def as_bf16(mask):
@@ -76,16 +80,17 @@
     return (column >> 3) * CAP + slot, low
 
 
-def pack_kernel(experts, ids_ref, rows_ref, *refs):
+def pack_kernel(eps, pairs, ids_ref, rows_ref, *refs):
     *meta_refs, out_ref, pos_ref = refs
     step = pl.program_id(0)
     toks, features = rows_ref.shape
     count = out_ref.shape[0]
     piece = features // PARTS
+    experts = eps * pairs
 
     @pl.when(step == 0)
     def _():
-        first, second = ids_ref[0:1, :], ids_ref[1:2, :]
+        first, second = (message_of(ids_ref[k : k + 1, :], eps, pairs) for k in range(2))
         expert = iota((experts, toks), 0)
         in_first, in_second = expert == first, expert == second
         both = as_bf16(in_first | in_second)
@@ -115,7 +120,7 @@
         columns = dot(router_ref[...], shifted).astype(BF16)
         tile_row = iota((count, META), 0) & (TILE - 1)
         pick_row = step * count + iota((count, experts), 0)
-        pick_column = iota((count, experts), 1)
+        pick_column = message_of(iota((count, experts), 1), eps, pairs)
         total = jnp.zeros((count, META), F32)
         for r in range(3):
             lanes = slice(r * META, (r + 1) * META)
@@ -127,10 +132,10 @@
 SMALL = pl.BlockSpec(memory_space=pltpu.SMEM)
 
 
-def pack(ids_t, rows, experts, meta=()):
+def pack(ids_t, rows, eps, pairs, meta=()):
     toks, features = rows.shape
     width = features * CAP // TILE + (META if meta else 0)
-    out_rows = experts * TILE
+    out_rows = eps * pairs * TILE
     steps = PACK_STEPS
     meta_specs = []
     if meta:
@@ -141,7 +146,7 @@
             SMALL,
         ]
     return pl.pallas_call(
-        functools.partial(pack_kernel, experts),
+        functools.partial(pack_kernel, eps, pairs),
         grid=(steps,),
         in_specs=[
             pl.BlockSpec((2, toks), lambda i: (0, 0)),
@@ -157,11 +162,11 @@
     )(ids_t, rows, *meta)
 
 
-def fill_choosing(ids_ref, choose_ref):
+def fill_choosing(eps, pairs, ids_ref, choose_ref):
     toks = ids_ref.shape[0]
     columns = choose_ref.shape[2]
-    experts = columns // TILE
-    first, second = ids_ref[:, 0:1], ids_ref[:, 1:2]
+    experts = eps * pairs
+    first, second = (message_of(ids_ref[:, k : k + 1], eps, pairs) for k in range(2))
     expert = iota((toks, experts), 1)
     in_first, in_second = expert == first, expert == second
     both = as_bf16(in_first | in_second)
@@ -197,8 +202,8 @@
         out_ref[:, cols] = (base_ref[:, cols].astype(F32) + value).astype(BF16)
 
 
-def mixed_kernel(ids_ref, tokens_ref, band0, band1, band2, out_ref, choose_ref):
-    fill_choosing(ids_ref, choose_ref)
+def mixed_kernel(eps, pairs, ids_ref, tokens_ref, band0, band1, band2, out_ref, choose_ref):
+    fill_choosing(eps, pairs, ids_ref, choose_ref)
     add_pieces(tokens_ref, choose_ref, (band0, band1, band2), out_ref)
 
 
@@ -228,15 +233,13 @@
     )(*inputs, *([bands] * BANDS))
 
 
-def sums_kernel(scale, meta_ref, core_ref, router_ref, own_ref, other_ref):
+def sums_kernel(scale, eps, pairs, meta_ref, core_ref, router_ref, own_ref, other_ref):
     messages = meta_ref[...]
     tiles = messages.shape[0]
     experts, shard = router_ref.shape
     lower = core_ref[0, 0] == 0
-    rows = [
-        dot(as_bf16(iota((experts, tiles), 1) == iota((experts, tiles), 0) * TILE + 5 + r), messages)
-        for r in range(3)
-    ]
+    start = message_of(iota((experts, tiles), 0), eps, pairs) * TILE
+    rows = [dot(as_bf16(iota((experts, tiles), 1) == start + 5 + r), messages) for r in range(3)]
     router = jnp.concatenate(rows, axis=1) * scale
     router_ref[...] = jnp.where(lower, router[:, :shard], router[:, META // 2 : META // 2 + shard])
     total = dot(as_bf16((iota((TILE, tiles), 1) & (TILE - 1)) == iota((TILE, tiles), 0)), messages)
@@ -246,11 +249,11 @@
     other_ref[...] = jnp.where(lower, second, first)
 
 
-def summed(messages, core, shard, scale):
+def summed(messages, core, eps, pairs, shard, scale):
     tiles, width = messages.shape
     row = jax.ShapeDtypeStruct((1, shard), F32)
     return pl.pallas_call(
-        functools.partial(sums_kernel, scale),
+        functools.partial(sums_kernel, scale, eps, pairs),
         grid=(1,),
         in_specs=[pl.BlockSpec((tiles, META), lambda i: (0, width // META - 1)), SMALL],
         out_specs=[
@@ -306,8 +309,9 @@
         lower = core_ref[0, 0] == 0
         first, second = jnp.where(lower, own, other), jnp.where(lower, other, own)
         for part, ref in ((0, gain_ref), (3, column_ref)):
-            for pair in range(features // (5 * META)):
-                at = pair * TILE + part
+            pairs = features // (5 * META)
+            for pair in range(pairs):
+                at = pair * (own.shape[0] // pairs) + part
                 rows = [first[at + r : at + r + 1] for r in range(3)]
                 rows += [second[at + r : at + r + 1] for r in range(3)]
                 rows = [rows[0], rows[1], rows[2] + rows[3], rows[4], rows[5]]
@@ -437,9 +441,11 @@
                 meta_ref[pair * TILE + 5 + r : pair * TILE + 6 + r, :] = jnp.where(
                     lower, lanes(router_sum, at), lanes(router_sum, at + 2)
                 )
-        meta = meta_ref[...].astype(BF16)
-        for at in range(0, send_ref.shape[0], pairs * TILE):
-            send_ref[at : at + pairs * TILE, BANDS * piece :] = meta
+        count = send_ref.shape[0] // pairs
+        for pair in range(pairs):
+            meta = meta_ref[pair * TILE : (pair + 1) * TILE]
+            meta = jnp.concatenate([meta] * (count // TILE), axis=0).astype(BF16)
+            send_ref[pair * count : (pair + 1) * count, BANDS * piece :] = meta
 
 
 def by_group(kernel, inputs, outputs, flops, name, scratch=()):
@@ -626,10 +632,10 @@
     wide, line, fold = (rows, 128), (1, features), (8, features)
     shuffling = 2 * rows * features * CAP * PARTS * GROUP // PARTS
     b16, f32 = jnp.dtype(BF16), jnp.dtype(F32)
-    meta_spec = pl.BlockSpec((pairs * TILE, META), lambda g: (0, width // META))
-
-    cot_sent = pack(ids_t, cotangent, experts)
-    arrived = exchange(pack(ids_t, tokens, experts, (norm_gain, router_weight.T, core)))
+    meta_spec = pl.BlockSpec((tiles, META), lambda g: (0, width // META))
+
+    cot_sent = pack(ids_t, cotangent, eps, pairs)
+    arrived = exchange(pack(ids_t, tokens, eps, pairs, (norm_gain, router_weight.T, core)))
     arrived, cot_sent = lax.optimization_barrier((arrived, cot_sent))
     arrived_other = swap(arrived)
     cot_arrived = exchange(cot_sent)
@@ -720,12 +726,16 @@
     out_rows = jax.ShapeDtypeStruct((toks, features), BF16)
     choosing = jax.ShapeDtypeStruct((BANDS, 2 * toks, tiles), BF16)
     mixed, choose = token_side(
-        mixed_kernel, [expert_ids, tokens], result_back, [out_rows, choosing], "mixed"
+        functools.partial(mixed_kernel, eps, pairs),
+        [expert_ids, tokens],
+        result_back,
+        [out_rows, choosing],
+        "mixed",
     )
     (grad_tokens,) = token_side(
         grad_tokens_kernel, [choose, cotangent], grad_back, [out_rows], "grad_tokens"
     )
-    grad_router, own_gain, other_gain = summed(grad_back, core, shard, 1.0 / math.sqrt(toks * devices))
+    grad_router, own_gain, other_gain = summed(grad_back, core, eps, pairs, shard, 1.0 / math.sqrt(toks * devices))
     grad_gain = (own_gain + swap(other_gain)).reshape(shard)
     grad_router = grad_router.T
     return mixed, grad_tokens, grad_router, grad_gain

time: 261 us -> 256 us (0.981)
  starting transfers between devices: 47.7 us -> 42.6 us
    all_to_all x4, starting transfers between devices: 39.6 us -> 34.5 us  [exchange(): lax.all_to_all(blocks, CHIPS, split_axis=0, concat_axis=0, tiled=True)]
  transfers between devices with their start and end apart: 10 -> 10, of which waited for: 4 -> 4; matrix products, arithmetic and copies ran while one was open for 0% -> 0% of each run, Pallas kernels for 40% -> 41%
where the time goes in v5:
time: 256 us; the launch traced here: 255 us
  Pallas kernels  111 us (43%)
  waiting for transfers between devices  98.9 us (39%)
  starting transfers between devices  42.6 us (17%)
    all_to_all x4, waiting for transfers between devices, exchange(): lax.all_to_all(blocks, CHIPS, split_axis=0, concat_axis=0, tiled=True)  98.9 us
    pallas_call x4, Pallas kernels, by_group(): pl.pallas_call(kernel, grid=(steps,), in_specs=[spec(value.shape, rows) f...  37.6 us
    pallas_call x2, Pallas kernels, expert_call(): pl.pallas_call(kernel, grid=(2 * half,), in_specs=in_specs, out_specs=out...  37.2 us
    all_to_all x4, starting transfers between devices, exchange(): lax.all_to_all(blocks, CHIPS, split_axis=0, concat_axis=0, tiled=True)  34.5 us
    pallas_call x2, Pallas kernels, last_call(): pl.pallas_call(functools.partial(last_kernel, product=product), grid=(PAR...  15.2 us
    pallas_call x2, Pallas kernels, token_side(): pl.pallas_call(kernel, grid=(1,), in_specs=[whole(value.shape) for value...  10.3 us
    pallas_call x2, Pallas kernels, pack(): pl.pallas_call(functools.partial(pack_kernel, eps, pairs), grid=(steps,),...  8.99 us
    ppermute x6, starting transfers between devices, swap(): return lax.ppermute(value, 'core', [(0, 1), (1, 0)])  8.19 us
  transfers between devices with their start and end apart: 10, of which 4 were waited for; matrix products, arithmetic and copies ran while one was open for 0% of the time, Pallas kernels for 41%

profile of v5, /device:TPU:1, one launch (start us, length us, event | category | flops | bytes accessed | tf_op | source)
XLA Modules:
  0.0 254.7 jit_solution(431643984552957945)
XLA Ops:
  0.6 4.8 %pack.2 = bf16[512,3968]{1,0:T(8,128)(2,1)} custom-call(s32[2,128]{1,0:T(2,128)} %bitcast.17, bf16[128,5120]{1,0:T(8,128)(2,1)} %tokens_ref.1, bf16[320]{0:T(512)(128)(2,1)} %refs_0_.1, bf16[64,320]{1,0:T(8,128)(2,1)} %bitcast.16, s32[1,1]{1,0:T(1,128)} %bitcast.2.refs_2_.core_ref), custom_call_target="tpu_custom_call" | custom-call | flops 1040187392 | bytes 4063232 | tf_op jit(solution)/shard_map/pack/pallas_call | solution.py:148
  5.4 12.2 %all-to-all-start = ((bf16[64,8,3968]{2,1,0:T(8,128)(2,1)}), bf16[64,8,3968]{2,1,0:T(8,128)(2,1)}, u32[]{:S(2)}, u32[]{:S(2)}) async-start(bf16[64,8,3968]{2,1,0:T(8,128)(2,1)} %bitcast.13), calls=%async_computation | async-start | bytes 8126464 | tf_op jit(solution)/shard_map/all_to_all | solution.py:610
  17.6 4.2 %pack.3 = bf16[512,3840]{1,0:T(8,128)(2,1)} custom-call(s32[2,128]{1,0:T(2,128)} %bitcast.18, bf16[128,5120]{1,0:T(8,128)(2,1)} %cot_ref.1), custom_call_target="tpu_custom_call" | custom-call | flops 1006632960 | bytes 3932160 | tf_op jit(solution)/shard_map/pack/pallas_call | solution.py:148
  21.8 46.0 %all-to-all-done = bf16[64,8,3968]{2,1,0:T(8,128)(2,1)} async-done(((bf16[64,8,3968]{2,1,0:T(8,128)(2,1)}), bf16[64,8,3968]{2,1,0:T(8,128)(2,1)}, u32[]{:S(2)}, u32[]{:S(2)}) %all-to-all-start) | async-done | bytes 4063264 | tf_op jit(solution)/shard_map/all_to_all | solution.py:610
  67.8 2.8 %collective-permute-start = (bf16[512,3968]{1,0:T(8,128)(2,1)}, bf16[512,3968]{1,0:T(8,128)(2,1)}, u32[]{:S(2)}, u32[]{:S(2)}) collective-permute-start(bf16[512,3968]{1,0:T(8,128)(2,1)} %bitcast.4.own_ref.own_meta), channel_id=1, source_target_pairs={{0,1},{1,0},{2,3},{3,2},{4,5},{5,4},{6,7},{7,6},{8,9},{9,8},{10,11... | collective-permute-start | bytes 12189704 | tf_op jit(solution)/shard_map/ppermute | solution.py:615
  70.7 7.2 %all-to-all-start.1 = ((bf16[64,8,3840]{2,1,0:T(8,128)(2,1)}), bf16[64,8,3840]{2,1,0:T(8,128)(2,1)}, u32[]{:S(2)}, u32[]{:S(2)}) async-start(bf16[64,8,3840]{2,1,0:T(8,128)(2,1)} %bitcast.14), calls=%async_computation.1 | async-start | bytes 7864320 | tf_op jit(solution)/shard_map/all_to_all | solution.py:610
  77.9 0.0 collective-permute-done.other_ref.other_meta
  77.9 10.7 %norm.1 = (bf16[384,5120]{1,0:T(8,128)(2,1)}, bf16[384,5120]{1,0:T(8,128)(2,1)}, f32[384,128]{1,0:T(8,128)}, f32[384,128]{1,0:T(8,128)}, f32[384,128]{1,0:T(8,12...) custom-call(bf16[512,3968]{1,0:T(8,128)(2,1)} %bitcast.4.own_ref.own_meta, ...), custom_call_target="tpu_custom_call" | custom-call | flops 377487360 | bytes 24821764 | tf_op jit(solution)/shard_map/norm/pallas_call | solution.py:466
  88.6 19.0 %forward.1 = (bf16[384,5120]{1,0:T(8,128)(2,1)}, bf16[384,768]{1,0:T(8,128)(2,1)}, f32[768,768]{1,0:T(8,128)}) custom-call(bf16[384,5120]{1,0:T(8,128)(2,1)} %get-tuple-element.33.own_ref.normed_ref, bf16[384,5120]{1,0:T(8,128)(2,1)} %get-tuple-element.34.other_ref, bf16[1,5120,768]{2,1,0:T(8,128)(2,1)} %weight_ref.3, bf16[1,768,5120]{2,1,0:T(8,128)(2,1)} %down_ref.3), custom_call_target="tpu_custom_call" | custom-call | flops 9059696640 | bytes 31457280 | tf_op jit(solution)/shard_map/forward/pallas_call | solution.py:571
  107.7 0.3 collective-permute-start.1
  108.0 7.6 %forward_own.1.own_ref = bf16[384,5120]{1,0:T(8,128)(2,1)} custom-call(bf16[384,768]{1,0:T(8,128)(2,1)} %get-tuple-element.35.x_ref, bf16[1,768,5120]{2,1,0:T(8,128)(2,1)} %down_ref.3), custom_call_target="tpu_custom_call" | custom-call | flops 193273528320 | bytes 754974720 | tf_op jit(solution)/shard_map/forward_own/pallas_call | solution.py:596
  115.6 0.0 collective-permute-done.1.other_ref
  115.6 7.1 %out.1 = (bf16[384,5120]{1,0:T(8,128)(2,1)}, bf16[512,3840]{1,0:T(8,128)(2,1)}) custom-call(bf16[384,5120]{1,0:T(8,128)(2,1)} %forward_own.1.own_ref, bf16[384,5120]{1,0:T(8,128)(2,1)} %collective-permute-done.1.other_ref, f32[384,128]{1,0:T(8,128)} %get-tuple-element.37.gate_ref.own_gate, bf16[192,192]{1,0:T(8,128)(2,1)} %constant.9.clone.back_ref), custom_call_target="tpu_custom_call" | custom-call | flops 188743680 | bytes 15998976 | tf_op jit(solution)/shard_map/out/pallas_call | solution.py:466
  122.7 5.1 %all-to-all-done.1 = bf16[64,8,3840]{2,1,0:T(8,128)(2,1)} async-done(((bf16[64,8,3840]{2,1,0:T(8,128)(2,1)}), bf16[64,8,3840]{2,1,0:T(8,128)(2,1)}, u32[]{:S(2)}, u32[]{:S(2)}) %all-to-all-start.1) | async-done | bytes 3932192 | tf_op jit(solution)/shard_map/all_to_all | solution.py:610
  127.7 2.2 collective-permute-start.2
  129.9 6.8 %all-to-all-start.2 = ((bf16[64,8,3840]{2,1,0:T(8,128)(2,1)}), bf16[64,8,3840]{2,1,0:T(8,128)(2,1)}, u32[]{:S(2)}, u32[]{:S(2)}) async-start(bf16[64,8,3840]{2,1,0:T(8,128)(2,1)} %bitcast.15), calls=%async_computation.2 | async-start | bytes 7864320 | tf_op jit(solution)/shard_map/all_to_all | solution.py:610
  136.7 0.0 collective-permute-done.2.other_ref
  136.7 9.3 %cot.1 = (bf16[384,5120]{1,0:T(8,128)(2,1)}, bf16[384,5120]{1,0:T(8,128)(2,1)}, f32[384,128]{1,0:T(8,128)}, f32[8,5120]{1,0:T(8,128)}) custom-call(bf16[512,3840]{1,0:T(8,128)(2,1)} %bitcast.6.own_ref, bf16[512,3840]{1,0:T(8,128)(2,1)} %collective-permute-done.2.other_ref, f32[384,128]{1,0:T(8,128)} %get-tuple-element.37.gate_ref.own_gate, ...), custom_call_target="tpu_custom_call" | custom-call | flops 377487360 | bytes 24420352 | tf_op jit(solution)/shard_map/cot/pallas_call | solution.py:466
  146.0 0.4 collective-permute-start.4
  146.4 18.1 %backward.1 = (bf16[384,5120]{1,0:T(8,128)(2,1)}, bf16[384,768]{1,0:T(8,128)(2,1)}) custom-call(bf16[384,5120]{1,0:T(8,128)(2,1)} %get-tuple-element.45.own_ref, bf16[384,5120]{1,0:T(8,128)(2,1)} %get-tuple-element.46.other_ref, bf16[1,768,5120]{2,1,0:T(8,128)(2,1)} %down_ref.3, bf16[1,5120,768]{2,1,0:T(8,128)(2,1)} %weight_ref.3, ...), custom_call_target="tpu_custom_call" | custom-call | flops 9059696640 | bytes 31457280 | tf_op jit(solution)/shard_map/backward/pallas_call | solution.py:571
  164.5 0.2 collective-permute-start.3
  164.7 7.6 %backward_own.1.own_ref = bf16[384,5120]{1,0:T(8,128)(2,1)} custom-call(bf16[384,768]{1,0:T(8,128)(2,1)} %get-tuple-element.48.x_ref, bf16[1,5120,768]{2,1,0:T(8,128)(2,1)} %weight_ref.3), custom_call_target="tpu_custom_call" | custom-call | flops 193273528320 | bytes 754974720 | tf_op jit(solution)/shard_map/backward_own/pallas_call | solution.py:596
  172.3 0.0 collective-permute-done.4.other_router
  172.3 0.0 collective-permute-done.3.other_ref
  172.3 10.5 %grad.1 = bf16[512,3968]{1,0:T(8,128)(2,1)} custom-call(bf16[384,5120]{1,0:T(8,128)(2,1)} %backward_own.1.own_ref, bf16[384,5120]{1,0:T(8,128)(2,1)} %collective-permute-done.3.other_ref, f32[384,128]{1,0:T(8,128)} %get-tuple-element.50.choice_ref, f32[384,128]{1,0:T(8,128)} %get-tuple-element.51.scale_ref, ...), custom_call_target="tpu_custom_call" | custom-call | flops 188743680 | bytes 16695300 | tf_op jit(solution)/shard_map/grad/pallas_call | solution.py:466
  182.8 3.6 %all-to-all-done.2 = bf16[64,8,3840]{2,1,0:T(8,128)(2,1)} async-done(((bf16[64,8,3840]{2,1,0:T(8,128)(2,1)}), bf16[64,8,3840]{2,1,0:T(8,128)(2,1)}, u32[]{:S(2)}, u32[]{:S(2)}) %all-to-all-start.2) | async-done | bytes 3932192 | tf_op jit(solution)/shard_map/all_to_all | solution.py:610
  186.5 0.0 copy-start
  186.5 8.3 %all-to-all-start.3 = ((bf16[64,8,3968]{2,1,0:T(8,128)(2,1)}), bf16[64,8,3968]{2,1,0:T(8,128)(2,1)}, u32[]{:S(2)}, u32[]{:S(2)}) async-start(bf16[64,8,3968]{2,1,0:T(8,128)(2,1)} %bitcast.12), calls=%async_computation.3 | async-start | bytes 8126464 | tf_op jit(solution)/shard_map/all_to_all | solution.py:610
  194.8 0.0 copy-done
  194.8 0.7 copy.13.ids_ref
  195.5 5.3 %mixed.1 = (bf16[128,5120]{1,0:T(8,128)(2,1)}, bf16[3,256,512]{2,1,0:T(8,128)(2,1)}) custom-call(s32[128,2]{1,0:T(8,128)} %copy.13.ids_ref, bf16[128,5120]{1,0:T(8,128)(2,1)} %tokens_ref.1, bf16[512,3840]{1,0:T(8,128)(2,1)} %bitcast.8.band0.band1.band2, bf16[512,3840]{1,0:T(8,128)(2,1)} %bitcast.8.band0.band1.band2, bf16[512,3840]{1,0:T(8,128)(2,1)} %bitcast.8.band0.band1.band2), custom_call_target="tpu_custom_call" | custom-call | flops 1006632960 | bytes 3932160 | tf_op jit(solution)/shard_map/mixed/pallas_call | solution.py:224
  200.8 44.2 %all-to-all-done.3 = bf16[64,8,3968]{2,1,0:T(8,128)(2,1)} async-done(((bf16[64,8,3968]{2,1,0:T(8,128)(2,1)}), bf16[64,8,3968]{2,1,0:T(8,128)(2,1)}, u32[]{:S(2)}, u32[]{:S(2)}) %all-to-all-start.3) | async-done | bytes 4063264 | tf_op jit(solution)/shard_map/all_to_all | solution.py:610
  244.9 1.9 sums.1
  246.8 2.3 collective-permute-start.5
  249.1 0.0 copy-start.1
  249.1 5.0 %grad_tokens.1 = bf16[128,5120]{1,0:T(8,128)(2,1)} custom-call(bf16[3,256,512]{2,1,0:T(8,128)(2,1)} %get-tuple-element.41.choose_ref, bf16[128,5120]{1,0:T(8,128)(2,1)} %cot_ref.1, bf16[512,3968]{1,0:T(8,128)(2,1)} %bitcast.10.band0.band1.band2.meta_ref, bf16[512,3968]{1,0:T(8,128)(2,1)} %bitcast.10.band0.band1.band2.meta_ref, ...), custom_call_target="tpu_custom_call" | custom-call | flops 1006632960 | bytes 3932160 | tf_op jit(solution)/shard_map/grad_tokens/pallas_call | solution.py:224
  254.1 0.0 collective-permute-done.5
  254.1 0.0 copy-done.1
  254.1 0.6 add_reduce_fusion
Async XLA Ops:
  5.4 62.4 %all-to-all-start = ((bf16[64,8,3968]{2,1,0:T(8,128)(2,1)}), bf16[64,8,3968]{2,1,0:T(8,128)(2,1)}, u32[]{:S(2)}, u32[]{:S(2)}) async-start(bf16[64,8,3968]{2,1,0:T(8,128)(2,1)} %bitcast.13), calls=%async_computation | async-start | bytes 8126464 | tf_op jit(solution)/shard_map/all_to_all | solution.py:610
  67.8 10.1 %collective-permute-start = (bf16[512,3968]{1,0:T(8,128)(2,1)}, bf16[512,3968]{1,0:T(8,128)(2,1)}, u32[]{:S(2)}, u32[]{:S(2)}) collective-permute-start(bf16[512,3968]{1,0:T(8,128)(2,1)} %bitcast.4.own_ref.own_meta), channel_id=1, source_target_pairs={{0,1},{1,0},{2,3},{3,2},{4,5},{5,4},{6,7},{7,6},{8,9},{9,8},{10,11... | collective-permute-start | bytes 12189704 | tf_op jit(solution)/shard_map/ppermute | solution.py:615
  70.7 57.0 %all-to-all-start.1 = ((bf16[64,8,3840]{2,1,0:T(8,128)(2,1)}), bf16[64,8,3840]{2,1,0:T(8,128)(2,1)}, u32[]{:S(2)}, u32[]{:S(2)}) async-start(bf16[64,8,3840]{2,1,0:T(8,128)(2,1)} %bitcast.14), calls=%async_computation.1 | async-start | bytes 7864320 | tf_op jit(solution)/shard_map/all_to_all | solution.py:610
  107.7 7.9 %collective-permute-start.1 = (bf16[384,5120]{1,0:T(8,128)(2,1)}, bf16[384,5120]{1,0:T(8,128)(2,1)}, u32[]{:S(2)}, u32[]{:S(2)}) collective-permute-start(bf16[384,5120]{1,0:T(8,128)(2,1)} %get-tuple-element.36), channel_id=1, source_target_pairs={{0,1},{1,0},{2,3},{3,2},{4,5},{5,4},{6,7},{7,6},{8,9},{9,8},{10,11... | collective-permute-start | bytes 11796488 | tf_op jit(solution)/shard_map/ppermute | solution.py:615
  127.7 8.9 %collective-permute-start.2 = (bf16[512,3840]{1,0:T(8,128)(2,1)}, bf16[512,3840]{1,0:T(8,128)(2,1)}, u32[]{:S(2)}, u32[]{:S(2)}) collective-permute-start(bf16[512,3840]{1,0:T(8,128)(2,1)} %bitcast.6.own_ref), channel_id=1, source_target_pairs={{0,1},{1,0},{2,3},{3,2},{4,5},{5,4},{6,7},{7,6},{8,9},{9,8},{10,11... | collective-permute-start | bytes 11796488 | tf_op jit(solution)/shard_map/ppermute | solution.py:615
  129.9 56.6 %all-to-all-start.2 = ((bf16[64,8,3840]{2,1,0:T(8,128)(2,1)}), bf16[64,8,3840]{2,1,0:T(8,128)(2,1)}, u32[]{:S(2)}, u32[]{:S(2)}) async-start(bf16[64,8,3840]{2,1,0:T(8,128)(2,1)} %bitcast.15), calls=%async_computation.2 | async-start | bytes 7864320 | tf_op jit(solution)/shard_map/all_to_all | solution.py:610
  146.0 26.3 %collective-permute-start.4 = (f32[8,5120]{1,0:T(8,128)}, f32[8,5120]{1,0:T(8,128)}, u32[]{:S(2)}, u32[]{:S(2)}) collective-permute-start(f32[8,5120]{1,0:T(8,128)} %get-tuple-element.54.own_router), channel_id=1, source_target_pairs={{0,1},{1,0},{2,3},{3,2},{4,5},{5,4},{6,7},{7,6},{8,9},{9,8},{10,11... | collective-permute-start | bytes 491528 | tf_op jit(solution)/shard_map/ppermute | solution.py:615
  164.5 7.8 %collective-permute-start.3 = (bf16[384,5120]{1,0:T(8,128)(2,1)}, bf16[384,5120]{1,0:T(8,128)(2,1)}, u32[]{:S(2)}, u32[]{:S(2)}) collective-permute-start(bf16[384,5120]{1,0:T(8,128)(2,1)} %get-tuple-element.49), channel_id=1, source_target_pairs={{0,1},{1,0},{2,3},{3,2},{4,5},{5,4},{6,7},{7,6},{8,9},{9,8},{10,11... | collective-permute-start | bytes 11796488 | tf_op jit(solution)/shard_map/ppermute | solution.py:615
  186.5 8.3 %copy-start = (s32[128,2]{0,1:T(2,128)S(1)}, s32[128,2]{0,1:T(2,128)}, u32[]{:S(2)}) copy-start(s32[128,2]{0,1:T(2,128)} %param.14) | copy-start | bytes 3076
  186.5 58.5 %all-to-all-start.3 = ((bf16[64,8,3968]{2,1,0:T(8,128)(2,1)}), bf16[64,8,3968]{2,1,0:T(8,128)(2,1)}, u32[]{:S(2)}, u32[]{:S(2)}) async-start(bf16[64,8,3968]{2,1,0:T(8,128)(2,1)} %bitcast.12), calls=%async_computation.3 | async-start | bytes 8126464 | tf_op jit(solution)/shard_map/all_to_all | solution.py:610
  246.8 7.3 %collective-permute-start.5 = (f32[1,320]{1,0:T(1,128)}, f32[1,320]{1,0:T(1,128)S(1)}, u32[]{:S(2)}, u32[]{:S(2)}) collective-permute-start(f32[1,320]{1,0:T(1,128)} %get-tuple-element.57), channel_id=1, source_target_pairs={{0,1},{1,0},{2,3},{3,2},{4,5},{5,4},{6,7},{7,6},{8,9},{9,8},{10,11... | collective-permute-start | bytes 3848 | tf_op jit(solution)/shard_map/ppermute | solution.py:615
  249.1 5.0 %copy-start.1 = (f32[1,320]{1,0:T(1,128)S(1)}, f32[1,320]{1,0:T(1,128)}, u32[]{:S(2)}) copy-start(f32[1,320]{1,0:T(1,128)} %get-tuple-element.56) | copy-start | bytes 3844

commit v6 on v5

--- a/solution.py
+++ b/solution.py
@@ -23,9 +23,9 @@
 META = 128
 SUB = 4
 VMEM_LIMIT = 56 * 1024 * 1024
-CHIPS = ("pair", "ep")
-FSDP = ("pair", "core")
-EVERY = ("ep", "pair", "core")
+CHIPS = ("side", "line", "ep")
+FSDP = ("line", "side", "core")
+EVERY = ("ep", "line", "side", "core")
 
 
 def params(steps):
@@ -51,7 +51,11 @@
 
 
 def message_of(expert, eps, pairs):
-    return expert % pairs * eps + expert // pairs
+    return place_of(expert % pairs, pairs) * eps + expert // pairs
+
+
+def place_of(pair, pairs):
+    return pair % 2 * (pairs // 2) + pair // 2
 
 
 def as_bf16(mask):
@@ -311,7 +315,7 @@
         for part, ref in ((0, gain_ref), (3, column_ref)):
             pairs = features // (5 * META)
             for pair in range(pairs):
-                at = pair * (own.shape[0] // pairs) + part
+                at = place_of(pair, pairs) * (own.shape[0] // pairs) + part
                 rows = [first[at + r : at + r + 1] for r in range(3)]
                 rows += [second[at + r : at + r + 1] for r in range(3)]
                 rows = [rows[0], rows[1], rows[2] + rows[3], rows[4], rows[5]]
@@ -445,7 +449,8 @@
         for pair in range(pairs):
             meta = meta_ref[pair * TILE : (pair + 1) * TILE]
             meta = jnp.concatenate([meta] * (count // TILE), axis=0).astype(BF16)
-            send_ref[pair * count : (pair + 1) * count, BANDS * piece :] = meta
+            at = place_of(pair, pairs) * count
+            send_ref[at : at + count, BANDS * piece :] = meta
 
 
 def by_group(kernel, inputs, outputs, flops, name, scratch=()):
@@ -617,7 +622,8 @@
 
 def body(tokens, norm_gain, router_weight, up_weight, down_weight, expert_ids, cotangent):
     toks, features = tokens.shape
-    eps, pairs, cores = (lax.axis_size(name) for name in EVERY)
+    eps, lines, sides, cores = (lax.axis_size(name) for name in EVERY)
+    pairs = lines * sides
     experts = eps * pairs
     shard = features // (pairs * cores)
     rows = experts * CAP
@@ -743,7 +749,7 @@
 
 def solution(mesh):
     eps, fsdp = mesh.devices.shape
-    fine = Mesh(mesh.devices.reshape(eps, fsdp // 2, 2), EVERY)
+    fine = Mesh(mesh.devices.reshape(eps, fsdp // 4, 2, 2), EVERY)
     in_specs = (
         P(EVERY, None),
         P(FSDP),

time: 256 us -> 258 us (level)
  starting transfers between devices: 42.6 us -> 48.9 us
  waiting for transfers between devices: 98.9 us -> 93.1 us
    all_to_all x4, starting transfers between devices: 34.5 us -> 42.1 us  [exchange(): lax.all_to_all(blocks, CHIPS, split_axis=0, concat_axis=0, tiled=True)]
    all_to_all x4, waiting for transfers between devices: 98.9 us -> 93 us  [exchange(): lax.all_to_all(blocks, CHIPS, split_axis=0, concat_axis=0, tiled=True)]
where the time goes in v6:
time: 258 us; the launch traced here: 255 us
  Pallas kernels  111 us (43%)
  waiting for transfers between devices  93.1 us (36%)
  starting transfers between devices  48.9 us (19%)
    all_to_all x4, waiting for transfers between devices, exchange(): lax.all_to_all(blocks, CHIPS, split_axis=0, concat_axis=0, tiled=True)  93 us
    all_to_all x4, starting transfers between devices, exchange(): lax.all_to_all(blocks, CHIPS, split_axis=0, concat_axis=0, tiled=True)  42.1 us
    pallas_call x4, Pallas kernels, by_group(): pl.pallas_call(kernel, grid=(steps,), in_specs=[spec(value.shape, rows) f...  37.6 us
    pallas_call x2, Pallas kernels, expert_call(): pl.pallas_call(kernel, grid=(2 * half,), in_specs=in_specs, out_specs=out...  37.2 us
    pallas_call x2, Pallas kernels, last_call(): pl.pallas_call(functools.partial(last_kernel, product=product), grid=(PAR...  15.2 us
    pallas_call x2, Pallas kernels, token_side(): pl.pallas_call(kernel, grid=(1,), in_specs=[whole(value.shape) for value...  10.3 us
    pallas_call x2, Pallas kernels, pack(): pl.pallas_call(functools.partial(pack_kernel, eps, pairs), grid=(steps,),...  9 us
    ppermute x6, starting transfers between devices, swap(): return lax.ppermute(value, 'core', [(0, 1), (1, 0)])  6.78 us
  transfers between devices with their start and end apart: 10, of which 4 were waited for; matrix products, arithmetic and copies ran while one was open for 0% of the time, Pallas kernels for 41%

profile of v6, /device:TPU:1, one launch (start us, length us, event | category | flops | bytes accessed | tf_op | source)
XLA Modules:
  0.0 255.3 jit_solution(15447465328836081337)
XLA Ops:
  0.6 4.8 %pack.2 = bf16[512,3968]{1,0:T(8,128)(2,1)} custom-call(s32[2,128]{1,0:T(2,128)} %bitcast.17, bf16[128,5120]{1,0:T(8,128)(2,1)} %tokens_ref.1, bf16[320]{0:T(512)(128)(2,1)} %refs_0_.1, bf16[64,320]{1,0:T(8,128)(2,1)} %bitcast.16, s32[1,1]{1,0:T(1,128)} %bitcast.2.refs_2_.core_ref), custom_call_target="tpu_custom_call" | custom-call | flops 1040187392 | bytes 4063232 | tf_op jit(solution)/shard_map/pack/pallas_call | solution.py:152
  5.4 12.2 %all-to-all-start = ((bf16[64,8,3968]{2,1,0:T(8,128)(2,1)}), bf16[64,8,3968]{2,1,0:T(8,128)(2,1)}, u32[]{:S(2)}, u32[]{:S(2)}) async-start(bf16[64,8,3968]{2,1,0:T(8,128)(2,1)} %bitcast.13), calls=%async_computation | async-start | bytes 8126464 | tf_op jit(solution)/shard_map/all_to_all | solution.py:615
  17.6 4.2 %pack.3 = bf16[512,3840]{1,0:T(8,128)(2,1)} custom-call(s32[2,128]{1,0:T(2,128)} %bitcast.18, bf16[128,5120]{1,0:T(8,128)(2,1)} %cot_ref.1), custom_call_target="tpu_custom_call" | custom-call | flops 1006632960 | bytes 3932160 | tf_op jit(solution)/shard_map/pack/pallas_call | solution.py:152
  21.8 43.4 %all-to-all-done = bf16[64,8,3968]{2,1,0:T(8,128)(2,1)} async-done(((bf16[64,8,3968]{2,1,0:T(8,128)(2,1)}), bf16[64,8,3968]{2,1,0:T(8,128)(2,1)}, u32[]{:S(2)}, u32[]{:S(2)}) %all-to-all-start) | async-done | bytes 4063264 | tf_op jit(solution)/shard_map/all_to_all | solution.py:615
  65.3 2.4 collective-permute-start
  67.6 10.5 %all-to-all-start.1 = ((bf16[64,8,3840]{2,1,0:T(8,128)(2,1)}), bf16[64,8,3840]{2,1,0:T(8,128)(2,1)}, u32[]{:S(2)}, u32[]{:S(2)}) async-start(bf16[64,8,3840]{2,1,0:T(8,128)(2,1)} %bitcast.14), calls=%async_computation.1 | async-start | bytes 7864320 | tf_op jit(solution)/shard_map/all_to_all | solution.py:615
  78.2 0.0 collective-permute-done.other_ref.other_meta
  78.2 10.7 %norm.1 = (bf16[384,5120]{1,0:T(8,128)(2,1)}, bf16[384,5120]{1,0:T(8,128)(2,1)}, f32[384,128]{1,0:T(8,128)}, f32[384,128]{1,0:T(8,128)}, f32[384,128]{1,0:T(8,12...) custom-call(bf16[512,3968]{1,0:T(8,128)(2,1)} %bitcast.4.own_ref.own_meta, ...), custom_call_target="tpu_custom_call" | custom-call | flops 377487360 | bytes 24821764 | tf_op jit(solution)/shard_map/norm/pallas_call | solution.py:471
  88.9 19.0 %forward.1 = (bf16[384,5120]{1,0:T(8,128)(2,1)}, bf16[384,768]{1,0:T(8,128)(2,1)}, f32[768,768]{1,0:T(8,128)}) custom-call(bf16[384,5120]{1,0:T(8,128)(2,1)} %get-tuple-element.33.own_ref.normed_ref, bf16[384,5120]{1,0:T(8,128)(2,1)} %get-tuple-element.34.other_ref, bf16[1,5120,768]{2,1,0:T(8,128)(2,1)} %weight_ref.3, bf16[1,768,5120]{2,1,0:T(8,128)(2,1)} %down_ref.3), custom_call_target="tpu_custom_call" | custom-call | flops 9059696640 | bytes 31457280 | tf_op jit(solution)/shard_map/forward/pallas_call | solution.py:576
  108.0 0.3 collective-permute-start.1
  108.2 7.6 %forward_own.1.own_ref = bf16[384,5120]{1,0:T(8,128)(2,1)} custom-call(bf16[384,768]{1,0:T(8,128)(2,1)} %get-tuple-element.35.x_ref, bf16[1,768,5120]{2,1,0:T(8,128)(2,1)} %down_ref.3), custom_call_target="tpu_custom_call" | custom-call | flops 193273528320 | bytes 754974720 | tf_op jit(solution)/shard_map/forward_own/pallas_call | solution.py:601
  115.8 0.0 collective-permute-done.1.other_ref
  115.8 7.1 %out.1 = (bf16[384,5120]{1,0:T(8,128)(2,1)}, bf16[512,3840]{1,0:T(8,128)(2,1)}) custom-call(bf16[384,5120]{1,0:T(8,128)(2,1)} %forward_own.1.own_ref, bf16[384,5120]{1,0:T(8,128)(2,1)} %collective-permute-done.1.other_ref, f32[384,128]{1,0:T(8,128)} %get-tuple-element.37.gate_ref.own_gate, bf16[192,192]{1,0:T(8,128)(2,1)} %constant.9.clone.back_ref), custom_call_target="tpu_custom_call" | custom-call | flops 188743680 | bytes 15998976 | tf_op jit(solution)/shard_map/out/pallas_call | solution.py:471
  122.9 4.7 %all-to-all-done.1 = bf16[64,8,3840]{2,1,0:T(8,128)(2,1)} async-done(((bf16[64,8,3840]{2,1,0:T(8,128)(2,1)}), bf16[64,8,3840]{2,1,0:T(8,128)(2,1)}, u32[]{:S(2)}, u32[]{:S(2)}) %all-to-all-start.1) | async-done | bytes 3932192 | tf_op jit(solution)/shard_map/all_to_all | solution.py:615
  127.7 0.8 collective-permute-start.2
  128.4 9.8 %all-to-all-start.2 = ((bf16[64,8,3840]{2,1,0:T(8,128)(2,1)}), bf16[64,8,3840]{2,1,0:T(8,128)(2,1)}, u32[]{:S(2)}, u32[]{:S(2)}) async-start(bf16[64,8,3840]{2,1,0:T(8,128)(2,1)} %bitcast.15), calls=%async_computation.2 | async-start | bytes 7864320 | tf_op jit(solution)/shard_map/all_to_all | solution.py:615
  138.2 0.0 collective-permute-done.2.other_ref
  138.2 9.3 %cot.1 = (bf16[384,5120]{1,0:T(8,128)(2,1)}, bf16[384,5120]{1,0:T(8,128)(2,1)}, f32[384,128]{1,0:T(8,128)}, f32[8,5120]{1,0:T(8,128)}) custom-call(bf16[512,3840]{1,0:T(8,128)(2,1)} %bitcast.6.own_ref, bf16[512,3840]{1,0:T(8,128)(2,1)} %collective-permute-done.2.other_ref, f32[384,128]{1,0:T(8,128)} %get-tuple-element.37.gate_ref.own_gate, ...), custom_call_target="tpu_custom_call" | custom-call | flops 377487360 | bytes 24420352 | tf_op jit(solution)/shard_map/cot/pallas_call | solution.py:471
  147.5 0.4 collective-permute-start.4
  147.9 18.1 %backward.1 = (bf16[384,5120]{1,0:T(8,128)(2,1)}, bf16[384,768]{1,0:T(8,128)(2,1)}) custom-call(bf16[384,5120]{1,0:T(8,128)(2,1)} %get-tuple-element.45.own_ref, bf16[384,5120]{1,0:T(8,128)(2,1)} %get-tuple-element.46.other_ref, bf16[1,768,5120]{2,1,0:T(8,128)(2,1)} %down_ref.3, bf16[1,5120,768]{2,1,0:T(8,128)(2,1)} %weight_ref.3, ...), custom_call_target="tpu_custom_call" | custom-call | flops 9059696640 | bytes 31457280 | tf_op jit(solution)/shard_map/backward/pallas_call | solution.py:576
  166.0 0.2 collective-permute-start.3
  166.3 7.6 %backward_own.1.own_ref = bf16[384,5120]{1,0:T(8,128)(2,1)} custom-call(bf16[384,768]{1,0:T(8,128)(2,1)} %get-tuple-element.48.x_ref, bf16[1,5120,768]{2,1,0:T(8,128)(2,1)} %weight_ref.3), custom_call_target="tpu_custom_call" | custom-call | flops 193273528320 | bytes 754974720 | tf_op jit(solution)/shard_map/backward_own/pallas_call | solution.py:601
  173.9 0.0 collective-permute-done.4.other_router
  173.9 0.0 collective-permute-done.3.other_ref
  173.9 10.5 %grad.1 = bf16[512,3968]{1,0:T(8,128)(2,1)} custom-call(bf16[384,5120]{1,0:T(8,128)(2,1)} %backward_own.1.own_ref, bf16[384,5120]{1,0:T(8,128)(2,1)} %collective-permute-done.3.other_ref, f32[384,128]{1,0:T(8,128)} %get-tuple-element.50.choice_ref, f32[384,128]{1,0:T(8,128)} %get-tuple-element.51.scale_ref, ...), custom_call_target="tpu_custom_call" | custom-call | flops 188743680 | bytes 16695300 | tf_op jit(solution)/shard_map/grad/pallas_call | solution.py:471
  184.4 3.3 %all-to-all-done.2 = bf16[64,8,3840]{2,1,0:T(8,128)(2,1)} async-done(((bf16[64,8,3840]{2,1,0:T(8,128)(2,1)}), bf16[64,8,3840]{2,1,0:T(8,128)(2,1)}, u32[]{:S(2)}, u32[]{:S(2)}) %all-to-all-start.2) | async-done | bytes 3932192 | tf_op jit(solution)/shard_map/all_to_all | solution.py:615
  187.7 0.0 copy-start
  187.7 9.7 %all-to-all-start.3 = ((bf16[64,8,3968]{2,1,0:T(8,128)(2,1)}), bf16[64,8,3968]{2,1,0:T(8,128)(2,1)}, u32[]{:S(2)}, u32[]{:S(2)}) async-start(bf16[64,8,3968]{2,1,0:T(8,128)(2,1)} %bitcast.12), calls=%async_computation.3 | async-start | bytes 8126464 | tf_op jit(solution)/shard_map/all_to_all | solution.py:615
  197.4 0.0 copy-done
  197.4 0.7 copy.13.ids_ref
  198.1 5.3 %mixed.1 = (bf16[128,5120]{1,0:T(8,128)(2,1)}, bf16[3,256,512]{2,1,0:T(8,128)(2,1)}) custom-call(s32[128,2]{1,0:T(8,128)} %copy.13.ids_ref, bf16[128,5120]{1,0:T(8,128)(2,1)} %tokens_ref.1, bf16[512,3840]{1,0:T(8,128)(2,1)} %bitcast.8.band0.band1.band2, bf16[512,3840]{1,0:T(8,128)(2,1)} %bitcast.8.band0.band1.band2, bf16[512,3840]{1,0:T(8,128)(2,1)} %bitcast.8.band0.band1.band2), custom_call_target="tpu_custom_call" | custom-call | flops 1006632960 | bytes 3932160 | tf_op jit(solution)/shard_map/mixed/pallas_call | solution.py:228
  203.4 41.6 %all-to-all-done.3 = bf16[64,8,3968]{2,1,0:T(8,128)(2,1)} async-done(((bf16[64,8,3968]{2,1,0:T(8,128)(2,1)}), bf16[64,8,3968]{2,1,0:T(8,128)(2,1)}, u32[]{:S(2)}, u32[]{:S(2)}) %all-to-all-start.3) | async-done | bytes 4063264 | tf_op jit(solution)/shard_map/all_to_all | solution.py:615
  245.0 1.9 sums.1
  246.9 2.8 %collective-permute-start.5 = (f32[1,320]{1,0:T(1,128)}, f32[1,320]{1,0:T(1,128)S(1)}, u32[]{:S(2)}, u32[]{:S(2)}) collective-permute-start(f32[1,320]{1,0:T(1,128)} %get-tuple-element.57), channel_id=1, source_target_pairs={{0,1},{1,0},{2,3},{3,2},{4,5},{5,4},{6,7},{7,6},{8,9},{9,8},{10,11... | collective-permute-start | bytes 3848 | tf_op jit(solution)/shard_map/ppermute | solution.py:620
  249.7 0.0 copy-start.1
  249.7 5.0 %grad_tokens.1 = bf16[128,5120]{1,0:T(8,128)(2,1)} custom-call(bf16[3,256,512]{2,1,0:T(8,128)(2,1)} %get-tuple-element.41.choose_ref, bf16[128,5120]{1,0:T(8,128)(2,1)} %cot_ref.1, bf16[512,3968]{1,0:T(8,128)(2,1)} %bitcast.10.band0.band1.band2.meta_ref, bf16[512,3968]{1,0:T(8,128)(2,1)} %bitcast.10.band0.band1.band2.meta_ref, ...), custom_call_target="tpu_custom_call" | custom-call | flops 1006632960 | bytes 3932160 | tf_op jit(solution)/shard_map/grad_tokens/pallas_call | solution.py:228
  254.7 0.0 collective-permute-done.5
  254.7 0.0 copy-done.1
  254.7 0.6 add_reduce_fusion
Async XLA Ops:
  5.4 59.9 %all-to-all-start = ((bf16[64,8,3968]{2,1,0:T(8,128)(2,1)}), bf16[64,8,3968]{2,1,0:T(8,128)(2,1)}, u32[]{:S(2)}, u32[]{:S(2)}) async-start(bf16[64,8,3968]{2,1,0:T(8,128)(2,1)} %bitcast.13), calls=%async_computation | async-start | bytes 8126464 | tf_op jit(solution)/shard_map/all_to_all | solution.py:615
  65.3 12.9 %collective-permute-start = (bf16[512,3968]{1,0:T(8,128)(2,1)}, bf16[512,3968]{1,0:T(8,128)(2,1)}, u32[]{:S(2)}, u32[]{:S(2)}) collective-permute-start(bf16[512,3968]{1,0:T(8,128)(2,1)} %bitcast.4.own_ref.own_meta), channel_id=1, source_target_pairs={{0,1},{1,0},{2,3},{3,2},{4,5},{5,4},{6,7},{7,6},{8,9},{9,8},{10,11... | collective-permute-start | bytes 12189704 | tf_op jit(solution)/shard_map/ppermute | solution.py:620
  67.6 60.0 %all-to-all-start.1 = ((bf16[64,8,3840]{2,1,0:T(8,128)(2,1)}), bf16[64,8,3840]{2,1,0:T(8,128)(2,1)}, u32[]{:S(2)}, u32[]{:S(2)}) async-start(bf16[64,8,3840]{2,1,0:T(8,128)(2,1)} %bitcast.14), calls=%async_computation.1 | async-start | bytes 7864320 | tf_op jit(solution)/shard_map/all_to_all | solution.py:615
  108.0 7.9 %collective-permute-start.1 = (bf16[384,5120]{1,0:T(8,128)(2,1)}, bf16[384,5120]{1,0:T(8,128)(2,1)}, u32[]{:S(2)}, u32[]{:S(2)}) collective-permute-start(bf16[384,5120]{1,0:T(8,128)(2,1)} %get-tuple-element.36), channel_id=1, source_target_pairs={{0,1},{1,0},{2,3},{3,2},{4,5},{5,4},{6,7},{7,6},{8,9},{9,8},{10,11... | collective-permute-start | bytes 11796488 | tf_op jit(solution)/shard_map/ppermute | solution.py:620
  127.7 10.6 %collective-permute-start.2 = (bf16[512,3840]{1,0:T(8,128)(2,1)}, bf16[512,3840]{1,0:T(8,128)(2,1)}, u32[]{:S(2)}, u32[]{:S(2)}) collective-permute-start(bf16[512,3840]{1,0:T(8,128)(2,1)} %bitcast.6.own_ref), channel_id=1, source_target_pairs={{0,1},{1,0},{2,3},{3,2},{4,5},{5,4},{6,7},{7,6},{8,9},{9,8},{10,11... | collective-permute-start | bytes 11796488 | tf_op jit(solution)/shard_map/ppermute | solution.py:620
  128.4 59.3 %all-to-all-start.2 = ((bf16[64,8,3840]{2,1,0:T(8,128)(2,1)}), bf16[64,8,3840]{2,1,0:T(8,128)(2,1)}, u32[]{:S(2)}, u32[]{:S(2)}) async-start(bf16[64,8,3840]{2,1,0:T(8,128)(2,1)} %bitcast.15), calls=%async_computation.2 | async-start | bytes 7864320 | tf_op jit(solution)/shard_map/all_to_all | solution.py:615
  147.5 26.3 %collective-permute-start.4 = (f32[8,5120]{1,0:T(8,128)}, f32[8,5120]{1,0:T(8,128)}, u32[]{:S(2)}, u32[]{:S(2)}) collective-permute-start(f32[8,5120]{1,0:T(8,128)} %get-tuple-element.54.own_router), channel_id=1, source_target_pairs={{0,1},{1,0},{2,3},{3,2},{4,5},{5,4},{6,7},{7,6},{8,9},{9,8},{10,11... | collective-permute-start | bytes 491528 | tf_op jit(solution)/shard_map/ppermute | solution.py:620
  166.0 7.8 %collective-permute-start.3 = (bf16[384,5120]{1,0:T(8,128)(2,1)}, bf16[384,5120]{1,0:T(8,128)(2,1)}, u32[]{:S(2)}, u32[]{:S(2)}) collective-permute-start(bf16[384,5120]{1,0:T(8,128)(2,1)} %get-tuple-element.49), channel_id=1, source_target_pairs={{0,1},{1,0},{2,3},{3,2},{4,5},{5,4},{6,7},{7,6},{8,9},{9,8},{10,11... | collective-permute-start | bytes 11796488 | tf_op jit(solution)/shard_map/ppermute | solution.py:620
  187.7 9.7 %copy-start = (s32[128,2]{0,1:T(2,128)S(1)}, s32[128,2]{0,1:T(2,128)}, u32[]{:S(2)}) copy-start(s32[128,2]{0,1:T(2,128)} %param.14) | copy-start | bytes 3076
  187.7 57.3 %all-to-all-start.3 = ((bf16[64,8,3968]{2,1,0:T(8,128)(2,1)}), bf16[64,8,3968]{2,1,0:T(8,128)(2,1)}, u32[]{:S(2)}, u32[]{:S(2)}) async-start(bf16[64,8,3968]{2,1,0:T(8,128)(2,1)} %bitcast.12), calls=%async_computation.3 | async-start | bytes 8126464 | tf_op jit(solution)/shard_map/all_to_all | solution.py:615
  246.9 7.8 %collective-permute-start.5 = (f32[1,320]{1,0:T(1,128)}, f32[1,320]{1,0:T(1,128)S(1)}, u32[]{:S(2)}, u32[]{:S(2)}) collective-permute-start(f32[1,320]{1,0:T(1,128)} %get-tuple-element.57), channel_id=1, source_target_pairs={{0,1},{1,0},{2,3},{3,2},{4,5},{5,4},{6,7},{7,6},{8,9},{9,8},{10,11... | collective-permute-start | bytes 3848 | tf_op jit(solution)/shard_map/ppermute | solution.py:620
  249.7 5.0 %copy-start.1 = (f32[1,320]{1,0:T(1,128)S(1)}, f32[1,320]{1,0:T(1,128)}, u32[]{:S(2)}) copy-start(f32[1,320]{1,0:T(1,128)} %get-tuple-element.56) | copy-start | bytes 3844

commit v7 on v5

--- a/solution.py
+++ b/solution.py
@@ -239,10 +239,13 @@
     experts, shard = router_ref.shape
     lower = core_ref[0, 0] == 0
     start = message_of(iota((experts, tiles), 0), eps, pairs) * TILE
-    rows = [dot(as_bf16(iota((experts, tiles), 1) == start + 5 + r), messages) for r in range(3)]
+    picks = [as_bf16(iota((experts, tiles), 1) == start + 5 + r) for r in range(3)]
+    picks.append(as_bf16((iota((2 * TILE, tiles), 1) & (TILE - 1)) == iota((2 * TILE, tiles), 0)))
+    picked = dot(jnp.concatenate(picks, axis=0), messages)
+    rows = [picked[r * experts : (r + 1) * experts] for r in range(3)]
     router = jnp.concatenate(rows, axis=1) * scale
     router_ref[...] = jnp.where(lower, router[:, :shard], router[:, META // 2 : META // 2 + shard])
-    total = dot(as_bf16((iota((TILE, tiles), 1) & (TILE - 1)) == iota((TILE, tiles), 0)), messages)
+    total = picked[3 * experts :]
     total = jnp.concatenate([total[r : r + 1] for r in range(5)], axis=1) * scale
     first, second = total[:, :shard], total[:, shard : 2 * shard]
     own_ref[...] = jnp.where(lower, first, second)

time: 256 us -> 256 us (level)
  no operation moved by 1% of the time
where the time goes in v7:
time: 256 us; the launch traced here: 255 us
  Pallas kernels  111 us (43%)
  waiting for transfers between devices  98.9 us (39%)
  starting transfers between devices  42.6 us (17%)
    all_to_all x4, waiting for transfers between devices, exchange(): lax.all_to_all(blocks, CHIPS, split_axis=0, concat_axis=0, tiled=True)  98.9 us
    pallas_call x4, Pallas kernels, by_group(): pl.pallas_call(kernel, grid=(steps,), in_specs=[spec(value.shape, rows) f...  37.6 us
    pallas_call x2, Pallas kernels, expert_call(): pl.pallas_call(kernel, grid=(2 * half,), in_specs=in_specs, out_specs=out...  37.2 us
    all_to_all x4, starting transfers between devices, exchange(): lax.all_to_all(blocks, CHIPS, split_axis=0, concat_axis=0, tiled=True)  34.5 us
    pallas_call x2, Pallas kernels, last_call(): pl.pallas_call(functools.partial(last_kernel, product=product), grid=(PAR...  15.2 us
    pallas_call x2, Pallas kernels, token_side(): pl.pallas_call(kernel, grid=(1,), in_specs=[whole(value.shape) for value...  10.3 us
    pallas_call x2, Pallas kernels, pack(): pl.pallas_call(functools.partial(pack_kernel, eps, pairs), grid=(steps,),...  8.99 us
    ppermute x6, starting transfers between devices, swap(): return lax.ppermute(value, 'core', [(0, 1), (1, 0)])  8.19 us
  transfers between devices with their start and end apart: 10, of which 4 were waited for; matrix products, arithmetic and copies ran while one was open for 0% of the time, Pallas kernels for 41%

profile of v7, /device:TPU:1, one launch (start us, length us, event | category | flops | bytes accessed | tf_op | source)
XLA Modules:
  0.0 254.7 jit_solution(9178020194968673225)
XLA Ops:
  0.6 4.8 %pack.2 = bf16[512,3968]{1,0:T(8,128)(2,1)} custom-call(s32[2,128]{1,0:T(2,128)} %bitcast.17, bf16[128,5120]{1,0:T(8,128)(2,1)} %tokens_ref.1, bf16[320]{0:T(512)(128)(2,1)} %refs_0_.1, bf16[64,320]{1,0:T(8,128)(2,1)} %bitcast.16, s32[1,1]{1,0:T(1,128)} %bitcast.2.refs_2_.core_ref), custom_call_target="tpu_custom_call" | custom-call | flops 1040187392 | bytes 4063232 | tf_op jit(solution)/shard_map/pack/pallas_call | solution.py:148
  5.4 12.2 %all-to-all-start = ((bf16[64,8,3968]{2,1,0:T(8,128)(2,1)}), bf16[64,8,3968]{2,1,0:T(8,128)(2,1)}, u32[]{:S(2)}, u32[]{:S(2)}) async-start(bf16[64,8,3968]{2,1,0:T(8,128)(2,1)} %bitcast.13), calls=%async_computation | async-start | bytes 8126464 | tf_op jit(solution)/shard_map/all_to_all | solution.py:613
  17.6 4.2 %pack.3 = bf16[512,3840]{1,0:T(8,128)(2,1)} custom-call(s32[2,128]{1,0:T(2,128)} %bitcast.18, bf16[128,5120]{1,0:T(8,128)(2,1)} %cot_ref.1), custom_call_target="tpu_custom_call" | custom-call | flops 1006632960 | bytes 3932160 | tf_op jit(solution)/shard_map/pack/pallas_call | solution.py:148
  21.8 46.0 %all-to-all-done = bf16[64,8,3968]{2,1,0:T(8,128)(2,1)} async-done(((bf16[64,8,3968]{2,1,0:T(8,128)(2,1)}), bf16[64,8,3968]{2,1,0:T(8,128)(2,1)}, u32[]{:S(2)}, u32[]{:S(2)}) %all-to-all-start) | async-done | bytes 4063264 | tf_op jit(solution)/shard_map/all_to_all | solution.py:613
  67.8 2.8 %collective-permute-start = (bf16[512,3968]{1,0:T(8,128)(2,1)}, bf16[512,3968]{1,0:T(8,128)(2,1)}, u32[]{:S(2)}, u32[]{:S(2)}) collective-permute-start(bf16[512,3968]{1,0:T(8,128)(2,1)} %bitcast.4.own_ref.own_meta), channel_id=1, source_target_pairs={{0,1},{1,0},{2,3},{3,2},{4,5},{5,4},{6,7},{7,6},{8,9},{9,8},{10,11... | collective-permute-start | bytes 12189704 | tf_op jit(solution)/shard_map/ppermute | solution.py:618
  70.7 7.2 %all-to-all-start.1 = ((bf16[64,8,3840]{2,1,0:T(8,128)(2,1)}), bf16[64,8,3840]{2,1,0:T(8,128)(2,1)}, u32[]{:S(2)}, u32[]{:S(2)}) async-start(bf16[64,8,3840]{2,1,0:T(8,128)(2,1)} %bitcast.14), calls=%async_computation.1 | async-start | bytes 7864320 | tf_op jit(solution)/shard_map/all_to_all | solution.py:613
  77.9 0.0 collective-permute-done.other_ref.other_meta
  77.9 10.7 %norm.1 = (bf16[384,5120]{1,0:T(8,128)(2,1)}, bf16[384,5120]{1,0:T(8,128)(2,1)}, f32[384,128]{1,0:T(8,128)}, f32[384,128]{1,0:T(8,128)}, f32[384,128]{1,0:T(8,12...) custom-call(bf16[512,3968]{1,0:T(8,128)(2,1)} %bitcast.4.own_ref.own_meta, ...), custom_call_target="tpu_custom_call" | custom-call | flops 377487360 | bytes 24821764 | tf_op jit(solution)/shard_map/norm/pallas_call | solution.py:469
  88.6 19.0 %forward.1 = (bf16[384,5120]{1,0:T(8,128)(2,1)}, bf16[384,768]{1,0:T(8,128)(2,1)}, f32[768,768]{1,0:T(8,128)}) custom-call(bf16[384,5120]{1,0:T(8,128)(2,1)} %get-tuple-element.33.own_ref.normed_ref, bf16[384,5120]{1,0:T(8,128)(2,1)} %get-tuple-element.34.other_ref, bf16[1,5120,768]{2,1,0:T(8,128)(2,1)} %weight_ref.3, bf16[1,768,5120]{2,1,0:T(8,128)(2,1)} %down_ref.3), custom_call_target="tpu_custom_call" | custom-call | flops 9059696640 | bytes 31457280 | tf_op jit(solution)/shard_map/forward/pallas_call | solution.py:574
  107.7 0.3 collective-permute-start.1
  108.0 7.6 %forward_own.1.own_ref = bf16[384,5120]{1,0:T(8,128)(2,1)} custom-call(bf16[384,768]{1,0:T(8,128)(2,1)} %get-tuple-element.35.x_ref, bf16[1,768,5120]{2,1,0:T(8,128)(2,1)} %down_ref.3), custom_call_target="tpu_custom_call" | custom-call | flops 193273528320 | bytes 754974720 | tf_op jit(solution)/shard_map/forward_own/pallas_call | solution.py:599
  115.6 0.0 collective-permute-done.1.other_ref
  115.6 7.1 %out.1 = (bf16[384,5120]{1,0:T(8,128)(2,1)}, bf16[512,3840]{1,0:T(8,128)(2,1)}) custom-call(bf16[384,5120]{1,0:T(8,128)(2,1)} %forward_own.1.own_ref, bf16[384,5120]{1,0:T(8,128)(2,1)} %collective-permute-done.1.other_ref, f32[384,128]{1,0:T(8,128)} %get-tuple-element.37.gate_ref.own_gate, bf16[192,192]{1,0:T(8,128)(2,1)} %constant.9.clone.back_ref), custom_call_target="tpu_custom_call" | custom-call | flops 188743680 | bytes 15998976 | tf_op jit(solution)/shard_map/out/pallas_call | solution.py:469
  122.7 5.1 %all-to-all-done.1 = bf16[64,8,3840]{2,1,0:T(8,128)(2,1)} async-done(((bf16[64,8,3840]{2,1,0:T(8,128)(2,1)}), bf16[64,8,3840]{2,1,0:T(8,128)(2,1)}, u32[]{:S(2)}, u32[]{:S(2)}) %all-to-all-start.1) | async-done | bytes 3932192 | tf_op jit(solution)/shard_map/all_to_all | solution.py:613
  127.7 2.2 collective-permute-start.2
  129.9 6.8 %all-to-all-start.2 = ((bf16[64,8,3840]{2,1,0:T(8,128)(2,1)}), bf16[64,8,3840]{2,1,0:T(8,128)(2,1)}, u32[]{:S(2)}, u32[]{:S(2)}) async-start(bf16[64,8,3840]{2,1,0:T(8,128)(2,1)} %bitcast.15), calls=%async_computation.2 | async-start | bytes 7864320 | tf_op jit(solution)/shard_map/all_to_all | solution.py:613
  136.7 0.0 collective-permute-done.2.other_ref
  136.7 9.3 %cot.1 = (bf16[384,5120]{1,0:T(8,128)(2,1)}, bf16[384,5120]{1,0:T(8,128)(2,1)}, f32[384,128]{1,0:T(8,128)}, f32[8,5120]{1,0:T(8,128)}) custom-call(bf16[512,3840]{1,0:T(8,128)(2,1)} %bitcast.6.own_ref, bf16[512,3840]{1,0:T(8,128)(2,1)} %collective-permute-done.2.other_ref, f32[384,128]{1,0:T(8,128)} %get-tuple-element.37.gate_ref.own_gate, ...), custom_call_target="tpu_custom_call" | custom-call | flops 377487360 | bytes 24420352 | tf_op jit(solution)/shard_map/cot/pallas_call | solution.py:469
  146.0 0.4 collective-permute-start.4
  146.4 18.1 %backward.1 = (bf16[384,5120]{1,0:T(8,128)(2,1)}, bf16[384,768]{1,0:T(8,128)(2,1)}) custom-call(bf16[384,5120]{1,0:T(8,128)(2,1)} %get-tuple-element.45.own_ref, bf16[384,5120]{1,0:T(8,128)(2,1)} %get-tuple-element.46.other_ref, bf16[1,768,5120]{2,1,0:T(8,128)(2,1)} %down_ref.3, bf16[1,5120,768]{2,1,0:T(8,128)(2,1)} %weight_ref.3, ...), custom_call_target="tpu_custom_call" | custom-call | flops 9059696640 | bytes 31457280 | tf_op jit(solution)/shard_map/backward/pallas_call | solution.py:574
  164.5 0.2 collective-permute-start.3
  164.7 7.6 %backward_own.1.own_ref = bf16[384,5120]{1,0:T(8,128)(2,1)} custom-call(bf16[384,768]{1,0:T(8,128)(2,1)} %get-tuple-element.48.x_ref, bf16[1,5120,768]{2,1,0:T(8,128)(2,1)} %weight_ref.3), custom_call_target="tpu_custom_call" | custom-call | flops 193273528320 | bytes 754974720 | tf_op jit(solution)/shard_map/backward_own/pallas_call | solution.py:599
  172.3 0.0 collective-permute-done.4.other_router
  172.3 0.0 collective-permute-done.3.other_ref
  172.3 10.5 %grad.1 = bf16[512,3968]{1,0:T(8,128)(2,1)} custom-call(bf16[384,5120]{1,0:T(8,128)(2,1)} %backward_own.1.own_ref, bf16[384,5120]{1,0:T(8,128)(2,1)} %collective-permute-done.3.other_ref, f32[384,128]{1,0:T(8,128)} %get-tuple-element.50.choice_ref, f32[384,128]{1,0:T(8,128)} %get-tuple-element.51.scale_ref, ...), custom_call_target="tpu_custom_call" | custom-call | flops 188743680 | bytes 16695300 | tf_op jit(solution)/shard_map/grad/pallas_call | solution.py:469
  182.8 3.6 %all-to-all-done.2 = bf16[64,8,3840]{2,1,0:T(8,128)(2,1)} async-done(((bf16[64,8,3840]{2,1,0:T(8,128)(2,1)}), bf16[64,8,3840]{2,1,0:T(8,128)(2,1)}, u32[]{:S(2)}, u32[]{:S(2)}) %all-to-all-start.2) | async-done | bytes 3932192 | tf_op jit(solution)/shard_map/all_to_all | solution.py:613
  186.5 0.0 copy-start
  186.5 8.3 %all-to-all-start.3 = ((bf16[64,8,3968]{2,1,0:T(8,128)(2,1)}), bf16[64,8,3968]{2,1,0:T(8,128)(2,1)}, u32[]{:S(2)}, u32[]{:S(2)}) async-start(bf16[64,8,3968]{2,1,0:T(8,128)(2,1)} %bitcast.12), calls=%async_computation.3 | async-start | bytes 8126464 | tf_op jit(solution)/shard_map/all_to_all | solution.py:613
  194.8 0.0 copy-done
  194.8 0.7 copy.13.ids_ref
  195.5 5.3 %mixed.1 = (bf16[128,5120]{1,0:T(8,128)(2,1)}, bf16[3,256,512]{2,1,0:T(8,128)(2,1)}) custom-call(s32[128,2]{1,0:T(8,128)} %copy.13.ids_ref, bf16[128,5120]{1,0:T(8,128)(2,1)} %tokens_ref.1, bf16[512,3840]{1,0:T(8,128)(2,1)} %bitcast.8.band0.band1.band2, bf16[512,3840]{1,0:T(8,128)(2,1)} %bitcast.8.band0.band1.band2, bf16[512,3840]{1,0:T(8,128)(2,1)} %bitcast.8.band0.band1.band2), custom_call_target="tpu_custom_call" | custom-call | flops 1006632960 | bytes 3932160 | tf_op jit(solution)/shard_map/mixed/pallas_call | solution.py:224
  200.8 44.2 %all-to-all-done.3 = bf16[64,8,3968]{2,1,0:T(8,128)(2,1)} async-done(((bf16[64,8,3968]{2,1,0:T(8,128)(2,1)}), bf16[64,8,3968]{2,1,0:T(8,128)(2,1)}, u32[]{:S(2)}, u32[]{:S(2)}) %all-to-all-start.3) | async-done | bytes 4063264 | tf_op jit(solution)/shard_map/all_to_all | solution.py:613
  244.9 1.9 sums.1
  246.8 2.3 collective-permute-start.5
  249.1 0.0 copy-start.1
  249.1 5.0 %grad_tokens.1 = bf16[128,5120]{1,0:T(8,128)(2,1)} custom-call(bf16[3,256,512]{2,1,0:T(8,128)(2,1)} %get-tuple-element.41.choose_ref, bf16[128,5120]{1,0:T(8,128)(2,1)} %cot_ref.1, bf16[512,3968]{1,0:T(8,128)(2,1)} %bitcast.10.band0.band1.band2.meta_ref, bf16[512,3968]{1,0:T(8,128)(2,1)} %bitcast.10.band0.band1.band2.meta_ref, ...), custom_call_target="tpu_custom_call" | custom-call | flops 1006632960 | bytes 3932160 | tf_op jit(solution)/shard_map/grad_tokens/pallas_call | solution.py:224
  254.1 0.0 collective-permute-done.5
  254.1 0.0 copy-done.1
  254.1 0.6 add_reduce_fusion
Async XLA Ops:
  5.4 62.4 %all-to-all-start = ((bf16[64,8,3968]{2,1,0:T(8,128)(2,1)}), bf16[64,8,3968]{2,1,0:T(8,128)(2,1)}, u32[]{:S(2)}, u32[]{:S(2)}) async-start(bf16[64,8,3968]{2,1,0:T(8,128)(2,1)} %bitcast.13), calls=%async_computation | async-start | bytes 8126464 | tf_op jit(solution)/shard_map/all_to_all | solution.py:613
  67.8 10.1 %collective-permute-start = (bf16[512,3968]{1,0:T(8,128)(2,1)}, bf16[512,3968]{1,0:T(8,128)(2,1)}, u32[]{:S(2)}, u32[]{:S(2)}) collective-permute-start(bf16[512,3968]{1,0:T(8,128)(2,1)} %bitcast.4.own_ref.own_meta), channel_id=1, source_target_pairs={{0,1},{1,0},{2,3},{3,2},{4,5},{5,4},{6,7},{7,6},{8,9},{9,8},{10,11... | collective-permute-start | bytes 12189704 | tf_op jit(solution)/shard_map/ppermute | solution.py:618
  70.7 57.0 %all-to-all-start.1 = ((bf16[64,8,3840]{2,1,0:T(8,128)(2,1)}), bf16[64,8,3840]{2,1,0:T(8,128)(2,1)}, u32[]{:S(2)}, u32[]{:S(2)}) async-start(bf16[64,8,3840]{2,1,0:T(8,128)(2,1)} %bitcast.14), calls=%async_computation.1 | async-start | bytes 7864320 | tf_op jit(solution)/shard_map/all_to_all | solution.py:613
  107.7 7.9 %collective-permute-start.1 = (bf16[384,5120]{1,0:T(8,128)(2,1)}, bf16[384,5120]{1,0:T(8,128)(2,1)}, u32[]{:S(2)}, u32[]{:S(2)}) collective-permute-start(bf16[384,5120]{1,0:T(8,128)(2,1)} %get-tuple-element.36), channel_id=1, source_target_pairs={{0,1},{1,0},{2,3},{3,2},{4,5},{5,4},{6,7},{7,6},{8,9},{9,8},{10,11... | collective-permute-start | bytes 11796488 | tf_op jit(solution)/shard_map/ppermute | solution.py:618
  127.7 8.9 %collective-permute-start.2 = (bf16[512,3840]{1,0:T(8,128)(2,1)}, bf16[512,3840]{1,0:T(8,128)(2,1)}, u32[]{:S(2)}, u32[]{:S(2)}) collective-permute-start(bf16[512,3840]{1,0:T(8,128)(2,1)} %bitcast.6.own_ref), channel_id=1, source_target_pairs={{0,1},{1,0},{2,3},{3,2},{4,5},{5,4},{6,7},{7,6},{8,9},{9,8},{10,11... | collective-permute-start | bytes 11796488 | tf_op jit(solution)/shard_map/ppermute | solution.py:618
  129.9 56.6 %all-to-all-start.2 = ((bf16[64,8,3840]{2,1,0:T(8,128)(2,1)}), bf16[64,8,3840]{2,1,0:T(8,128)(2,1)}, u32[]{:S(2)}, u32[]{:S(2)}) async-start(bf16[64,8,3840]{2,1,0:T(8,128)(2,1)} %bitcast.15), calls=%async_computation.2 | async-start | bytes 7864320 | tf_op jit(solution)/shard_map/all_to_all | solution.py:613
  146.0 26.3 %collective-permute-start.4 = (f32[8,5120]{1,0:T(8,128)}, f32[8,5120]{1,0:T(8,128)}, u32[]{:S(2)}, u32[]{:S(2)}) collective-permute-start(f32[8,5120]{1,0:T(8,128)} %get-tuple-element.54.own_router), channel_id=1, source_target_pairs={{0,1},{1,0},{2,3},{3,2},{4,5},{5,4},{6,7},{7,6},{8,9},{9,8},{10,11... | collective-permute-start | bytes 491528 | tf_op jit(solution)/shard_map/ppermute | solution.py:618
  164.5 7.8 %collective-permute-start.3 = (bf16[384,5120]{1,0:T(8,128)(2,1)}, bf16[384,5120]{1,0:T(8,128)(2,1)}, u32[]{:S(2)}, u32[]{:S(2)}) collective-permute-start(bf16[384,5120]{1,0:T(8,128)(2,1)} %get-tuple-element.49), channel_id=1, source_target_pairs={{0,1},{1,0},{2,3},{3,2},{4,5},{5,4},{6,7},{7,6},{8,9},{9,8},{10,11... | collective-permute-start | bytes 11796488 | tf_op jit(solution)/shard_map/ppermute | solution.py:618
  186.5 8.3 %copy-start = (s32[128,2]{0,1:T(2,128)S(1)}, s32[128,2]{0,1:T(2,128)}, u32[]{:S(2)}) copy-start(s32[128,2]{0,1:T(2,128)} %param.14) | copy-start | bytes 3076
  186.5 58.5 %all-to-all-start.3 = ((bf16[64,8,3968]{2,1,0:T(8,128)(2,1)}), bf16[64,8,3968]{2,1,0:T(8,128)(2,1)}, u32[]{:S(2)}, u32[]{:S(2)}) async-start(bf16[64,8,3968]{2,1,0:T(8,128)(2,1)} %bitcast.12), calls=%async_computation.3 | async-start | bytes 8126464 | tf_op jit(solution)/shard_map/all_to_all | solution.py:613
  246.8 7.3 %collective-permute-start.5 = (f32[1,320]{1,0:T(1,128)}, f32[1,320]{1,0:T(1,128)S(1)}, u32[]{:S(2)}, u32[]{:S(2)}) collective-permute-start(f32[1,320]{1,0:T(1,128)} %get-tuple-element.57), channel_id=1, source_target_pairs={{0,1},{1,0},{2,3},{3,2},{4,5},{5,4},{6,7},{7,6},{8,9},{9,8},{10,11... | collective-permute-start | bytes 3848 | tf_op jit(solution)/shard_map/ppermute | solution.py:618
  249.1 5.0 %copy-start.1 = (f32[1,320]{1,0:T(1,128)S(1)}, f32[1,320]{1,0:T(1,128)}, u32[]{:S(2)}) copy-start(f32[1,320]{1,0:T(1,128)} %get-tuple-element.56) | copy-start | bytes 3844
